TPU v7x, 32 devices: a whole 2x2x4 slice. The times are simulated.
32 devices in a mesh: session: 4 (over y, x), ctx: 8 (over z, core).
Axes of the slice: x: 2, y: 2, z: 4, core: 2. Of those that a mesh axis runs over, the one named last changes fastest.
Arguments:
- frames: float32 [6144, 1024], P(('session', 'ctx')), parts along dimension 0, may hold values from -6 to 6
- attend_gain: float32 [1024], replicated, may hold values from 0.25 to 1.75
- query_weight: bfloat16 [1024, 1024], replicated, may hold values from -8 to 8
- key_weight: bfloat16 [1024, 1024], replicated, may hold values from -8 to 8
- value_weight: bfloat16 [1024, 1024], replicated, may hold values from -0.1875 to 0.1875
- output_weight: bfloat16 [1024, 1024], replicated, may hold values from -0.1875 to 0.1875
- mixer_gain: float32 [1024], replicated, may hold values from 0.25 to 1.75
- depthwise: float32 [31, 1024], replicated, may hold values from -1 to 1
- mixer_bias: float32 [1024], replicated, may hold values from -3 to 3
Outputs:
- block_out: float32 [6144, 1024], P(('session', 'ctx')), parts along dimension 0
There are 4 independent parts, one for each index of `session`. A program takes and returns all parts, laid end to end along the dimension named above; an argument that names none is the same for every part. Nothing has to cross between parts.
All inputs are finite; a program needn't handle non-finite values.
Results may differ from a plain program's by a relative error of at most 0.0031.
Values may be sent and summed in bfloat16 or wider, within the bound.
No kernel may reach another device: no remote copies, remote signals or barrier semaphores. Data moves between devices by JAX's collectives and lax.ppermute only.
A program may use at most 256 MiB of HBM per device.

v0:
```python
import jax
import jax.numpy as jnp
from jax import lax
from jax.sharding import PartitionSpec as P

HEADS = 16
KERNEL = 31


def with_halo(block, sides, width):
    for axis, dim in sides:
        count = lax.axis_size(axis)
        forward = [(i, i + 1) for i in range(count - 1)]
        backward = [(target, source) for source, target in forward]
        low = lax.ppermute(
            lax.slice_in_dim(block, block.shape[dim] - width, None, axis=dim), axis, forward
        )
        high = lax.ppermute(lax.slice_in_dim(block, 0, width, axis=dim), axis, backward)
        block = jnp.concatenate([low, block, high], axis=dim)
    return block


def norm_rows(values_in, gain):
    center = jnp.mean(values_in, axis=1, keepdims=True)
    spread = jnp.mean(jnp.square(values_in - center), axis=1, keepdims=True)
    return (values_in - center) * lax.rsqrt(spread + 1e-05) * gain


def project(source, weight):
    return jnp.dot(source, weight, preferred_element_type=jnp.float32).astype(jnp.bfloat16)


def per_device(
    frames,
    attend_gain,
    query_weight,
    key_weight,
    value_weight,
    output_weight,
    mixer_gain,
    depthwise,
    mixer_bias,
):
    row_count, feature_count = frames.shape
    head_size = feature_count // HEADS
    score_scale = head_size ** (-0.5)
    normed = norm_rows(frames, attend_gain).astype(jnp.bfloat16)
    query_heads = project(normed, query_weight).reshape(row_count, HEADS, head_size)
    normed_block = lax.all_gather(normed, "ctx", axis=0, tiled=True)
    key_block = project(normed_block, key_weight)
    highest = jnp.full((HEADS, row_count), -1e30, jnp.float32)
    block_rows = key_block.shape[0]
    key_heads = key_block.reshape(block_rows, HEADS, head_size)
    value_heads = project(normed_block, value_weight).reshape(block_rows, HEADS, head_size)
    scores = (
        jnp.einsum("qhd,khd->hqk", query_heads, key_heads, preferred_element_type=jnp.float32)
        * score_scale
    )
    new_high = jnp.maximum(highest, jnp.max(scores, axis=2))
    weights = jnp.exp(scores - new_high[:, :, None])
    partial_sum = jnp.einsum(
        "hqk,khd->qhd",
        weights.astype(jnp.bfloat16),
        value_heads,
        preferred_element_type=jnp.float32,
    )
    totals = jnp.sum(weights, axis=2)
    running = partial_sum
    highest, totals, running = (new_high, totals, running)
    context = (
        (running / jnp.transpose(totals)[:, :, None])
        .reshape(row_count, feature_count)
        .astype(jnp.bfloat16)
    )
    attended = frames + jnp.dot(context, output_weight, preferred_element_type=jnp.float32)
    mixer_in = norm_rows(attended, mixer_gain)
    half_width = KERNEL // 2
    padded = with_halo(mixer_in, (("ctx", 0),), half_width)
    convolved = jnp.zeros_like(mixer_in) + mixer_bias
    for tap_index in range(KERNEL):
        convolved = convolved + padded[tap_index : tap_index + row_count] * depthwise[tap_index]
    return attended + jax.nn.silu(convolved)


def solution(mesh):
    in_specs = (P(("session", "ctx"), None), P(), P(), P(), P(), P(), P(), P(), P())
    out_specs = P(("session", "ctx"), None)
    return jax.shard_map(
        per_device, mesh=mesh, in_specs=in_specs, out_specs=out_specs, check_vma=False
    )
```

profile of v0, /device:TPU:1, one launch (start us, length us, event | category | flops | bytes accessed | tf_op | source)
XLA Modules:
  0.0 114.6 jit_solution(3139987779421140237)
XLA Ops:
  6.5 1.4 %reduce_sum.45 = f32[192]{0:T(256)S(1)} reduce(f32[192,1024]{1,0:T(8,128)} %param.9, f32[]{:T(128)} %constant.5.clone.1), dimensions={1}, to_apply=%region_0.0 | reduce | flops 196416 | bytes 787204 | tf_op jit(solution)/shard_map/reduce_sum | solution.py:24
  7.9 0.0 copy-start.3
  8.0 1.4 %multiply_reduce_fusion.2 = f32[192]{0:T(256)S(1)} fusion(f32[192,1024]{1,0:T(8,128)} %param.9, f32[192]{0:T(256)S(1)} %broadcast_multiply_fusion.1), kind=kLoop, calls=%fused_computation.160 | loop fusion | flops 589632 | bytes 787968 | tf_op jit(solution)/shard_map/reduce_sum | solution.py:25
  9.4 2.1 %multiply_convert_fusion = bf16[192,1024]{1,0:T(8,128)(2,1)} fusion(f32[192,1024]{1,0:T(8,128)} %param.9, f32[1024]{0:T(1024)} %param.10, f32[192]{0:T(256)S(1)} %add_rsqrt_fusion.1, f32[192]{0:T(256)S(1)} %broadcast_multiply_fusion.1), kind=kLoop, calls=%fused_computation.159 | loop fusion | flops 786432 | bytes 1185280 | tf_op jit(solution)/shard_map/convert_element_type | solution.py:47
  11.4 0.0 all-gather.2.cloned.1.call-update
  11.5 2.3 %convolution_convert_fusion.2 = bf16[192,1024]{1,0:T(8,128)(2,1)S(1)} fusion(bf16[192,1024]{1,0:T(8,128)(2,1)} %multiply_convert_fusion, bf16[1024,1024]{1,0:T(8,128)(2,1)} %param.11), kind=kOutput, calls=%fused_computation.39 | convolution fusion | flops 402849792 | bytes 2883584 | tf_op jit(solution)/shard_map/dot_general | solution.py:30
  13.8 0.2 copy.11
  14.0 0.1 fusion.102
  14.1 38.3 %all-gather.2.cloned.1.call-done = bf16[1536,1024]{1,0:T(8,128)(2,1)} async-done(((bf16[192,1024]{1,0:T(8,128)(2,1)}), bf16[1536,1024]{1,0:T(8,128)(2,1)}) %all-gather.2.cloned.1.call-update) | async-done | bytes 3145744 | tf_op jit(solution)/shard_map/all_gather | solution.py:49
  52.4 5.6 %convolution_convert_fusion = bf16[1536,1024]{0,1:T(8,128)(2,1)S(1)} fusion(bf16[1536,1024]{1,0:T(8,128)(2,1)} %all-gather.2.cloned.1.call-done, bf16[1024,1024]{1,0:T(8,128)(2,1)S(1)} %copy-done), kind=kOutput, calls=%fused_computation.35 | convolution fusion | flops 3222798336 | bytes 8388608 | tf_op jit(solution)/shard_map/dot_general | solution.py:30
  58.0 7.9 %multiply_reduce_fusion = (f32[16,192]{1,0:T(8,128)S(1)}, f32[16,192,1536]{2,1,0:T(8,128)}) fusion(bf16[192,16,64]{0,2,1:T(8,128)(2,1)S(1)} %bitcast.52, bf16[1536,16,64]{0,2,1:T(8,128)(2,1)S(1)} %bitcast.51), kind=kOutput, calls=%fused_computation.1 | convolution fusion | flops 613413888 | bytes 22425600 | tf_op jit(solution)/shard_map/qhd,khd->hqk/dot_general | solution.py:56
  65.9 9.6 %fusion = f32[16,192]{1,0:T(8,128)S(1)} fusion(f32[16,192,1536]{2,1,0:T(8,128)} %get-tuple-element.39, f32[16,192]{1,0:T(8,128)S(1)} %broadcast_maximum_fusion), kind=kLoop, calls=%fused_computation.2 | loop fusion | flops 14152704 | bytes 18898944 | tf_op jit(solution)/shard_map/reduce_sum | solution.py:67
  75.6 7.7 %convolution_convert_fusion.1 = bf16[1536,1024]{0,1:T(8,128)(2,1)} fusion(bf16[1536,1024]{1,0:T(8,128)(2,1)} %all-gather.2.cloned.1.call-done, bf16[1024,1024]{1,0:T(8,128)(2,1)} %param.13), kind=kOutput, calls=%fused_computation.36 | convolution fusion | flops 3222798336 | bytes 8388608 | tf_op jit(solution)/shard_map/dot_general | solution.py:30
  83.3 11.0 %divide_convert_fusion = bf16[192,16,64]{0,2,1:T(8,128)(2,1)S(1)} fusion(bf16[1536,16,64]{0,2,1:T(8,128)(2,1)} %bitcast.86, f32[16,192,1536]{2,1,0:T(8,128)} %get-tuple-element.39, f32[16,192]{1,0:T(8,128)S(1)} %broadcast_maximum_fusion, f32[192,16]{0,1:T(8,128)S(1)} %bitcast.54), kind=kOutput, calls=%fused_computation.40 | convolution fusion | flops 618528768 | bytes 22437888 | tf_op jit(solution)/shard_map/hqk,khd->qhd/dot_general | solution.py:61
  94.3 0.0 copy-start.4
  94.3 0.0 copy-start.5
  94.3 0.7 fusion.104
  95.0 0.2 multiply_reduce_fusion.1
  95.3 0.2 multiply_multiply_fusion
  95.5 2.3 %collective-permute-start = (f32[15,1024]{1,0:T(8,128)S(1)}, f32[15,1024]{1,0:T(8,128)S(1)}, u32[]{:S(2)}, u32[]{:S(2)}) collective-permute-start(f32[15,1024]{1,0:T(8,128)S(1)} %get-tuple-element.5), channel_id=1, source_target_pairs={{0,1},{1,2},{2,3},{3,4},{4,5},{5,6},{6,7},{8,9},{9,10},{10,11},{11... | collective-permute-start | bytes 184328 | tf_op jit(solution)/shard_map/ppermute | solution.py:15
  97.8 2.0 %collective-permute-start.1 = (f32[15,1024]{1,0:T(8,128)S(1)}, f32[15,1024]{1,0:T(8,128)S(1)}, u32[]{:S(2)}, u32[]{:S(2)}) collective-permute-start(f32[15,1024]{1,0:T(8,128)S(1)} %get-tuple-element.6), channel_id=1, source_target_pairs={{1,0},{2,1},{3,2},{4,3},{5,4},{6,5},{7,6},{9,8},{10,9},{11,10},{12... | collective-permute-start | bytes 184328 | tf_op jit(solution)/shard_map/ppermute | solution.py:18
  99.9 0.0 collective-permute-done
  99.9 3.5 %collective-permute-done.1 = f32[15,1024]{1,0:T(8,128)S(1)} collective-permute-done((f32[15,1024]{1,0:T(8,128)S(1)}, f32[15,1024]{1,0:T(8,128)S(1)}, u32[]{:S(2)}, u32[]{:S(2)}) %collective-permute-start.1) | collective-permute-done | bytes 61472 | tf_op jit(solution)/shard_map/ppermute | solution.py:18
  103.4 4.4 %multiply_add_fusion = f32[192,1024]{1,0:T(8,128)} fusion(f32[192,1024]{1,0:T(8,128)S(1)} %get-tuple-element.41, f32[15,1024]{1,0:T(8,128)S(1)} %collective-permute-done.1, f32[192,1024]{1,0:T(8,128)S(1)} %multiply_multiply_fusion, f32[15,1024]{1,0:T(8,128)S(1)} %collective-permute-done, f32[1024]{0:T(1024)S(1)} %bitcast.84, f32[1024]{0:T(1024)S(1)} %bitcast.85, ...), kind=kLoop, calls=%fused_computation.156 | loop fusion | flops 19070976 | bytes 2613248 | tf_op jit(solution)/shard_map/add | solution.py:82
  (17 shorter events, 0.1 us)
Async XLA Ops:
  6.5 45.9 %copy-start = (bf16[1024,1024]{1,0:T(8,128)(2,1)S(1)}, bf16[1024,1024]{1,0:T(8,128)(2,1)}, u32[]{:S(2)}) copy-start(bf16[1024,1024]{1,0:T(8,128)(2,1)} %param.12) | copy-start | bytes 6291460
  6.5 45.9 %all-gather.2.cloned.1.call-start = ((), (), s32[]{:S(2)}) async-start(), calls=%async_computation | async-start | bytes 3538944 | tf_op jit(solution)/shard_map/all_gather | solution.py:49
  7.9 6.0 %copy-start.3 = (f32[31,1024]{1,0:T(8,128)S(1)}, f32[31,1024]{1,0:T(8,128)}, u32[]{:S(2)}) copy-start(f32[31,1024]{1,0:T(8,128)} %param.16) | copy-start | bytes 380932
  83.2 11.0 %copy-start.1 = (f32[192,1024]{1,0:T(8,128)S(1)}, f32[192,1024]{1,0:T(8,128)}, u32[]{:S(2)}) copy-start(f32[192,1024]{1,0:T(8,128)} %param.9) | copy-start | bytes 2359300
  83.3 11.0 %copy-start.2 = (bf16[1024,1024]{1,0:T(8,128)(2,1)S(1)}, bf16[1024,1024]{1,0:T(8,128)(2,1)}, u32[]{:S(2)}) copy-start(bf16[1024,1024]{1,0:T(8,128)(2,1)} %param.14) | copy-start | bytes 6291460
  94.3 1.0 copy-start.4
  94.3 9.1 %copy-start.5 = (f32[1024]{0:T(1024)S(1)}, f32[1024]{0:T(1024)}, u32[]{:S(2)}) copy-start(f32[1024]{0:T(1024)} %param.17) | copy-start | bytes 12292
  95.5 4.4 %collective-permute-start = (f32[15,1024]{1,0:T(8,128)S(1)}, f32[15,1024]{1,0:T(8,128)S(1)}, u32[]{:S(2)}, u32[]{:S(2)}) collective-permute-start(f32[15,1024]{1,0:T(8,128)S(1)} %get-tuple-element.5), channel_id=1, source_target_pairs={{0,1},{1,2},{2,3},{3,4},{4,5},{5,6},{6,7},{8,9},{9,10},{10,11},{11... | collective-permute-start | bytes 184328 | tf_op jit(solution)/shard_map/ppermute | solution.py:15
  97.8 5.6 %collective-permute-start.1 = (f32[15,1024]{1,0:T(8,128)S(1)}, f32[15,1024]{1,0:T(8,128)S(1)}, u32[]{:S(2)}, u32[]{:S(2)}) collective-permute-start(f32[15,1024]{1,0:T(8,128)S(1)} %get-tuple-element.6), channel_id=1, source_target_pairs={{1,0},{2,1},{3,2},{4,3},{5,4},{6,5},{7,6},{9,8},{10,9},{11,10},{12... | collective-permute-start | bytes 184328 | tf_op jit(solution)/shard_map/ppermute | solution.py:18
Sparse Core Ops, SparseCore 0:
  11.6 40.7 all-gather.1
where the time goes:
time: 115 us
  waiting for transfers between devices  41.8 us (36%)
  matrix products  35.2 us (31%)
  other arithmetic  19.3 us (17%)
  between operations  13.6 us (12%)
  starting transfers between devices  4.33 us (4%)
    all_gather x1, waiting for transfers between devices, per_device(): normed_block = lax.all_gather(normed, 'ctx', axis=0, tiled=True)  38.3 us
    dot_general x3, matrix products, project(): jnp.dot(source, weight, preferred_element_type=jnp.float32)  15.6 us
    dot_general x1, matrix products, per_device(): jnp.einsum('hqk,khd->qhd', weights.astype(jnp.bfloat16), value_heads, pre...  11 us
    reduce_sum x1, other arithmetic, per_device(): totals = jnp.sum(weights, axis=2)  9.63 us
    dot_general x1, matrix products, per_device(): jnp.einsum('qhd,khd->hqk', query_heads, key_heads, preferred_element_type...  7.93 us
    add x1, other arithmetic, per_device(): return attended + jax.nn.silu(convolved)  4.41 us
    ppermute x1, waiting for transfers between devices, with_halo(): lax.ppermute(lax.slice_in_dim(block, 0, width, axis=dim), axis, backward)  3.49 us
  transfers between devices with their start and end apart: 3, of which 2 were waited for; matrix products, arithmetic and copies ran while one was open for 2% of the time, Pallas kernels for 0%

commit v1 on v0

v1 whole, which is shorter than its diff:
```python
import functools

import jax
import jax.numpy as jnp
from jax import lax
from jax.experimental import pallas as pl
from jax.experimental.pallas import tpu as pltpu
from jax.sharding import PartitionSpec as P

HEADS = 16
KERNEL = 31
HALO = 16
LANES = 128
EPSILON = 1e-05
VMEM_LIMIT = 48 * 1024 * 1024

VMEM = pl.BlockSpec(memory_space=pltpu.VMEM)
SMEM = pl.BlockSpec(memory_space=pltpu.SMEM)
f32 = jnp.float32
bf16 = jnp.bfloat16


def norm_rows(values_in, gain):
    center = jnp.mean(values_in, axis=1, keepdims=True)
    spread = jnp.mean(jnp.square(values_in - center), axis=1, keepdims=True)
    return (values_in - center) * lax.rsqrt(spread + EPSILON) * gain


def norm_kernel(place, frames, gain, normed, outer_edge, inner_edge):
    rows = frames.shape[0]
    normed[...] = norm_rows(frames[...], gain[...]).astype(bf16)

    @pl.when(place[0] == 0)
    def _():
        outer_edge[...] = frames[:HALO, :]
        inner_edge[...] = frames[rows - HALO :, :]

    @pl.when(place[0] != 0)
    def _():
        outer_edge[...] = frames[rows - HALO :, :]
        inner_edge[...] = frames[:HALO, :]


def attend_block(blocks, query, key_weight, value_weight, keys, values, highest, totals, running, first):
    query_rows, width = query.shape
    head_size = width // HEADS
    pairs = width // LANES
    start = 0
    for block in blocks:
        rows = block.shape[0]
        for low in range(0, width, 256):
            span = slice(low, low + 256)
            keys[start : start + rows, span] = jnp.dot(
                block[...], key_weight[:, span], preferred_element_type=f32
            ).astype(bf16)
            values[start : start + rows, span] = jnp.dot(
                block[...], value_weight[:, span], preferred_element_type=f32
            ).astype(bf16)
        start += rows
    ones = jnp.ones((start, LANES), bf16)
    lane = lax.broadcasted_iota(jnp.int32, (query_rows, LANES), 1)
    low_half = lane < head_size
    for pair in range(pairs):
        span = slice(pair * LANES, (pair + 1) * LANES)
        query_pair = query[:, span]
        key_pair = keys[:start, span]
        value_pair = jnp.concatenate([values[:start, span], ones], axis=1)
        tops, outs = [], []
        for half in range(2):
            mine = low_half if half == 0 else jnp.logical_not(low_half)
            query_head = jnp.where(mine, query_pair, jnp.zeros_like(query_pair))
            scores = lax.dot_general(
                query_head, key_pair, (((1,), (1,)), ((), ())), preferred_element_type=f32
            )
            top = jnp.max(scores, axis=1, keepdims=True)
            weights = jnp.exp(scores - top).astype(bf16)
            outs.append(jnp.dot(weights, value_pair, preferred_element_type=f32))
            tops.append(jnp.broadcast_to(top, (query_rows, LANES)))
        top = jnp.where(low_half, tops[0], tops[1])
        numerator = jnp.where(low_half, outs[0][:, :LANES], outs[1][:, :LANES])
        total = jnp.where(low_half, outs[0][:, LANES:], outs[1][:, LANES:])
        if first:
            highest[:, span] = top
            totals[:, span] = total
            running[:, span] = numerator
        else:
            new_top = jnp.maximum(highest[:, span], top)
            old_scale = jnp.exp(highest[:, span] - new_top)
            scale = jnp.exp(top - new_top)
            highest[:, span] = new_top
            totals[:, span] = totals[:, span] * old_scale + total * scale
            running[:, span] = running[:, span] * old_scale + numerator * scale


def first_kernel(
    place, normed, sibling, outer, inner, gain, query_weight, key_weight, value_weight,
    query, highest, totals, running, extended, keys, values,
):
    rows, width = normed.shape
    scale = (width // HEADS) ** (-0.5)
    is_high = place[0] != 0
    left = jnp.where(is_high, inner[...], outer[...])
    right = jnp.where(is_high, outer[...], inner[...])
    extended[:HALO, :] = norm_rows(left, gain[...]).astype(bf16)
    extended[HALO : HALO + rows, :] = normed[...]
    extended[HALO + rows :, :] = norm_rows(right, gain[...]).astype(bf16)
    for low in range(0, width, 256):
        span = slice(low, low + 256)
        rounded = jnp.dot(extended[...], query_weight[:, span], preferred_element_type=f32).astype(bf16)
        query[:, span] = rounded * jnp.asarray(scale, bf16)
    attend_block(
        (normed, sibling), query, key_weight, value_weight, keys, values, highest, totals, running, True
    )


def block_kernel(
    one, two, query, key_weight, value_weight, highest_in, totals_in, running_in,
    highest, totals, running, keys, values,
):
    highest[...] = highest_in[...]
    totals[...] = totals_in[...]
    running[...] = running_in[...]
    attend_block((one, two), query, key_weight, value_weight, keys, values, highest, totals, running, False)


def last_kernel(
    place, one, two, query, key_weight, value_weight, highest_in, totals_in, running_in,
    frames, outer, inner, output_weight, gain, depthwise, bias,
    block_out, highest, totals, running, keys, values, attended, mixer_in,
):
    rows, width = frames.shape
    highest[...] = highest_in[...]
    totals[...] = totals_in[...]
    running[...] = running_in[...]
    attend_block((one, two), query, key_weight, value_weight, keys, values, highest, totals, running, False)
    is_high = place[0] != 0
    context = (running[...] / totals[...]).astype(bf16)
    attended[:HALO, :] = jnp.where(is_high, inner[...], outer[...])
    attended[HALO : HALO + rows, :] = frames[...]
    attended[HALO + rows :, :] = jnp.where(is_high, outer[...], inner[...])
    for low in range(0, width, 256):
        span = slice(low, low + 256)
        attended[:, span] += jnp.dot(context, output_weight[:, span], preferred_element_type=f32)
    mixer_in[...] = norm_rows(attended[...], gain[...])

    @pl.when(place[1] == 0)
    def _():
        mixer_in[:HALO, :] = jnp.zeros((HALO, width), f32)

    @pl.when(place[2] == 0)
    def _():
        mixer_in[HALO + rows :, :] = jnp.zeros((HALO, width), f32)

    offset = HALO - KERNEL // 2
    for low in range(0, width, LANES):
        span = slice(low, low + LANES)
        convolved = jnp.zeros((rows, LANES), f32) + bias[:, span]
        for shift in range(8):
            part = None
            for tap in range(KERNEL):
                if (tap + offset) % 8 != shift:
                    continue
                base = tap + offset - shift
                size = rows + 8 if shift else rows
                term = mixer_in[base : base + size, span] * depthwise[tap : tap + 1, span]
                part = term if part is None else part + term
            if part is not None:
                convolved = convolved + part[shift : shift + rows]
        block_out[:, span] = attended[HALO : HALO + rows, span] + convolved / (1.0 + jnp.exp(-convolved))


def call(kernel, outs, scratch=(), flops=0, nbytes=0, aliases=None, smem=0, count=0):
    return pl.pallas_call(
        kernel,
        out_shape=outs,
        in_specs=[SMEM] * smem + [VMEM] * (count - smem),
        out_specs=jax.tree.map(lambda _: VMEM, outs),
        scratch_shapes=list(scratch),
        input_output_aliases=aliases or {},
        compiler_params=pltpu.CompilerParams(vmem_limit_bytes=VMEM_LIMIT),
        cost_estimate=pl.CostEstimate(flops=flops, bytes_accessed=nbytes, transcendentals=0),
    )


def per_device(
    frames,
    attend_gain,
    query_weight,
    key_weight,
    value_weight,
    output_weight,
    mixer_gain,
    depthwise,
    mixer_bias,
):
    rows, width = frames.shape
    count = lax.axis_size("ctx")
    chips = count // 2
    me = lax.axis_index("ctx")
    place = jnp.stack([me % 2, (me > 0).astype(jnp.int32), (me < count - 1).astype(jnp.int32)]).astype(jnp.int32)

    ring = list(range(0, chips, 2)) + list(range(1, chips, 2))[::-1]
    steps = [(ring[i], ring[(i + 1) % chips]) for i in range(chips)]
    forward = [(2 * a + core, 2 * b + core) for a, b in steps for core in range(2)]
    backward = [(b, a) for a, b in forward]
    swap = [(i, i ^ 1) for i in range(count)]
    cross = [(i, j) for k in range(1, count - 1, 2) for i, j in ((k, k + 1), (k + 1, k))]

    def send(value, pairs):
        return lax.ppermute(value, "ctx", pairs)

    query_rows = rows + 2 * HALO
    edge = jax.ShapeDtypeStruct((HALO, width), f32)
    state = [jax.ShapeDtypeStruct((query_rows, width), f32)] * 3
    gain = attend_gain.reshape(1, width)
    normed, outer_edge, inner_edge = call(
        norm_kernel, [jax.ShapeDtypeStruct((rows, width), bf16), edge, edge], smem=1, count=3,
        flops=10 * rows * width, nbytes=6 * rows * width,
    )(place, frames, gain)

    ahead = [normed]
    behind = [normed]
    for _ in range(chips // 2):
        ahead.append(send(ahead[-1], forward))
    for _ in range((chips - 1) // 2):
        behind.append(send(behind[-1], backward))
    arrived = []
    for step in range(1, chips // 2 + 1):
        arrived.append(ahead[step])
        if step < len(behind):
            arrived.append(behind[step])

    outer = send(outer_edge, cross)
    inner = send(inner_edge, swap)
    sibling = send(normed, swap)
    weight_flops = 4 * 2 * rows * width * width
    block_flops = weight_flops + 16 * query_rows * 2 * rows * width
    projected = [pltpu.VMEM((2 * rows, width), bf16)] * 2
    query, *carry = call(
        first_kernel,
        [jax.ShapeDtypeStruct((query_rows, width), bf16)] + state,
        scratch=[pltpu.VMEM((query_rows, width), bf16)] + projected,
        smem=1, count=9, flops=block_flops, nbytes=6 * width * width,
    )(place, normed, sibling, outer, inner, gain, query_weight, key_weight, value_weight)
    for block in arrived[:-1]:
        carry = call(
            block_kernel, state, scratch=projected, count=8, aliases={5: 0, 6: 1, 7: 2},
            flops=block_flops, nbytes=4 * width * width,
        )(block, send(block, swap), query, key_weight, value_weight, *carry)
    block = arrived[-1]
    return call(
        last_kernel,
        jax.ShapeDtypeStruct((rows, width), f32),
        scratch=[pltpu.VMEM((query_rows, width), f32)] * 3
        + projected
        + [pltpu.VMEM((query_rows, width), f32)] * 2,
        smem=1, count=16, flops=block_flops, nbytes=6 * width * width,
    )(
        place, block, send(block, swap), query, key_weight, value_weight, *carry,
        frames, outer, inner, output_weight, mixer_gain.reshape(1, width), depthwise, mixer_bias.reshape(1, width),
    )


def solution(mesh):
    in_specs = (P(("session", "ctx"), None), P(), P(), P(), P(), P(), P(), P(), P())
    out_specs = P(("session", "ctx"), None)
    return jax.shard_map(
        per_device, mesh=mesh, in_specs=in_specs, out_specs=out_specs, check_vma=False
    )
```

time: 115 us -> 63.3 us (0.55)
  Pallas kernels: 0 us -> 36.5 us
  matrix products: 35.2 us -> 0 us
  waiting for transfers between devices: 41.8 us -> 9.81 us
  other arithmetic: 19.3 us -> 0.08 us
  between operations: 13.6 us -> 0.16 us
  starting transfers between devices: 4.33 us -> 14.2 us
  local copies, waits for them, and re-layouts: 0.34 us -> 1.85 us
    all_gather x1 -> x0, waiting for transfers between devices: 38.3 us -> none  [per_device(): normed_block = lax.all_gather(normed, 'ctx', axis=0, tiled=True)]
    pallas_call x0 -> x5, Pallas kernels: none -> 36.5 us  [the longest x2 14.5 us: per_device(): call(block_kernel, state, scratch=projected, count=8, aliases={5: 0, 6: 1...]
    dot_general x6 -> x0, matrix products: 35.2 us -> none  [the longest x3 15.6 us: project(): jnp.dot(source, weight, preferred_element_type=jnp.float32)]
    reduce_sum x4 -> x0, other arithmetic: 12.7 us -> none  [the longest x1 9.63 us: per_device(): totals = jnp.sum(weights, axis=2)]
    ppermute x2 -> x9, starting transfers between devices: 4.33 us -> 14.2 us  [send(): return lax.ppermute(value, 'ctx', pairs)]
    ppermute x2 -> x9, waiting for transfers between devices: 3.5 us -> 9.81 us  [send(): return lax.ppermute(value, 'ctx', pairs)]
    add x1 -> x0, other arithmetic: 4.41 us -> none  [per_device(): return attended + jax.nn.silu(convolved)]
    convert_element_type x1 -> x0, other arithmetic: 2.06 us -> none  [per_device(): normed = norm_rows(frames, attend_gain).astype(jnp.bfloat16)]
  transfers between devices with their start and end apart: 3 -> 9, of which waited for: 2 -> 3; matrix products, arithmetic and copies ran while one was open for 2% -> 0% of each run, Pallas kernels for 0% -> 37%
where the time goes in v1:
time: 63.3 us; the launch traced here: 62.6 us
  Pallas kernels  36.5 us (58%)
  starting transfers between devices  14.2 us (22%)
  waiting for transfers between devices  9.81 us (15%)
  local copies, waits for them, and re-layouts  1.85 us (3%)
    pallas_call x2, Pallas kernels, per_device(): call(block_kernel, state, scratch=projected, count=8, aliases={5: 0, 6: 1...  14.5 us
    ppermute x9, starting transfers between devices, send(): return lax.ppermute(value, 'ctx', pairs)  14.2 us
    pallas_call x1, Pallas kernels, per_device(): call(last_kernel, jax.ShapeDtypeStruct((rows, width), f32), scratch=[pltp...  12.4 us
    ppermute x9, waiting for transfers between devices, send(): return lax.ppermute(value, 'ctx', pairs)  9.81 us
    pallas_call x1, Pallas kernels, per_device(): call(first_kernel, [jax.ShapeDtypeStruct((query_rows, width), bf16)] + st...  8.75 us
    unnamed x14, local copies, waits for them, and re-layouts  1.85 us
  transfers between devices with their start and end apart: 9, of which 3 were waited for; matrix products, arithmetic and copies ran while one was open for 0% of the time, Pallas kernels for 37%

profile of v1, /device:TPU:1, one launch (start us, length us, event | category | flops | bytes accessed | tf_op | source)
XLA Modules:
  0.0 62.6 jit_solution(16255197858875700797)
XLA Ops:
  0.0 0.1 pad_add_fusion.place
  0.1 1.1 %copy-done = f32[192,1024]{1,0:T(8,128)S(1)} copy-done((f32[192,1024]{1,0:T(8,128)S(1)}, f32[192,1024]{1,0:T(8,128)}, u32[]{:S(2)}) %copy-start) | copy-done | bytes 786456
  1.2 0.7 %copy-done.4 = f32[1024]{0:T(1024)S(1)} copy-done((f32[1024]{0:T(1024)S(1)}, f32[1024]{0:T(1024)}, u32[]{:S(2)}) %copy-start.4) | copy-done | bytes 4120
  1.9 0.8 %shard_map.91 = (bf16[192,1024]{1,0:T(8,128)(2,1)S(1)}, f32[16,1024]{1,0:T(8,128)S(1)}, f32[16,1024]{1,0:T(8,128)S(1)}) custom-call(s32[3]{0:T(128)S(1)} %pad_add_fusion.place, f32[192,1024]{1,0:T(8,128)S(1)} %copy-done, f32[1,1024]{1,0:T(1,128)S(1)} %bitcast.6), custom_call_target="tpu_custom_call" | custom-call | flops 1966080 | bytes 1179648 | tf_op jit(solution)/shard_map/pallas_call | solution.py:216
  2.7 3.2 %collective-permute-start = (bf16[192,1024]{1,0:T(8,128)(2,1)S(1)}, bf16[192,1024]{1,0:T(8,128)(2,1)S(1)}, u32[]{:S(2)}, u32[]{:S(2)}) collective-permute-start(bf16[192,1024]{1,0:T(8,128)(2,1)S(1)} %get-tuple-element.18.normed), channel_id=1, source_target_pairs={{0,4},{1,5},{4,6},{5,7},{6,2},{7,3},{2,0},{3,1},{8,12},{9,13},{12,... | collective-permute-start | bytes 1179656 | tf_op jit(solution)/shard_map/ppermute | solution.py:210
  5.9 0.0 collective-permute-start.6
  5.9 1.0 %collective-permute-start.3 = (bf16[192,1024]{1,0:T(8,128)(2,1)S(1)}, bf16[192,1024]{1,0:T(8,128)(2,1)S(1)}, u32[]{:S(2)}, u32[]{:S(2)}) collective-permute-start(bf16[192,1024]{1,0:T(8,128)(2,1)S(1)} %get-tuple-element.18.normed), channel_id=1, source_target_pairs={{0,1},{1,0},{2,3},{3,2},{4,5},{5,4},{6,7},{7,6},{8,9},{9,8},{10,11... | collective-permute-start | bytes 1179656 | tf_op jit(solution)/shard_map/ppermute | solution.py:210
  6.9 3.4 %collective-permute-start.4 = (f32[16,1024]{1,0:T(8,128)S(1)}, f32[16,1024]{1,0:T(8,128)S(1)}, u32[]{:S(2)}, u32[]{:S(2)}) collective-permute-start(f32[16,1024]{1,0:T(8,128)S(1)} %get-tuple-element.19), channel_id=1, source_target_pairs={{1,2},{2,1},{3,4},{4,3},{5,6},{6,5},{9,10},{10,9},{11,12},{12,11},... | collective-permute-start | bytes 196616 | tf_op jit(solution)/shard_map/ppermute | solution.py:210
  10.3 3.5 %collective-permute-done.one = bf16[192,1024]{1,0:T(8,128)(2,1)S(1)} collective-permute-done((bf16[192,1024]{1,0:T(8,128)(2,1)S(1)}, bf16[192,1024]{1,0:T(8,128)(2,1)S(1)}, u32[]{:S(2)}, u32[]{:S(2)}) %collective-permute-start) | collective-permute-done | bytes 393248 | tf_op jit(solution)/shard_map/ppermute | solution.py:210
  13.8 3.0 %collective-permute-start.1 = (bf16[192,1024]{1,0:T(8,128)(2,1)S(1)}, bf16[192,1024]{1,0:T(8,128)(2,1)S(1)}, u32[]{:S(2)}, u32[]{:S(2)}) collective-permute-start(bf16[192,1024]{1,0:T(8,128)(2,1)S(1)} %collective-permute-done.one), channel_id=1, source_target_pairs={{0,4},{1,5},{4,6},{5,7},{6,2},{7,3},{2,0},{3,1},{8,12},{9,13},{12,... | collective-permute-start | bytes 1179656 | tf_op jit(solution)/shard_map/ppermute | solution.py:210
  16.8 3.0 %collective-permute-start.8 = (bf16[192,1024]{1,0:T(8,128)(2,1)S(1)}, bf16[192,1024]{1,0:T(8,128)(2,1)S(1)}, u32[]{:S(2)}, u32[]{:S(2)}) collective-permute-start(bf16[192,1024]{1,0:T(8,128)(2,1)S(1)} %collective-permute-done.one), channel_id=1, source_target_pairs={{0,1},{1,0},{2,3},{3,2},{4,5},{5,4},{6,7},{7,6},{8,9},{9,8},{10,11... | collective-permute-start | bytes 1179656 | tf_op jit(solution)/shard_map/ppermute | solution.py:210
  19.8 3.7 %collective-permute-done.4.outer = f32[16,1024]{1,0:T(8,128)S(1)} collective-permute-done((f32[16,1024]{1,0:T(8,128)S(1)}, f32[16,1024]{1,0:T(8,128)S(1)}, u32[]{:S(2)}, u32[]{:S(2)}) %collective-permute-start.4) | collective-permute-done | bytes 65568 | tf_op jit(solution)/shard_map/ppermute | solution.py:210
  23.6 0.0 collective-permute-start.5
  23.6 2.5 %collective-permute-done.6.one = bf16[192,1024]{1,0:T(8,128)(2,1)S(1)} collective-permute-done((bf16[192,1024]{1,0:T(8,128)(2,1)S(1)}, bf16[192,1024]{1,0:T(8,128)(2,1)S(1)}, u32[]{:S(2)}, u32[]{:S(2)}) %collective-permute-start.6) | collective-permute-done | bytes 393248 | tf_op jit(solution)/shard_map/ppermute | solution.py:210
  26.1 0.6 collective-permute-start.7
  26.7 8.8 %shard_map.92 = (bf16[224,1024]{1,0:T(8,128)(2,1)S(1)}, f32[224,1024]{1,0:T(8,128)S(1)}, f32[224,1024]{1,0:T(8,128)S(1)}, f32[224,1024]{1,0:T(8,128)S(1)}) custom-call(s32[3]{0:T(128)S(1)} %pad_add_fusion.place, bf16[192,1024]{1,0:T(8,128)(2,1)S(1)} %get-tuple-element.18.normed, bf16[192,1024]{1,0:T(8,128)(2,1)S(1)} %collective-permute-done.3.sibling, ...), custom_call_target="tpu_custom_call" | custom-call | flops 3019898880 | bytes 6291456 | tf_op jit(solution)/shard_map/pallas_call | solution.py:239
  35.5 0.1 collective-permute-start.2
  35.6 7.1 %shard_map.93 = (f32[224,1024]{1,0:T(8,128)S(1)}, f32[224,1024]{1,0:T(8,128)S(1)}, f32[224,1024]{1,0:T(8,128)S(1)}) custom-call(bf16[192,1024]{1,0:T(8,128)(2,1)S(1)} %collective-permute-done.one, bf16[192,1024]{1,0:T(8,128)(2,1)S(1)} %collective-permute-done.8.two, ...), custom_call_target="tpu_custom_call", output_to_operand_aliasing={{0}: (5, {}), {1}: (6, {}), {2}: (7, {})} | custom-call | flops 3019898880 | bytes 4194304 | tf_op jit(solution)/shard_map/pallas_call | solution.py:246
  42.7 0.0 copy-start.1
  42.7 0.0 copy-start.3
  42.7 0.0 copy-start.5
  42.7 0.0 copy-start.6
  42.7 7.4 %shard_map.94 = (f32[224,1024]{1,0:T(8,128)S(1)}, f32[224,1024]{1,0:T(8,128)S(1)}, f32[224,1024]{1,0:T(8,128)S(1)}) custom-call(bf16[192,1024]{1,0:T(8,128)(2,1)S(1)} %collective-permute-done.6.one, bf16[192,1024]{1,0:T(8,128)(2,1)S(1)} %collective-permute-done.7.two, ...), custom_call_target="tpu_custom_call", output_to_operand_aliasing={{0}: (5, {}), {1}: (6, {}), {2}: (7, {})} | custom-call | flops 3019898880 | bytes 4194304 | tf_op jit(solution)/shard_map/pallas_call | solution.py:246
  50.2 12.4 %shard_map.95 = f32[192,1024]{1,0:T(8,128)} custom-call(s32[3]{0:T(128)S(1)} %pad_add_fusion.place, bf16[192,1024]{1,0:T(8,128)(2,1)S(1)} %collective-permute-done.1.one, bf16[192,1024]{1,0:T(8,128)(2,1)S(1)} %collective-permute-done.2.two, bf16[224,1024]{1,0:T(8,128)(2,1)S(1)} %get-tuple-element.21.query, bf16[1024,1024]{1,0:T(8,128)(2,1)} %key_weight.7, ...), custom_call_target="tpu_custom_call" | custom-call | flops 3019898880 | bytes 6291456 | tf_op jit(solution)/shard_map/pallas_call | solution.py:251
  (14 shorter events, 0.0 us)
Async XLA Ops:
  0.1 1.1 %copy-start = (f32[192,1024]{1,0:T(8,128)S(1)}, f32[192,1024]{1,0:T(8,128)}, u32[]{:S(2)}) copy-start(f32[192,1024]{1,0:T(8,128)} %frames.3) | copy-start | bytes 2359300
  1.2 0.7 %copy-start.4 = (f32[1024]{0:T(1024)S(1)}, f32[1024]{0:T(1024)}, u32[]{:S(2)}) copy-start(f32[1024]{0:T(1024)} %param.10) | copy-start | bytes 12292
  2.7 11.1 %collective-permute-start = (bf16[192,1024]{1,0:T(8,128)(2,1)S(1)}, bf16[192,1024]{1,0:T(8,128)(2,1)S(1)}, u32[]{:S(2)}, u32[]{:S(2)}) collective-permute-start(bf16[192,1024]{1,0:T(8,128)(2,1)S(1)} %get-tuple-element.18.normed), channel_id=1, source_target_pairs={{0,4},{1,5},{4,6},{5,7},{6,2},{7,3},{2,0},{3,1},{8,12},{9,13},{12,... | collective-permute-start | bytes 1179656 | tf_op jit(solution)/shard_map/ppermute | solution.py:210
  5.9 20.2 %collective-permute-start.6 = (bf16[192,1024]{1,0:T(8,128)(2,1)S(1)}, bf16[192,1024]{1,0:T(8,128)(2,1)S(1)}, u32[]{:S(2)}, u32[]{:S(2)}) collective-permute-start(bf16[192,1024]{1,0:T(8,128)(2,1)S(1)} %get-tuple-element.18.normed), channel_id=1, source_target_pairs={{4,0},{5,1},{6,4},{7,5},{2,6},{3,7},{0,2},{1,3},{12,8},{13,9},{14,... | collective-permute-start | bytes 1179656 | tf_op jit(solution)/shard_map/ppermute | solution.py:210
  5.9 20.8 %collective-permute-start.3 = (bf16[192,1024]{1,0:T(8,128)(2,1)S(1)}, bf16[192,1024]{1,0:T(8,128)(2,1)S(1)}, u32[]{:S(2)}, u32[]{:S(2)}) collective-permute-start(bf16[192,1024]{1,0:T(8,128)(2,1)S(1)} %get-tuple-element.18.normed), channel_id=1, source_target_pairs={{0,1},{1,0},{2,3},{3,2},{4,5},{5,4},{6,7},{7,6},{8,9},{9,8},{10,11... | collective-permute-start | bytes 1179656 | tf_op jit(solution)/shard_map/ppermute | solution.py:210
  6.9 16.7 %collective-permute-start.4 = (f32[16,1024]{1,0:T(8,128)S(1)}, f32[16,1024]{1,0:T(8,128)S(1)}, u32[]{:S(2)}, u32[]{:S(2)}) collective-permute-start(f32[16,1024]{1,0:T(8,128)S(1)} %get-tuple-element.19), channel_id=1, source_target_pairs={{1,2},{2,1},{3,4},{4,3},{5,6},{6,5},{9,10},{10,9},{11,12},{12,11},... | collective-permute-start | bytes 196616 | tf_op jit(solution)/shard_map/ppermute | solution.py:210
  13.8 21.6 %collective-permute-start.1 = (bf16[192,1024]{1,0:T(8,128)(2,1)S(1)}, bf16[192,1024]{1,0:T(8,128)(2,1)S(1)}, u32[]{:S(2)}, u32[]{:S(2)}) collective-permute-start(bf16[192,1024]{1,0:T(8,128)(2,1)S(1)} %collective-permute-done.one), channel_id=1, source_target_pairs={{0,4},{1,5},{4,6},{5,7},{6,2},{7,3},{2,0},{3,1},{8,12},{9,13},{12,... | collective-permute-start | bytes 1179656 | tf_op jit(solution)/shard_map/ppermute | solution.py:210
  16.8 18.7 %collective-permute-start.8 = (bf16[192,1024]{1,0:T(8,128)(2,1)S(1)}, bf16[192,1024]{1,0:T(8,128)(2,1)S(1)}, u32[]{:S(2)}, u32[]{:S(2)}) collective-permute-start(bf16[192,1024]{1,0:T(8,128)(2,1)S(1)} %collective-permute-done.one), channel_id=1, source_target_pairs={{0,1},{1,0},{2,3},{3,2},{4,5},{5,4},{6,7},{7,6},{8,9},{9,8},{10,11... | collective-permute-start | bytes 1179656 | tf_op jit(solution)/shard_map/ppermute | solution.py:210
  23.6 12.0 %copy-start.2 = (bf16[1024,1024]{1,0:T(8,128)(2,1)S(1)}, bf16[1024,1024]{1,0:T(8,128)(2,1)}, u32[]{:S(2)}) copy-start(bf16[1024,1024]{1,0:T(8,128)(2,1)} %key_weight.7) | copy-start | bytes 6291460
  23.6 3.1 %collective-permute-start.5 = (f32[16,1024]{1,0:T(8,128)S(1)}, f32[16,1024]{1,0:T(8,128)S(1)}, u32[]{:S(2)}, u32[]{:S(2)}) collective-permute-start(f32[16,1024]{1,0:T(8,128)S(1)} %get-tuple-element.20), channel_id=1, source_target_pairs={{0,1},{1,0},{2,3},{3,2},{4,5},{5,4},{6,7},{7,6},{8,9},{9,8},{10,11... | collective-permute-start | bytes 196616 | tf_op jit(solution)/shard_map/ppermute | solution.py:210
  26.1 16.6 %collective-permute-start.7 = (bf16[192,1024]{1,0:T(8,128)(2,1)S(1)}, bf16[192,1024]{1,0:T(8,128)(2,1)S(1)}, u32[]{:S(2)}, u32[]{:S(2)}) collective-permute-start(bf16[192,1024]{1,0:T(8,128)(2,1)S(1)} %collective-permute-done.6.one), channel_id=1, source_target_pairs={{0,1},{1,0},{2,3},{3,2},{4,5},{5,4},{6,7},{7,6},{8,9},{9,8},{10,11... | collective-permute-start | bytes 1179656 | tf_op jit(solution)/shard_map/ppermute | solution.py:210
  35.5 14.7 %collective-permute-start.2 = (bf16[192,1024]{1,0:T(8,128)(2,1)S(1)}, bf16[192,1024]{1,0:T(8,128)(2,1)S(1)}, u32[]{:S(2)}, u32[]{:S(2)}) collective-permute-start(bf16[192,1024]{1,0:T(8,128)(2,1)S(1)} %collective-permute-done.1.one), channel_id=1, source_target_pairs={{0,1},{1,0},{2,3},{3,2},{4,5},{5,4},{6,7},{7,6},{8,9},{9,8},{10,11... | collective-permute-start | bytes 1179656 | tf_op jit(solution)/shard_map/ppermute | solution.py:210
  42.7 7.5 %copy-start.1 = (f32[192,1024]{1,0:T(8,128)S(1)}, f32[192,1024]{1,0:T(8,128)}, u32[]{:S(2)}) copy-start(f32[192,1024]{1,0:T(8,128)} %frames.3) | copy-start | bytes 2359300
  42.7 7.5 %copy-start.3 = (f32[31,1024]{1,0:T(8,128)S(1)}, f32[31,1024]{1,0:T(8,128)}, u32[]{:S(2)}) copy-start(f32[31,1024]{1,0:T(8,128)} %depthwise.1) | copy-start | bytes 380932
  42.7 7.5 %copy-start.5 = (f32[1024]{0:T(1024)S(1)}, f32[1024]{0:T(1024)}, u32[]{:S(2)}) copy-start(f32[1024]{0:T(1024)} %param.15) | copy-start | bytes 12292
  42.7 7.5 %copy-start.6 = (f32[1024]{0:T(1024)S(1)}, f32[1024]{0:T(1024)}, u32[]{:S(2)}) copy-start(f32[1024]{0:T(1024)} %param.17) | copy-start | bytes 12292

commit v2 on v1

v2 whole, which is shorter than its diff:
```python
import functools

import jax
import jax.numpy as jnp
from jax import lax
from jax.experimental import pallas as pl
from jax.experimental.pallas import tpu as pltpu
from jax.sharding import PartitionSpec as P

HEADS = 16
KERNEL = 31
HALO = 16
LANES = 128
SPAN = 256
EPSILON = 1e-05
CEILING = 1e30
FLOOR = 1e-18
VMEM_LIMIT = 24 * 1024 * 1024
LONG = 20 * 10**9
FIRST = 1024
OWN = 1024
ADD = 1024
BLOCK = 1 * 10**9

VMEM = pl.BlockSpec(memory_space=pltpu.VMEM)
SMEM = pl.BlockSpec(memory_space=pltpu.SMEM)
HBM = pl.BlockSpec(memory_space=pltpu.HBM)
f32 = jnp.float32
bf16 = jnp.bfloat16


def norm_rows(values_in, gain):
    center = jnp.mean(values_in, axis=1, keepdims=True)
    spread = jnp.mean(jnp.square(values_in - center), axis=1, keepdims=True)
    return (values_in - center) * lax.rsqrt(spread + EPSILON) * gain


def norm_kernel(place, frames, gain, normed, outer_edge, inner_edge):
    rows = frames.shape[0]
    is_high = place[0] != 0
    first, last = frames[:HALO, :], frames[rows - HALO :, :]
    outer_edge[...] = jnp.where(is_high, last, first)
    inner_edge[...] = jnp.where(is_high, first, last)
    normed[...] = norm_rows(frames[...], gain[...]).astype(bf16)


def project(block, key_weight, value_weight, keys, values, start):
    rows, width = block.shape
    for low in range(0, width, SPAN):
        span = slice(low, low + SPAN)
        for weight, target in ((key_weight, keys), (value_weight, values)):
            target[start : start + rows, span] = jnp.dot(
                block[...], weight[:, span], preferred_element_type=f32
            ).astype(bf16)


def pair_scores(query, keys, span):
    low_half = lax.broadcasted_iota(jnp.int32, (query.shape[0], LANES), 1) < LANES // 2
    pair = query[:, span]
    zero = jnp.zeros_like(pair)
    both = jnp.concatenate([jnp.where(low_half, pair, zero), jnp.where(low_half, zero, pair)], axis=0)
    return lax.dot_general(both, keys[:, span], (((1,), (1,)), ((), ())), preferred_element_type=f32)


def pair_sums(weights, values, span):
    rows = weights.shape[0] // 2
    low_half = lax.broadcasted_iota(jnp.int32, (rows, LANES), 1) < LANES // 2
    pair = values[:, span]
    out = jnp.dot(
        weights.astype(bf16), jnp.concatenate([pair, jnp.ones_like(pair)], axis=1), preferred_element_type=f32
    )
    totals = jnp.where(low_half, out[:rows, LANES:], out[rows:, LANES:])
    return totals, jnp.where(low_half, out[:rows, :LANES], out[rows:, :LANES])


def attend(query, keys, values, old, new):
    query_rows, width = query.shape
    pairs = width // LANES
    most = least = None
    scores = pair_scores(query, keys, slice(0, LANES))
    for pair in range(pairs):
        span = slice(pair * LANES, (pair + 1) * LANES)
        now = scores
        if pair + 1 < pairs:
            scores = pair_scores(query, keys, slice((pair + 1) * LANES, (pair + 2) * LANES))
        totals, running = pair_sums(jnp.exp(now), values, span)
        if old is not None:
            totals = old[2][:, span] + totals
            running = old[3][:, span] + running
        new[2][:, span] = totals
        new[3][:, span] = running
        most = totals if most is None else jnp.maximum(most, totals)
        least = totals if least is None else jnp.minimum(least, totals)
    fits = jnp.logical_and(jnp.max(most) < CEILING, jnp.min(least) > FLOOR)
    if old is not None:
        fits = jnp.logical_and(fits, jnp.max(old[0][...]) == 0.0)
    new[0][...] = jnp.zeros_like(new[0])

    @pl.when(jnp.logical_not(fits))
    def _():
        new[0][...] = jnp.ones_like(new[0])

        @pl.loop(0, pairs)
        def _(pair):
            span = pl.ds(pl.multiple_of(pair * LANES, LANES), LANES)
            exact = pair_scores(query, keys, span)
            top = jnp.max(exact, axis=1, keepdims=True)
            totals, running = pair_sums(jnp.exp(exact - top), values, span)
            low_half = lax.broadcasted_iota(jnp.int32, (query_rows, LANES), 1) < LANES // 2
            wide = jnp.broadcast_to(top, (2 * query_rows, LANES))
            top = jnp.where(low_half, wide[:query_rows], wide[query_rows:])
            if old is not None:
                old_top = jnp.where(old[0][:1, :] == 0.0, 0.0, old[1][:, span])
                new_top = jnp.maximum(old_top, top)
                old_scale, scale = jnp.exp(old_top - new_top), jnp.exp(top - new_top)
                totals = old[2][:, span] * old_scale + totals * scale
                running = old[3][:, span] * old_scale + running * scale
                top = new_top
            new[1][:, span] = top
            new[2][:, span] = totals
            new[3][:, span] = running


def scaled_query(rows, query_weight, span, width):
    scale = jnp.asarray((width // HEADS) ** (-0.5), bf16)
    return jnp.dot(rows, query_weight[:, span], preferred_element_type=f32).astype(bf16) * scale


def own_kernel(normed, sibling, query_weight, key_weight, value_weight, query, keys, values):
    rows, width = normed.shape
    for low in range(0, width, SPAN):
        span = slice(low, low + SPAN)
        query[:, span] = scaled_query(normed[...], query_weight, span, width)
    project(normed, key_weight, value_weight, keys, values, 0)
    project(sibling, key_weight, value_weight, keys, values, rows)


def add_kernel(block, key_weight, value_weight, keys_in, values_in, keys, values, *, start):
    del keys_in, values_in
    project(block, key_weight, value_weight, keys, values, start)


def own_part_kernel(block, key_weight, value_weight, keys, values):
    project(block, key_weight, value_weight, keys, values, 0)


def first_kernel(
    place, own_query, outer, inner, gain, upper, lower, query_weight, key_weight, value_weight, keys_in, values_in,
    query, shifted, highest, totals, running, keys, values, halo, block, *, start,
):
    del keys_in, values_in
    rows, width = own_query.shape
    is_high = place[0] != 0
    halo[:HALO, :] = norm_rows(jnp.where(is_high, inner[...], outer[...]), gain[...]).astype(bf16)
    halo[HALO:, :] = norm_rows(jnp.where(is_high, outer[...], inner[...]), gain[...]).astype(bf16)
    query[HALO : HALO + rows, :] = own_query[...]
    for low in range(0, width, SPAN):
        span = slice(low, low + SPAN)
        edges = scaled_query(halo[...], query_weight, span, width)
        query[:HALO, span] = edges[:HALO]
        query[HALO + rows :, span] = edges[HALO:]
    half = upper.shape[0]
    block[:half, :] = upper[...]
    block[half:, :] = lower[...]
    project(block, key_weight, value_weight, keys, values, start)
    attend(query, keys, values, None, (shifted, highest, totals, running))


def block_kernel(
    block, query, key_weight, value_weight, shifted_in, highest_in, totals_in, running_in,
    shifted, highest, totals, running, keys, values,
):
    project(block, key_weight, value_weight, keys, values, 0)
    attend(
        query, keys, values, (shifted_in, highest_in, totals_in, running_in), (shifted, highest, totals, running)
    )


def last_kernel(
    place, sibling, keys_in, values_in, query, key_weight, value_weight,
    shifted_in, highest_in, totals_in, running_in,
    frames, outer, inner, output_weight, gain, depthwise, bias,
    block_out, keys, values, shifted, highest, totals, running, attended, mixer_in,
):
    del keys_in, values_in
    rows, width = frames.shape
    project(sibling, key_weight, value_weight, keys, values, rows)
    attend(
        query, keys, values, (shifted_in, highest_in, totals_in, running_in), (shifted, highest, totals, running)
    )
    is_high = place[0] != 0
    context = (running[...] / totals[...]).astype(bf16)
    attended[:HALO, :] = jnp.where(is_high, inner[...], outer[...])
    attended[HALO : HALO + rows, :] = frames[...]
    attended[HALO + rows :, :] = jnp.where(is_high, outer[...], inner[...])
    for low in range(0, width, SPAN):
        span = slice(low, low + SPAN)
        attended[:, span] += jnp.dot(context, output_weight[:, span], preferred_element_type=f32)
    mixer_in[...] = norm_rows(attended[...], gain[...])

    @pl.when(place[1] == 0)
    def _():
        mixer_in[:HALO, :] = jnp.zeros((HALO, width), f32)

    @pl.when(place[2] == 0)
    def _():
        mixer_in[HALO + rows :, :] = jnp.zeros((HALO, width), f32)

    offset = HALO - KERNEL // 2
    for low in range(0, width, LANES):
        span = slice(low, low + LANES)
        convolved = jnp.zeros((rows, LANES), f32) + bias[:, span]
        for shift in range(8):
            part = None
            for tap in range(KERNEL):
                if (tap + offset) % 8 != shift:
                    continue
                base = tap + offset - shift
                size = rows + 8 if shift else rows
                term = mixer_in[base : base + size, span] * depthwise[tap : tap + 1, span]
                part = term if part is None else part + term
            if part is not None:
                convolved = convolved + part[shift : shift + rows]
        block_out[:, span] = attended[HALO : HALO + rows, span] + convolved / (1.0 + jnp.exp(-convolved))


def call(kernel, outs, in_specs, scratch=(), flops=1024, aliases=None):
    return pl.pallas_call(
        kernel,
        out_shape=outs,
        in_specs=in_specs,
        out_specs=jax.tree.map(lambda _: VMEM, outs),
        scratch_shapes=list(scratch),
        input_output_aliases=aliases or {},
        compiler_params=pltpu.CompilerParams(vmem_limit_bytes=VMEM_LIMIT),
        cost_estimate=pl.CostEstimate(flops=flops, bytes_accessed=1024, transcendentals=0),
    )


def per_device(
    frames,
    attend_gain,
    query_weight,
    key_weight,
    value_weight,
    output_weight,
    mixer_gain,
    depthwise,
    mixer_bias,
):
    rows, width = frames.shape
    count = lax.axis_size("ctx")
    chips = count // 2
    me = lax.axis_index("ctx")
    place = jnp.stack([me % 2, (me > 0).astype(jnp.int32), (me < count - 1).astype(jnp.int32)]).astype(jnp.int32)

    ring = list(range(0, chips, 2)) + list(range(1, chips, 2))[::-1]
    steps = [(ring[i], ring[(i + 1) % chips]) for i in range(chips)]
    forward = [(2 * a + core, 2 * b + core) for a, b in steps for core in range(2)]
    backward = [(b, a) for a, b in forward]
    swap = [(i, i ^ 1) for i in range(count)]
    cross = [(i, j) for k in range(1, count - 1, 2) for i, j in ((k, k + 1), (k + 1, k))]
    siblings = [[2 * chip, 2 * chip + 1] for chip in range(chips)]

    def send(value, pairs):
        return lax.ppermute(value, "ctx", pairs)

    query_rows = rows + 2 * HALO
    state = [jax.ShapeDtypeStruct((8, LANES), f32)] + [jax.ShapeDtypeStruct((query_rows, width), f32)] * 3
    edge = jax.ShapeDtypeStruct((HALO, width), f32)
    gain = attend_gain.reshape(1, width)
    normed, outer_edge, inner_edge = call(
        norm_kernel,
        [jax.ShapeDtypeStruct((rows, width), bf16), edge, edge],
        [SMEM, VMEM, VMEM],
        flops=LONG,
    )(place, frames, gain)
    outer = send(outer_edge, cross)
    ahead = send(normed, forward)
    inner = send(inner_edge, swap)
    sibling = send(normed, swap)
    def tall(blocks):
        return [jax.ShapeDtypeStruct((blocks * rows, width), bf16)] * 2

    projected = [pltpu.VMEM((2 * rows, width), bf16)] * 2
    own_query, *pool = call(
        own_kernel, [jax.ShapeDtypeStruct((rows, width), bf16)] + tall(4), [VMEM] * 5, flops=OWN
    )(normed, sibling, query_weight, key_weight, value_weight)
    behind = send(normed, backward)

    block, own_query, outer, inner = lax.optimization_barrier((ahead, own_query, outer, inner))
    ahead = send(block, forward)
    half = rows // 2
    upper, lower = send(block[:half], swap), send(block[half:], swap)
    pool = call(
        functools.partial(add_kernel, start=2 * rows), tall(4), [VMEM] * 5, aliases={3: 0, 4: 1}, flops=ADD
    )(block, key_weight, value_weight, *pool)
    query, *carry = call(
        functools.partial(first_kernel, start=3 * rows),
        [jax.ShapeDtypeStruct((query_rows, width), bf16)] + state + tall(4),
        [SMEM] + [VMEM] * 11,
        [pltpu.VMEM((2 * HALO, width), bf16), pltpu.VMEM((rows, width), bf16)],
        aliases={10: 5, 11: 6},
        flops=FIRST,
    )(place, own_query, outer, inner, gain, upper, lower, query_weight, key_weight, value_weight, *pool)
    carry = carry[:4]
    for step in range(2, chips - 1):
        if step % 2:
            block, carry[2] = lax.optimization_barrier((ahead, carry[2]))
            ahead = send(block, forward)
        else:
            block, carry[2] = lax.optimization_barrier((behind, carry[2]))
            if step < chips - 2:
                behind = send(block, backward)
        both = lax.all_gather(block, "ctx", axis=0, tiled=True, axis_index_groups=siblings)
        carry = list(
            call(block_kernel, list(state), [VMEM] * 8, projected, flops=BLOCK)(
                both, query, key_weight, value_weight, *carry
            )
        )
    block, carry[2] = lax.optimization_barrier((ahead if chips % 2 == 0 else behind, carry[2]))
    other = send(block, swap)
    pool = call(own_part_kernel, tall(2), [VMEM] * 3)(block, key_weight, value_weight)
    block_out, *_ = call(
        last_kernel,
        [jax.ShapeDtypeStruct((rows, width), f32)] + tall(2),
        [SMEM] + [VMEM] * 17,
        [pltpu.VMEM((8, LANES), f32)] + [pltpu.VMEM((query_rows, width), f32)] * 5,
        aliases={2: 1, 3: 2},
    )(
        place, other, *pool, query, key_weight, value_weight, *carry,
        frames, outer, inner, output_weight, mixer_gain.reshape(1, width), depthwise, mixer_bias.reshape(1, width),
    )
    return block_out


def solution(mesh):
    in_specs = (P(("session", "ctx"), None), P(), P(), P(), P(), P(), P(), P(), P())
    out_specs = P(("session", "ctx"), None)
    return jax.shard_map(
        per_device, mesh=mesh, in_specs=in_specs, out_specs=out_specs, check_vma=False
    )
```

time: 63.3 us -> 61.9 us (0.978)
  waiting for transfers between devices: 9.81 us -> 4.1 us
  Pallas kernels: 36.5 us -> 40.3 us
  blocking collectives: 0 us -> 2.71 us
  starting transfers between devices: 14.2 us -> 12.1 us
    ppermute x9, waiting for transfers between devices: 9.81 us -> 4.1 us  [send(): return lax.ppermute(value, 'ctx', pairs)]
    pallas_call x4 -> x6, Pallas kernels: 35.7 us -> 39.5 us  [the longest x1 13.1 us: per_device(): call(last_kernel, [jax.ShapeDtypeStruct((rows, width), f32)] + tall(2), [...]
    all_gather x0 -> x1, blocking collectives: none -> 2.71 us  [per_device(): lax.all_gather(block, 'ctx', axis=0, tiled=True, axis_index_groups=siblings)]
    ppermute x9, starting transfers between devices: 14.2 us -> 12.1 us  [send(): return lax.ppermute(value, 'ctx', pairs)]
    unnamed x14 -> x22, local copies, waits for them, and re-layouts: 1.85 us -> 1.87 us
  transfers between devices with their start and end apart: 9 -> 9, of which waited for: 3 -> 2; matrix products, arithmetic and copies ran while one was open for 0% -> 0% of each run, Pallas kernels for 37% -> 43%
where the time goes in v2:
time: 61.9 us; the launch traced here: 61.3 us
  Pallas kernels  40.3 us (65%)
  starting transfers between devices  12.1 us (20%)
  waiting for transfers between devices  4.1 us (7%)
  blocking collectives  2.71 us (4%)
  local copies, waits for them, and re-layouts  1.89 us (3%)
    pallas_call x1, Pallas kernels, per_device(): call(last_kernel, [jax.ShapeDtypeStruct((rows, width), f32)] + tall(2), [...  13.1 us
    pallas_call x1, Pallas kernels, per_device(): call(functools.partial(first_kernel, start=3 * rows), [jax.ShapeDtypeStru...  12.9 us
    ppermute x9, starting transfers between devices, send(): return lax.ppermute(value, 'ctx', pairs)  12.1 us
    pallas_call x1, Pallas kernels, per_device(): call(block_kernel, list(state), [VMEM] * 8, projected, flops=BLOCK)  9.1 us
    ppermute x9, waiting for transfers between devices, send(): return lax.ppermute(value, 'ctx', pairs)  4.1 us
    all_gather x1, blocking collectives, per_device(): lax.all_gather(block, 'ctx', axis=0, tiled=True, axis_index_groups=siblings)  2.71 us
    pallas_call x1, Pallas kernels, per_device(): call(own_kernel, [jax.ShapeDtypeStruct((rows, width), bf16)] + tall(4), [...  2.27 us
    unnamed x22, local copies, waits for them, and re-layouts  1.87 us
  transfers between devices with their start and end apart: 9, of which 2 were waited for; matrix products, arithmetic and copies ran while one was open for 0% of the time, Pallas kernels for 43%

profile of v2, /device:TPU:1, one launch (start us, length us, event | category | flops | bytes accessed | tf_op | source)
XLA Modules:
  0.0 61.3 jit_solution(8918286522499080410)
XLA Ops:
  0.0 0.1 pad_add_fusion.place
  0.1 1.1 %copy-done.4 = f32[192,1024]{1,0:T(8,128)S(1)} copy-done((f32[192,1024]{1,0:T(8,128)S(1)}, f32[192,1024]{1,0:T(8,128)}, u32[]{:S(2)}) %copy-start.4) | copy-done | bytes 786456
  1.2 0.7 %copy-done.7 = f32[1024]{0:T(1024)S(1)} copy-done((f32[1024]{0:T(1024)S(1)}, f32[1024]{0:T(1024)}, u32[]{:S(2)}) %copy-start.7) | copy-done | bytes 4120
  1.9 0.8 %shard_map.91 = (bf16[192,1024]{1,0:T(8,128)(2,1)S(1)}, f32[16,1024]{1,0:T(8,128)S(1)}, f32[16,1024]{1,0:T(8,128)S(1)}) custom-call(s32[3]{0:T(128)S(1)} %pad_add_fusion.place, f32[192,1024]{1,0:T(8,128)S(1)} %copy-done.4, f32[1,1024]{1,0:T(1,128)S(1)} %bitcast.6), custom_call_target="tpu_custom_call" | custom-call | flops 20000000000 | bytes 1024 | tf_op jit(solution)/shard_map/pallas_call | solution.py:272
  2.7 0.1 collective-permute-start.1
  2.9 3.8 %collective-permute-start = (bf16[192,1024]{1,0:T(8,128)(2,1)S(1)}, bf16[192,1024]{1,0:T(8,128)(2,1)S(1)}, u32[]{:S(2)}, u32[]{:S(2)}) collective-permute-start(bf16[192,1024]{1,0:T(8,128)(2,1)S(1)} %get-tuple-element.33.normed), channel_id=1, source_target_pairs={{0,4},{1,5},{4,6},{5,7},{6,2},{7,3},{2,0},{3,1},{8,12},{9,13},{12,... | collective-permute-start | bytes 1179656 | tf_op jit(solution)/shard_map/ppermute | solution.py:266
  6.6 1.9 %collective-permute-start.2 = (f32[16,1024]{1,0:T(8,128)S(1)}, f32[16,1024]{1,0:T(8,128)S(1)}, u32[]{:S(2)}, u32[]{:S(2)}) collective-permute-start(f32[16,1024]{1,0:T(8,128)S(1)} %get-tuple-element.35), channel_id=1, source_target_pairs={{1,2},{2,1},{3,4},{4,3},{5,6},{6,5},{9,10},{10,9},{11,12},{12,11},... | collective-permute-start | bytes 196616 | tf_op jit(solution)/shard_map/ppermute | solution.py:266
  8.5 0.1 collective-permute-start.3
  8.6 1.9 %collective-permute-start.5 = (bf16[192,1024]{1,0:T(8,128)(2,1)S(1)}, bf16[192,1024]{1,0:T(8,128)(2,1)S(1)}, u32[]{:S(2)}, u32[]{:S(2)}) collective-permute-start(bf16[192,1024]{1,0:T(8,128)(2,1)S(1)} %get-tuple-element.33.normed), channel_id=1, source_target_pairs={{4,0},{5,1},{6,4},{7,5},{2,6},{3,7},{0,2},{1,3},{12,8},{13,9},{14,... | collective-permute-start | bytes 1179656 | tf_op jit(solution)/shard_map/ppermute | solution.py:266
  10.5 2.3 %shard_map.92 = (bf16[192,1024]{1,0:T(8,128)(2,1)S(1)}, bf16[768,1024]{1,0:T(8,128)(2,1)S(1)}, bf16[768,1024]{1,0:T(8,128)(2,1)S(1)}) custom-call(bf16[192,1024]{1,0:T(8,128)(2,1)S(1)} %get-tuple-element.33.normed, bf16[192,1024]{1,0:T(8,128)(2,1)S(1)} %collective-permute-done.1.sibling, bf16[1024,1024]{1,0:T(8,128)(2,1)S(1)} %copy-done.2, ...), custom_call_target="tpu_custom_call" | custom-call | flops 1024 | bytes 1024 | tf_op jit(solution)/shard_map/pallas_call | solution.py:286
  12.8 3.8 %collective-permute-done.2.outer = f32[16,1024]{1,0:T(8,128)S(1)} collective-permute-done((f32[16,1024]{1,0:T(8,128)S(1)}, f32[16,1024]{1,0:T(8,128)S(1)}, u32[]{:S(2)}, u32[]{:S(2)}) %collective-permute-start.2) | collective-permute-done | bytes 65568 | tf_op jit(solution)/shard_map/ppermute | solution.py:266
  16.6 0.1 collective-permute-start.7
  16.7 0.5 collective-permute-start.6
  17.2 3.4 %collective-permute-start.4 = (bf16[192,1024]{1,0:T(8,128)(2,1)S(1)}, bf16[192,1024]{1,0:T(8,128)(2,1)S(1)}, u32[]{:S(2)}, u32[]{:S(2)}) collective-permute-start(bf16[192,1024]{1,0:T(8,128)(2,1)S(1)} %collective-permute-done.block), channel_id=1, source_target_pairs={{0,4},{1,5},{4,6},{5,7},{6,2},{7,3},{2,0},{3,1},{8,12},{9,13},{12,... | collective-permute-start | bytes 1179656 | tf_op jit(solution)/shard_map/ppermute | solution.py:266
  20.5 1.0 %shard_map.93 = (bf16[768,1024]{1,0:T(8,128)(2,1)S(1)}, bf16[768,1024]{1,0:T(8,128)(2,1)S(1)}) custom-call(bf16[192,1024]{1,0:T(8,128)(2,1)S(1)} %collective-permute-done.block, bf16[1024,1024]{1,0:T(8,128)(2,1)S(1)} %copy-done, bf16[1024,1024]{1,0:T(8,128)(2,1)S(1)} %copy-done.1, ...), custom_call_target="tpu_custom_call", output_to_operand_aliasing={{0}: (3, {}), {1}: (4, {})} | custom-call | flops 1024 | bytes 1024 | tf_op jit(solution)/shard_map/pallas_call | solution.py:295
  21.6 12.9 %shard_map.94 = (bf16[224,1024]{1,0:T(8,128)(2,1)S(1)}, f32[8,128]{1,0:T(8,128)S(1)}, f32[224,1024]{1,0:T(8,128)S(1)}, f32[224,1024]{1,0:T(8,128)S(1)}, f32[224,...) custom-call(s32[3]{0:T(128)S(1)} %pad_add_fusion.place, ...), custom_call_target="tpu_custom_call", output_to_operand_aliasing={{5}: (10, {}), {6}: (11, {})} | custom-call | flops 1024 | bytes 1024 | tf_op jit(solution)/shard_map/pallas_call | solution.py:298
  34.5 2.7 %all_gather.3.block = bf16[384,1024]{1,0:T(8,128)(2,1)S(1)} all-gather(bf16[192,1024]{1,0:T(8,128)(2,1)S(1)} %collective-permute-done.5), channel_id=1, replica_groups={{0,1},{2,3},{4,5},{6,7},{8,9},{10,11},{12,13},{14,15},{16,17},{18,19},{..., dimensions={0}, use_global_device_ids=true | all-gather | bytes 1179648 | tf_op jit(solution)/shard_map/all_gather | solution.py:315
  37.3 9.1 %shard_map.95 = (f32[8,128]{1,0:T(8,128)S(1)}, f32[224,1024]{1,0:T(8,128)S(1)}, f32[224,1024]{1,0:T(8,128)S(1)}, f32[224,1024]{1,0:T(8,128)S(1)}) custom-call(bf16[384,1024]{1,0:T(8,128)(2,1)S(1)} %all_gather.3.block, bf16[224,1024]{1,0:T(8,128)(2,1)S(1)} %get-tuple-element.47.query, bf16[1024,1024]{1,0:T(8,128)(2,1)S(1)} %copy-done, ...), custom_call_target="tpu_custom_call" | custom-call | flops 1000000000 | bytes 1024 | tf_op jit(solution)/shard_map/pallas_call | solution.py:317
  46.4 0.0 copy-start.6
  46.4 0.0 copy-start.9
  46.4 0.4 collective-permute-start.8
  46.9 1.0 %shard_map.96 = (bf16[384,1024]{1,0:T(8,128)(2,1)S(1)}, bf16[384,1024]{1,0:T(8,128)(2,1)S(1)}) custom-call(bf16[192,1024]{1,0:T(8,128)(2,1)S(1)} %collective-permute-done.4.block, bf16[1024,1024]{1,0:T(8,128)(2,1)S(1)} %copy-done, bf16[1024,1024]{1,0:T(8,128)(2,1)S(1)} %copy-done.1), custom_call_target="tpu_custom_call" | custom-call | flops 1024 | bytes 1024 | tf_op jit(solution)/shard_map/pallas_call | solution.py:323
  47.9 0.3 collective-permute-done.8.sibling
  48.3 13.1 %shard_map.97 = (f32[192,1024]{1,0:T(8,128)}, bf16[384,1024]{1,0:T(8,128)(2,1)S(1)}, bf16[384,1024]{1,0:T(8,128)(2,1)S(1)}) custom-call(s32[3]{0:T(128)S(1)} %pad_add_fusion.place, bf16[192,1024]{1,0:T(8,128)(2,1)S(1)} %collective-permute-done.8.sibling, ...), custom_call_target="tpu_custom_call", output_to_operand_aliasing={{1}: (2, {}), {2}: (3, {})} | custom-call | flops 1024 | bytes 1024 | tf_op jit(solution)/shard_map/pallas_call | solution.py:324
  (26 shorter events, 0.1 us)
Async XLA Ops:
  0.1 1.1 %copy-start.4 = (f32[192,1024]{1,0:T(8,128)S(1)}, f32[192,1024]{1,0:T(8,128)}, u32[]{:S(2)}) copy-start(f32[192,1024]{1,0:T(8,128)} %frames.3) | copy-start | bytes 2359300
  1.2 0.7 %copy-start.7 = (f32[1024]{0:T(1024)S(1)}, f32[1024]{0:T(1024)}, u32[]{:S(2)}) copy-start(f32[1024]{0:T(1024)} %param.10) | copy-start | bytes 12292
  1.9 8.6 %copy-start = (bf16[1024,1024]{1,0:T(8,128)(2,1)S(1)}, bf16[1024,1024]{1,0:T(8,128)(2,1)}, u32[]{:S(2)}) copy-start(bf16[1024,1024]{1,0:T(8,128)(2,1)} %key_weight.11) | copy-start | bytes 6291460
  1.9 8.6 %copy-start.1 = (bf16[1024,1024]{1,0:T(8,128)(2,1)S(1)}, bf16[1024,1024]{1,0:T(8,128)(2,1)}, u32[]{:S(2)}) copy-start(bf16[1024,1024]{1,0:T(8,128)(2,1)} %value_weight.11) | copy-start | bytes 6291460
  1.9 8.6 %copy-start.2 = (bf16[1024,1024]{1,0:T(8,128)(2,1)S(1)}, bf16[1024,1024]{1,0:T(8,128)(2,1)}, u32[]{:S(2)}) copy-start(bf16[1024,1024]{1,0:T(8,128)(2,1)} %query_weight.3) | copy-start | bytes 6291460
  2.7 7.7 %collective-permute-start.1 = (bf16[192,1024]{1,0:T(8,128)(2,1)S(1)}, bf16[192,1024]{1,0:T(8,128)(2,1)S(1)}, u32[]{:S(2)}, u32[]{:S(2)}) collective-permute-start(bf16[192,1024]{1,0:T(8,128)(2,1)S(1)} %get-tuple-element.33.normed), channel_id=1, source_target_pairs={{0,1},{1,0},{2,3},{3,2},{4,5},{5,4},{6,7},{7,6},{8,9},{9,8},{10,11... | collective-permute-start | bytes 1179656 | tf_op jit(solution)/shard_map/ppermute | solution.py:266
  2.9 13.7 %collective-permute-start = (bf16[192,1024]{1,0:T(8,128)(2,1)S(1)}, bf16[192,1024]{1,0:T(8,128)(2,1)S(1)}, u32[]{:S(2)}, u32[]{:S(2)}) collective-permute-start(bf16[192,1024]{1,0:T(8,128)(2,1)S(1)} %get-tuple-element.33.normed), channel_id=1, source_target_pairs={{0,4},{1,5},{4,6},{5,7},{6,2},{7,3},{2,0},{3,1},{8,12},{9,13},{12,... | collective-permute-start | bytes 1179656 | tf_op jit(solution)/shard_map/ppermute | solution.py:266
  6.6 9.9 %collective-permute-start.2 = (f32[16,1024]{1,0:T(8,128)S(1)}, f32[16,1024]{1,0:T(8,128)S(1)}, u32[]{:S(2)}, u32[]{:S(2)}) collective-permute-start(f32[16,1024]{1,0:T(8,128)S(1)} %get-tuple-element.35), channel_id=1, source_target_pairs={{1,2},{2,1},{3,4},{4,3},{5,6},{6,5},{9,10},{10,9},{11,12},{12,11},... | collective-permute-start | bytes 196616 | tf_op jit(solution)/shard_map/ppermute | solution.py:266
  8.5 8.0 %collective-permute-start.3 = (f32[16,1024]{1,0:T(8,128)S(1)}, f32[16,1024]{1,0:T(8,128)S(1)}, u32[]{:S(2)}, u32[]{:S(2)}) collective-permute-start(f32[16,1024]{1,0:T(8,128)S(1)} %get-tuple-element.36), channel_id=1, source_target_pairs={{0,1},{1,0},{2,3},{3,2},{4,5},{5,4},{6,7},{7,6},{8,9},{9,8},{10,11... | collective-permute-start | bytes 196616 | tf_op jit(solution)/shard_map/ppermute | solution.py:266
  8.6 25.9 %collective-permute-start.5 = (bf16[192,1024]{1,0:T(8,128)(2,1)S(1)}, bf16[192,1024]{1,0:T(8,128)(2,1)S(1)}, u32[]{:S(2)}, u32[]{:S(2)}) collective-permute-start(bf16[192,1024]{1,0:T(8,128)(2,1)S(1)} %get-tuple-element.33.normed), channel_id=1, source_target_pairs={{4,0},{5,1},{6,4},{7,5},{2,6},{3,7},{0,2},{1,3},{12,8},{13,9},{14,... | collective-permute-start | bytes 1179656 | tf_op jit(solution)/shard_map/ppermute | solution.py:266
  16.6 5.0 %collective-permute-start.7 = (bf16[96,1024]{1,0:T(8,128)(2,1)S(1)}, bf16[96,1024]{1,0:T(8,128)(2,1)S(1)}, u32[]{:S(2)}, u32[]{:S(2)}) collective-permute-start(bf16[96,1024]{1,0:T(8,128)(2,1)S(1)} %get-tuple-element.61), channel_id=1, source_target_pairs={{0,1},{1,0},{2,3},{3,2},{4,5},{5,4},{6,7},{7,6},{8,9},{9,8},{10,11... | collective-permute-start | bytes 589832 | tf_op jit(solution)/shard_map/ppermute | solution.py:266
  16.7 4.9 %collective-permute-start.6 = (bf16[96,1024]{1,0:T(8,128)(2,1)S(1)}, bf16[96,1024]{1,0:T(8,128)(2,1)S(1)}, u32[]{:S(2)}, u32[]{:S(2)}) collective-permute-start(bf16[96,1024]{1,0:T(8,128)(2,1)S(1)} %get-tuple-element.62), channel_id=1, source_target_pairs={{0,1},{1,0},{2,3},{3,2},{4,5},{5,4},{6,7},{7,6},{8,9},{9,8},{10,11... | collective-permute-start | bytes 589832 | tf_op jit(solution)/shard_map/ppermute | solution.py:266
  17.2 29.2 %collective-permute-start.4 = (bf16[192,1024]{1,0:T(8,128)(2,1)S(1)}, bf16[192,1024]{1,0:T(8,128)(2,1)S(1)}, u32[]{:S(2)}, u32[]{:S(2)}) collective-permute-start(bf16[192,1024]{1,0:T(8,128)(2,1)S(1)} %collective-permute-done.block), channel_id=1, source_target_pairs={{0,4},{1,5},{4,6},{5,7},{6,2},{7,3},{2,0},{3,1},{8,12},{9,13},{12,... | collective-permute-start | bytes 1179656 | tf_op jit(solution)/shard_map/ppermute | solution.py:266
  20.5 1.1 %copy-start.8 = (f32[1024]{0:T(1024)S(1)}, f32[1024]{0:T(1024)}, u32[]{:S(2)}) copy-start(f32[1024]{0:T(1024)} %param.10) | copy-start | bytes 12292
  46.4 1.9 %copy-start.3 = (bf16[1024,1024]{1,0:T(8,128)(2,1)S(1)}, bf16[1024,1024]{1,0:T(8,128)(2,1)}, u32[]{:S(2)}) copy-start(bf16[1024,1024]{1,0:T(8,128)(2,1)} %output_weight.1) | copy-start | bytes 6291460
  46.4 1.8 %copy-start.5 = (f32[192,1024]{1,0:T(8,128)S(1)}, f32[192,1024]{1,0:T(8,128)}, u32[]{:S(2)}) copy-start(f32[192,1024]{1,0:T(8,128)} %frames.3) | copy-start | bytes 2359300
  46.4 1.8 %copy-start.6 = (f32[31,1024]{1,0:T(8,128)S(1)}, f32[31,1024]{1,0:T(8,128)}, u32[]{:S(2)}) copy-start(f32[31,1024]{1,0:T(8,128)} %depthwise.1) | copy-start | bytes 380932
  46.4 1.8 %copy-start.9 = (f32[1024]{0:T(1024)S(1)}, f32[1024]{0:T(1024)}, u32[]{:S(2)}) copy-start(f32[1024]{0:T(1024)} %param.15) | copy-start | bytes 12292
  46.4 1.8 %copy-start.10 = (f32[1024]{0:T(1024)S(1)}, f32[1024]{0:T(1024)}, u32[]{:S(2)}) copy-start(f32[1024]{0:T(1024)} %param.17) | copy-start | bytes 12292
  46.4 1.8 %collective-permute-start.8 = (bf16[192,1024]{1,0:T(8,128)(2,1)S(1)}, bf16[192,1024]{1,0:T(8,128)(2,1)S(1)}, u32[]{:S(2)}, u32[]{:S(2)}) collective-permute-start(bf16[192,1024]{1,0:T(8,128)(2,1)S(1)} %collective-permute-done.4.block), channel_id=1, source_target_pairs={{0,1},{1,0},{2,3},{3,2},{4,5},{5,4},{6,7},{7,6},{8,9},{9,8},{10,11... | collective-permute-start | bytes 1179656 | tf_op jit(solution)/shard_map/ppermute | solution.py:266

commit v3 on v2

--- a/solution.py
+++ b/solution.py
@@ -23,7 +23,6 @@
 BLOCK = 1 * 10**9
 
 VMEM = pl.BlockSpec(memory_space=pltpu.VMEM)
-SMEM = pl.BlockSpec(memory_space=pltpu.SMEM)
 HBM = pl.BlockSpec(memory_space=pltpu.HBM)
 f32 = jnp.float32
 bf16 = jnp.bfloat16
@@ -35,9 +34,13 @@
     return (values_in - center) * lax.rsqrt(spread + EPSILON) * gain
 
 
+def place_kernel(place, place_out):
+    place_out[...] = place[...]
+
+
 def norm_kernel(place, frames, gain, normed, outer_edge, inner_edge):
     rows = frames.shape[0]
-    is_high = place[0] != 0
+    is_high = place[:1, :1] > 0
     first, last = frames[:HALO, :], frames[rows - HALO :, :]
     outer_edge[...] = jnp.where(is_high, last, first)
     inner_edge[...] = jnp.where(is_high, first, last)
@@ -150,7 +153,7 @@
 ):
     del keys_in, values_in
     rows, width = own_query.shape
-    is_high = place[0] != 0
+    is_high = place[:1, :1] > 0
     halo[:HALO, :] = norm_rows(jnp.where(is_high, inner[...], outer[...]), gain[...]).astype(bf16)
     halo[HALO:, :] = norm_rows(jnp.where(is_high, outer[...], inner[...]), gain[...]).astype(bf16)
     query[HALO : HALO + rows, :] = own_query[...]
@@ -180,7 +183,7 @@
     place, sibling, keys_in, values_in, query, key_weight, value_weight,
     shifted_in, highest_in, totals_in, running_in,
     frames, outer, inner, output_weight, gain, depthwise, bias,
-    block_out, keys, values, shifted, highest, totals, running, attended, mixer_in,
+    block_out, keys, values, shifted, highest, totals, running, attended, mixer_in, held, sems,
 ):
     del keys_in, values_in
     rows, width = frames.shape
@@ -188,7 +191,7 @@
     attend(
         query, keys, values, (shifted_in, highest_in, totals_in, running_in), (shifted, highest, totals, running)
     )
-    is_high = place[0] != 0
+    is_high = place[:1, :1] > 0
     context = (running[...] / totals[...]).astype(bf16)
     attended[:HALO, :] = jnp.where(is_high, inner[...], outer[...])
     attended[HALO : HALO + rows, :] = frames[...]
@@ -198,15 +201,10 @@
         attended[:, span] += jnp.dot(context, output_weight[:, span], preferred_element_type=f32)
     mixer_in[...] = norm_rows(attended[...], gain[...])
 
-    @pl.when(place[1] == 0)
-    def _():
-        mixer_in[:HALO, :] = jnp.zeros((HALO, width), f32)
-
-    @pl.when(place[2] == 0)
-    def _():
-        mixer_in[HALO + rows :, :] = jnp.zeros((HALO, width), f32)
-
+    mixer_in[:HALO, :] = jnp.where(place[1:2, :1] > 0, mixer_in[:HALO, :], 0.0)
+    mixer_in[HALO + rows :, :] = jnp.where(place[2:3, :1] > 0, mixer_in[HALO + rows :, :], 0.0)
     offset = HALO - KERNEL // 2
+    copies = []
     for low in range(0, width, LANES):
         span = slice(low, low + LANES)
         convolved = jnp.zeros((rows, LANES), f32) + bias[:, span]
@@ -221,15 +219,19 @@
                 part = term if part is None else part + term
             if part is not None:
                 convolved = convolved + part[shift : shift + rows]
-        block_out[:, span] = attended[HALO : HALO + rows, span] + convolved / (1.0 + jnp.exp(-convolved))
-
-
-def call(kernel, outs, in_specs, scratch=(), flops=1024, aliases=None):
+        held[:, span] = attended[HALO : HALO + rows, span] + convolved / (1.0 + jnp.exp(-convolved))
+        copies.append(pltpu.make_async_copy(held.at[:, span], block_out.at[:, span], sems.at[low // LANES]))
+        copies[-1].start()
+    for copy in copies:
+        copy.wait()
+
+
+def call(kernel, outs, in_specs, scratch=(), flops=1024, aliases=None, out_specs=None):
     return pl.pallas_call(
         kernel,
         out_shape=outs,
         in_specs=in_specs,
-        out_specs=jax.tree.map(lambda _: VMEM, outs),
+        out_specs=out_specs or jax.tree.map(lambda _: VMEM, outs),
         scratch_shapes=list(scratch),
         input_output_aliases=aliases or {},
         compiler_params=pltpu.CompilerParams(vmem_limit_bytes=VMEM_LIMIT),
@@ -252,7 +254,9 @@
     count = lax.axis_size("ctx")
     chips = count // 2
     me = lax.axis_index("ctx")
-    place = jnp.stack([me % 2, (me > 0).astype(jnp.int32), (me < count - 1).astype(jnp.int32)]).astype(jnp.int32)
+    place = jnp.stack([me % 2, (me > 0).astype(jnp.int32), (me < count - 1).astype(jnp.int32)]).astype(f32)
+    place = jnp.broadcast_to(place[:, None], (3, LANES))
+    place = call(place_kernel, jax.ShapeDtypeStruct(place.shape, f32), [VMEM], flops=LONG)(place)
 
     ring = list(range(0, chips, 2)) + list(range(1, chips, 2))[::-1]
     steps = [(ring[i], ring[(i + 1) % chips]) for i in range(chips)]
@@ -272,7 +276,7 @@
     normed, outer_edge, inner_edge = call(
         norm_kernel,
         [jax.ShapeDtypeStruct((rows, width), bf16), edge, edge],
-        [SMEM, VMEM, VMEM],
+        [VMEM, VMEM, VMEM],
         flops=LONG,
     )(place, frames, gain)
     outer = send(outer_edge, cross)
@@ -298,7 +302,7 @@
     query, *carry = call(
         functools.partial(first_kernel, start=3 * rows),
         [jax.ShapeDtypeStruct((query_rows, width), bf16)] + state + tall(4),
-        [SMEM] + [VMEM] * 11,
+        [VMEM] + [VMEM] * 11,
         [pltpu.VMEM((2 * HALO, width), bf16), pltpu.VMEM((rows, width), bf16)],
         aliases={10: 5, 11: 6},
         flops=FIRST,
@@ -324,9 +328,12 @@
     block_out, *_ = call(
         last_kernel,
         [jax.ShapeDtypeStruct((rows, width), f32)] + tall(2),
-        [SMEM] + [VMEM] * 17,
-        [pltpu.VMEM((8, LANES), f32)] + [pltpu.VMEM((query_rows, width), f32)] * 5,
+        [VMEM] + [VMEM] * 17,
+        [pltpu.VMEM((8, LANES), f32)]
+        + [pltpu.VMEM((query_rows, width), f32)] * 5
+        + [pltpu.VMEM((rows, width), f32), pltpu.SemaphoreType.DMA((width // LANES,))],
         aliases={2: 1, 3: 2},
+        out_specs=[HBM, VMEM, VMEM],
     )(
         place, other, *pool, query, key_weight, value_weight, *carry,
         frames, outer, inner, output_weight, mixer_gain.reshape(1, width), depthwise, mixer_bias.reshape(1, width),

time: 61.9 us -> 59.4 us (0.960)
  Pallas kernels: 40.3 us -> 38.4 us
  local copies, waits for them, and re-layouts: 1.89 us -> 1.27 us
    pallas_call x1, Pallas kernels: 13.1 us -> 12.2 us  [per_device(): call(last_kernel, [jax.ShapeDtypeStruct((rows, width), f32)] + tall(2), [...]
    unnamed x22 -> x18, local copies, waits for them, and re-layouts: 1.87 us -> 1.17 us
  transfers between devices with their start and end apart: 9 -> 9, of which waited for: 2 -> 2; matrix products, arithmetic and copies ran while one was open for 0% -> 0% of each run, Pallas kernels for 43% -> 44%
where the time goes in v3:
time: 59.4 us; the launch traced here: 58.9 us
  Pallas kernels  38.4 us (65%)
  starting transfers between devices  12.1 us (20%)
  waiting for transfers between devices  4.09 us (7%)
  blocking collectives  2.7 us (5%)
  local copies, waits for them, and re-layouts  1.27 us (2%)
    pallas_call x1, Pallas kernels, per_device(): call(functools.partial(first_kernel, start=3 * rows), [jax.ShapeDtypeStru...  12.4 us
    pallas_call x1, Pallas kernels, per_device(): call(last_kernel, [jax.ShapeDtypeStruct((rows, width), f32)] + tall(2), [...  12.2 us
    ppermute x9, starting transfers between devices, send(): return lax.ppermute(value, 'ctx', pairs)  12.1 us
    pallas_call x1, Pallas kernels, per_device(): call(block_kernel, list(state), [VMEM] * 8, projected, flops=BLOCK)  9.08 us
    ppermute x9, waiting for transfers between devices, send(): return lax.ppermute(value, 'ctx', pairs)  4.09 us
    all_gather x1, blocking collectives, per_device(): lax.all_gather(block, 'ctx', axis=0, tiled=True, axis_index_groups=siblings)  2.7 us
    pallas_call x1, Pallas kernels, per_device(): call(own_kernel, [jax.ShapeDtypeStruct((rows, width), bf16)] + tall(4), [...  2.29 us
  transfers between devices with their start and end apart: 9, of which 2 were waited for; matrix products, arithmetic and copies ran while one was open for 0% of the time, Pallas kernels for 44%

profile of v3, /device:TPU:1, one launch (start us, length us, event | category | flops | bytes accessed | tf_op | source)
XLA Modules:
  0.0 58.9 jit_solution(15031120600818862095)
XLA Ops:
  0.0 0.1 add_convert_fusion
  0.1 0.1 broadcast_in_dim.2.place
  0.2 1.1 %copy-done.4 = f32[192,1024]{1,0:T(8,128)S(1)} copy-done((f32[192,1024]{1,0:T(8,128)S(1)}, f32[192,1024]{1,0:T(8,128)}, u32[]{:S(2)}) %copy-start.4) | copy-done | bytes 786456
  1.3 0.3 shard_map.92
  1.6 0.1 collective-permute-start.1
  1.7 3.8 %collective-permute-start = (bf16[192,1024]{1,0:T(8,128)(2,1)S(1)}, bf16[192,1024]{1,0:T(8,128)(2,1)S(1)}, u32[]{:S(2)}, u32[]{:S(2)}) collective-permute-start(bf16[192,1024]{1,0:T(8,128)(2,1)S(1)} %get-tuple-element.33.normed), channel_id=1, source_target_pairs={{0,4},{1,5},{4,6},{5,7},{6,2},{7,3},{2,0},{3,1},{8,12},{9,13},{12,... | collective-permute-start | bytes 1179656 | tf_op jit(solution)/shard_map/ppermute | solution.py:270
  5.5 1.9 %collective-permute-start.2 = (f32[16,1024]{1,0:T(8,128)S(1)}, f32[16,1024]{1,0:T(8,128)S(1)}, u32[]{:S(2)}, u32[]{:S(2)}) collective-permute-start(f32[16,1024]{1,0:T(8,128)S(1)} %get-tuple-element.35), channel_id=1, source_target_pairs={{1,2},{2,1},{3,4},{4,3},{5,6},{6,5},{9,10},{10,9},{11,12},{12,11},... | collective-permute-start | bytes 196616 | tf_op jit(solution)/shard_map/ppermute | solution.py:270
  7.4 0.1 collective-permute-start.3
  7.5 1.9 %collective-permute-start.5 = (bf16[192,1024]{1,0:T(8,128)(2,1)S(1)}, bf16[192,1024]{1,0:T(8,128)(2,1)S(1)}, u32[]{:S(2)}, u32[]{:S(2)}) collective-permute-start(bf16[192,1024]{1,0:T(8,128)(2,1)S(1)} %get-tuple-element.33.normed), channel_id=1, source_target_pairs={{4,0},{5,1},{6,4},{7,5},{2,6},{3,7},{0,2},{1,3},{12,8},{13,9},{14,... | collective-permute-start | bytes 1179656 | tf_op jit(solution)/shard_map/ppermute | solution.py:270
  9.3 2.3 %shard_map.93 = (bf16[192,1024]{1,0:T(8,128)(2,1)S(1)}, bf16[768,1024]{1,0:T(8,128)(2,1)S(1)}, bf16[768,1024]{1,0:T(8,128)(2,1)S(1)}) custom-call(bf16[192,1024]{1,0:T(8,128)(2,1)S(1)} %get-tuple-element.33.normed, bf16[192,1024]{1,0:T(8,128)(2,1)S(1)} %collective-permute-done.1.sibling, bf16[1024,1024]{1,0:T(8,128)(2,1)S(1)} %copy-done.2, ...), custom_call_target="tpu_custom_call" | custom-call | flops 1024 | bytes 1024 | tf_op jit(solution)/shard_map/pallas_call | solution.py:290
  11.6 3.8 %collective-permute-done.2.outer = f32[16,1024]{1,0:T(8,128)S(1)} collective-permute-done((f32[16,1024]{1,0:T(8,128)S(1)}, f32[16,1024]{1,0:T(8,128)S(1)}, u32[]{:S(2)}, u32[]{:S(2)}) %collective-permute-start.2) | collective-permute-done | bytes 65568 | tf_op jit(solution)/shard_map/ppermute | solution.py:270
  15.4 0.1 collective-permute-start.7
  15.5 0.5 collective-permute-start.6
  16.0 3.4 %collective-permute-start.4 = (bf16[192,1024]{1,0:T(8,128)(2,1)S(1)}, bf16[192,1024]{1,0:T(8,128)(2,1)S(1)}, u32[]{:S(2)}, u32[]{:S(2)}) collective-permute-start(bf16[192,1024]{1,0:T(8,128)(2,1)S(1)} %collective-permute-done.block), channel_id=1, source_target_pairs={{0,4},{1,5},{4,6},{5,7},{6,2},{7,3},{2,0},{3,1},{8,12},{9,13},{12,... | collective-permute-start | bytes 1179656 | tf_op jit(solution)/shard_map/ppermute | solution.py:270
  19.4 1.0 %shard_map.94 = (bf16[768,1024]{1,0:T(8,128)(2,1)S(1)}, bf16[768,1024]{1,0:T(8,128)(2,1)S(1)}) custom-call(bf16[192,1024]{1,0:T(8,128)(2,1)S(1)} %collective-permute-done.block, bf16[1024,1024]{1,0:T(8,128)(2,1)S(1)} %copy-done, bf16[1024,1024]{1,0:T(8,128)(2,1)S(1)} %copy-done.1, ...), custom_call_target="tpu_custom_call", output_to_operand_aliasing={{0}: (3, {}), {1}: (4, {})} | custom-call | flops 1024 | bytes 1024 | tf_op jit(solution)/shard_map/pallas_call | solution.py:299
  20.5 12.4 %shard_map.95 = (bf16[224,1024]{1,0:T(8,128)(2,1)S(1)}, f32[8,128]{1,0:T(8,128)S(1)}, f32[224,1024]{1,0:T(8,128)S(1)}, f32[224,1024]{1,0:T(8,128)S(1)}, f32[224,...) custom-call(f32[3,128]{1,0:T(4,128)S(1)} %shard_map.91.place, ...), custom_call_target="tpu_custom_call", output_to_operand_aliasing={{5}: (10, {}), {6}: (11, {})} | custom-call | flops 1024 | bytes 1024 | tf_op jit(solution)/shard_map/pallas_call | solution.py:302
  32.9 2.7 %all_gather.3.block = bf16[384,1024]{1,0:T(8,128)(2,1)S(1)} all-gather(bf16[192,1024]{1,0:T(8,128)(2,1)S(1)} %collective-permute-done.5), channel_id=1, replica_groups={{0,1},{2,3},{4,5},{6,7},{8,9},{10,11},{12,13},{14,15},{16,17},{18,19},{..., dimensions={0}, use_global_device_ids=true | all-gather | bytes 1179648 | tf_op jit(solution)/shard_map/all_gather | solution.py:319
  35.6 9.1 %shard_map.96 = (f32[8,128]{1,0:T(8,128)S(1)}, f32[224,1024]{1,0:T(8,128)S(1)}, f32[224,1024]{1,0:T(8,128)S(1)}, f32[224,1024]{1,0:T(8,128)S(1)}) custom-call(bf16[384,1024]{1,0:T(8,128)(2,1)S(1)} %all_gather.3.block, bf16[224,1024]{1,0:T(8,128)(2,1)S(1)} %get-tuple-element.47.query, bf16[1024,1024]{1,0:T(8,128)(2,1)S(1)} %copy-done, ...), custom_call_target="tpu_custom_call" | custom-call | flops 1000000000 | bytes 1024 | tf_op jit(solution)/shard_map/pallas_call | solution.py:321
  44.7 0.0 copy-start.3
  44.7 0.0 copy-start.5
  44.7 0.4 collective-permute-start.8
  45.2 1.0 %shard_map.97 = (bf16[384,1024]{1,0:T(8,128)(2,1)S(1)}, bf16[384,1024]{1,0:T(8,128)(2,1)S(1)}) custom-call(bf16[192,1024]{1,0:T(8,128)(2,1)S(1)} %collective-permute-done.4.block, bf16[1024,1024]{1,0:T(8,128)(2,1)S(1)} %copy-done, bf16[1024,1024]{1,0:T(8,128)(2,1)S(1)} %copy-done.1), custom_call_target="tpu_custom_call" | custom-call | flops 1024 | bytes 1024 | tf_op jit(solution)/shard_map/pallas_call | solution.py:327
  46.2 0.3 collective-permute-done.8.sibling
  46.5 12.2 %shard_map.98 = (f32[192,1024]{1,0:T(8,128)}, bf16[384,1024]{1,0:T(8,128)(2,1)S(1)}, bf16[384,1024]{1,0:T(8,128)(2,1)S(1)}) custom-call(f32[3,128]{1,0:T(4,128)S(1)} %shard_map.91.place, bf16[192,1024]{1,0:T(8,128)(2,1)S(1)} %collective-permute-done.8.sibling, ...), custom_call_target="tpu_custom_call", output_to_operand_aliasing={{1}: (2, {}), {2}: (3, {})} | custom-call | flops 1024 | bytes 1024 | tf_op jit(solution)/shard_map/pallas_call | solution.py:328
  (24 shorter events, 0.1 us)
Async XLA Ops:
  0.2 1.1 %copy-start.4 = (f32[192,1024]{1,0:T(8,128)S(1)}, f32[192,1024]{1,0:T(8,128)}, u32[]{:S(2)}) copy-start(f32[192,1024]{1,0:T(8,128)} %frames.3) | copy-start | bytes 2359300
  0.2 1.1 %copy-start.6 = (f32[1024]{0:T(1024)S(1)}, f32[1024]{0:T(1024)}, u32[]{:S(2)}) copy-start(f32[1024]{0:T(1024)} %param.10) | copy-start | bytes 12292
  1.3 8.0 %copy-start = (bf16[1024,1024]{1,0:T(8,128)(2,1)S(1)}, bf16[1024,1024]{1,0:T(8,128)(2,1)}, u32[]{:S(2)}) copy-start(bf16[1024,1024]{1,0:T(8,128)(2,1)} %key_weight.11) | copy-start | bytes 6291460
  1.3 8.0 %copy-start.1 = (bf16[1024,1024]{1,0:T(8,128)(2,1)S(1)}, bf16[1024,1024]{1,0:T(8,128)(2,1)}, u32[]{:S(2)}) copy-start(bf16[1024,1024]{1,0:T(8,128)(2,1)} %value_weight.11) | copy-start | bytes 6291460
  1.3 8.0 %copy-start.2 = (bf16[1024,1024]{1,0:T(8,128)(2,1)S(1)}, bf16[1024,1024]{1,0:T(8,128)(2,1)}, u32[]{:S(2)}) copy-start(bf16[1024,1024]{1,0:T(8,128)(2,1)} %query_weight.3) | copy-start | bytes 6291460
  1.6 7.7 %collective-permute-start.1 = (bf16[192,1024]{1,0:T(8,128)(2,1)S(1)}, bf16[192,1024]{1,0:T(8,128)(2,1)S(1)}, u32[]{:S(2)}, u32[]{:S(2)}) collective-permute-start(bf16[192,1024]{1,0:T(8,128)(2,1)S(1)} %get-tuple-element.33.normed), channel_id=1, source_target_pairs={{0,1},{1,0},{2,3},{3,2},{4,5},{5,4},{6,7},{7,6},{8,9},{9,8},{10,11... | collective-permute-start | bytes 1179656 | tf_op jit(solution)/shard_map/ppermute | solution.py:270
  1.7 13.7 %collective-permute-start = (bf16[192,1024]{1,0:T(8,128)(2,1)S(1)}, bf16[192,1024]{1,0:T(8,128)(2,1)S(1)}, u32[]{:S(2)}, u32[]{:S(2)}) collective-permute-start(bf16[192,1024]{1,0:T(8,128)(2,1)S(1)} %get-tuple-element.33.normed), channel_id=1, source_target_pairs={{0,4},{1,5},{4,6},{5,7},{6,2},{7,3},{2,0},{3,1},{8,12},{9,13},{12,... | collective-permute-start | bytes 1179656 | tf_op jit(solution)/shard_map/ppermute | solution.py:270
  5.5 9.9 %collective-permute-start.2 = (f32[16,1024]{1,0:T(8,128)S(1)}, f32[16,1024]{1,0:T(8,128)S(1)}, u32[]{:S(2)}, u32[]{:S(2)}) collective-permute-start(f32[16,1024]{1,0:T(8,128)S(1)} %get-tuple-element.35), channel_id=1, source_target_pairs={{1,2},{2,1},{3,4},{4,3},{5,6},{6,5},{9,10},{10,9},{11,12},{12,11},... | collective-permute-start | bytes 196616 | tf_op jit(solution)/shard_map/ppermute | solution.py:270
  7.4 8.0 %collective-permute-start.3 = (f32[16,1024]{1,0:T(8,128)S(1)}, f32[16,1024]{1,0:T(8,128)S(1)}, u32[]{:S(2)}, u32[]{:S(2)}) collective-permute-start(f32[16,1024]{1,0:T(8,128)S(1)} %get-tuple-element.36), channel_id=1, source_target_pairs={{0,1},{1,0},{2,3},{3,2},{4,5},{5,4},{6,7},{7,6},{8,9},{9,8},{10,11... | collective-permute-start | bytes 196616 | tf_op jit(solution)/shard_map/ppermute | solution.py:270
  7.5 25.4 %collective-permute-start.5 = (bf16[192,1024]{1,0:T(8,128)(2,1)S(1)}, bf16[192,1024]{1,0:T(8,128)(2,1)S(1)}, u32[]{:S(2)}, u32[]{:S(2)}) collective-permute-start(bf16[192,1024]{1,0:T(8,128)(2,1)S(1)} %get-tuple-element.33.normed), channel_id=1, source_target_pairs={{4,0},{5,1},{6,4},{7,5},{2,6},{3,7},{0,2},{1,3},{12,8},{13,9},{14,... | collective-permute-start | bytes 1179656 | tf_op jit(solution)/shard_map/ppermute | solution.py:270
  15.4 5.0 %collective-permute-start.7 = (bf16[96,1024]{1,0:T(8,128)(2,1)S(1)}, bf16[96,1024]{1,0:T(8,128)(2,1)S(1)}, u32[]{:S(2)}, u32[]{:S(2)}) collective-permute-start(bf16[96,1024]{1,0:T(8,128)(2,1)S(1)} %get-tuple-element.61), channel_id=1, source_target_pairs={{0,1},{1,0},{2,3},{3,2},{4,5},{5,4},{6,7},{7,6},{8,9},{9,8},{10,11... | collective-permute-start | bytes 589832 | tf_op jit(solution)/shard_map/ppermute | solution.py:270
  15.5 4.9 %collective-permute-start.6 = (bf16[96,1024]{1,0:T(8,128)(2,1)S(1)}, bf16[96,1024]{1,0:T(8,128)(2,1)S(1)}, u32[]{:S(2)}, u32[]{:S(2)}) collective-permute-start(bf16[96,1024]{1,0:T(8,128)(2,1)S(1)} %get-tuple-element.62), channel_id=1, source_target_pairs={{0,1},{1,0},{2,3},{3,2},{4,5},{5,4},{6,7},{7,6},{8,9},{9,8},{10,11... | collective-permute-start | bytes 589832 | tf_op jit(solution)/shard_map/ppermute | solution.py:270
  16.0 28.7 %collective-permute-start.4 = (bf16[192,1024]{1,0:T(8,128)(2,1)S(1)}, bf16[192,1024]{1,0:T(8,128)(2,1)S(1)}, u32[]{:S(2)}, u32[]{:S(2)}) collective-permute-start(bf16[192,1024]{1,0:T(8,128)(2,1)S(1)} %collective-permute-done.block), channel_id=1, source_target_pairs={{0,4},{1,5},{4,6},{5,7},{6,2},{7,3},{2,0},{3,1},{8,12},{9,13},{12,... | collective-permute-start | bytes 1179656 | tf_op jit(solution)/shard_map/ppermute | solution.py:270
  44.7 1.8 %copy-start.3 = (bf16[1024,1024]{1,0:T(8,128)(2,1)S(1)}, bf16[1024,1024]{1,0:T(8,128)(2,1)}, u32[]{:S(2)}) copy-start(bf16[1024,1024]{1,0:T(8,128)(2,1)} %output_weight.1) | copy-start | bytes 6291460
  44.7 1.8 %copy-start.5 = (f32[31,1024]{1,0:T(8,128)S(1)}, f32[31,1024]{1,0:T(8,128)}, u32[]{:S(2)}) copy-start(f32[31,1024]{1,0:T(8,128)} %depthwise.1) | copy-start | bytes 380932
  44.7 1.8 %copy-start.7 = (f32[1024]{0:T(1024)S(1)}, f32[1024]{0:T(1024)}, u32[]{:S(2)}) copy-start(f32[1024]{0:T(1024)} %param.15) | copy-start | bytes 12292
  44.7 1.8 %copy-start.8 = (f32[1024]{0:T(1024)S(1)}, f32[1024]{0:T(1024)}, u32[]{:S(2)}) copy-start(f32[1024]{0:T(1024)} %param.17) | copy-start | bytes 12292
  44.7 1.8 %collective-permute-start.8 = (bf16[192,1024]{1,0:T(8,128)(2,1)S(1)}, bf16[192,1024]{1,0:T(8,128)(2,1)S(1)}, u32[]{:S(2)}, u32[]{:S(2)}) collective-permute-start(bf16[192,1024]{1,0:T(8,128)(2,1)S(1)} %collective-permute-done.4.block), channel_id=1, source_target_pairs={{0,1},{1,0},{2,3},{3,2},{4,5},{5,4},{6,7},{7,6},{8,9},{9,8},{10,11... | collective-permute-start | bytes 1179656 | tf_op jit(solution)/shard_map/ppermute | solution.py:270

commit v4 on v3

--- a/solution.py
+++ b/solution.py
@@ -13,6 +13,7 @@
 LANES = 128
 SPAN = 256
 EPSILON = 1e-05
+PIECES = 3
 CEILING = 1e30
 FLOOR = 1e-18
 VMEM_LIMIT = 24 * 1024 * 1024
@@ -20,7 +21,7 @@
 FIRST = 1024
 OWN = 1024
 ADD = 1024
-BLOCK = 1 * 10**9
+BLOCK = 0 * 10**9 + 1024
 
 VMEM = pl.BlockSpec(memory_space=pltpu.VMEM)
 HBM = pl.BlockSpec(memory_space=pltpu.HBM)
@@ -57,6 +58,12 @@
             ).astype(bf16)
 
 
+def collect(pieces, block):
+    size = pieces[0].shape[0]
+    for index, piece in enumerate(pieces):
+        block[index * size : (index + 1) * size, :] = piece[...]
+
+
 def pair_scores(query, keys, span):
     low_half = lax.broadcasted_iota(jnp.int32, (query.shape[0], LANES), 1) < LANES // 2
     pair = query[:, span]
@@ -76,7 +83,7 @@
     return totals, jnp.where(low_half, out[:rows, :LANES], out[rows:, :LANES])
 
 
-def attend(query, keys, values, old, new):
+def attend(query, keys, values, old, new, context=None):
     query_rows, width = query.shape
     pairs = width // LANES
     most = least = None
@@ -90,18 +97,23 @@
         if old is not None:
             totals = old[2][:, span] + totals
             running = old[3][:, span] + running
-        new[2][:, span] = totals
-        new[3][:, span] = running
+        if context is not None:
+            context[:, span] = (running / totals).astype(bf16)
+        else:
+            new[2][:, span] = totals
+            new[3][:, span] = running
         most = totals if most is None else jnp.maximum(most, totals)
         least = totals if least is None else jnp.minimum(least, totals)
     fits = jnp.logical_and(jnp.max(most) < CEILING, jnp.min(least) > FLOOR)
     if old is not None:
         fits = jnp.logical_and(fits, jnp.max(old[0][...]) == 0.0)
-    new[0][...] = jnp.zeros_like(new[0])
+    if new is not None:
+        new[0][...] = jnp.zeros_like(new[0])
 
     @pl.when(jnp.logical_not(fits))
     def _():
-        new[0][...] = jnp.ones_like(new[0])
+        if new is not None:
+            new[0][...] = jnp.ones_like(new[0])
 
         @pl.loop(0, pairs)
         def _(pair):
@@ -119,9 +131,12 @@
                 totals = old[2][:, span] * old_scale + totals * scale
                 running = old[3][:, span] * old_scale + running * scale
                 top = new_top
-            new[1][:, span] = top
-            new[2][:, span] = totals
-            new[3][:, span] = running
+            if context is not None:
+                context[:, span] = (running / totals).astype(bf16)
+            else:
+                new[1][:, span] = top
+                new[2][:, span] = totals
+                new[3][:, span] = running
 
 
 def scaled_query(rows, query_weight, span, width):
@@ -129,13 +144,16 @@
     return jnp.dot(rows, query_weight[:, span], preferred_element_type=f32).astype(bf16) * scale
 
 
-def own_kernel(normed, sibling, query_weight, key_weight, value_weight, query, keys, values):
+def own_kernel(*refs):
+    normed, query_weight, key_weight, value_weight = refs[:4]
+    pieces, (query, keys, values, block) = refs[4 : 4 + PIECES], refs[4 + PIECES :]
     rows, width = normed.shape
     for low in range(0, width, SPAN):
         span = slice(low, low + SPAN)
         query[:, span] = scaled_query(normed[...], query_weight, span, width)
+    collect(pieces, block)
     project(normed, key_weight, value_weight, keys, values, 0)
-    project(sibling, key_weight, value_weight, keys, values, rows)
+    project(block, key_weight, value_weight, keys, values, rows)
 
 
 def add_kernel(block, key_weight, value_weight, keys_in, values_in, keys, values, *, start):
@@ -147,11 +165,10 @@
     project(block, key_weight, value_weight, keys, values, 0)
 
 
-def first_kernel(
-    place, own_query, outer, inner, gain, upper, lower, query_weight, key_weight, value_weight, keys_in, values_in,
-    query, shifted, highest, totals, running, keys, values, halo, block, *, start,
-):
-    del keys_in, values_in
+def first_kernel(*refs, start):
+    place, own_query, outer, inner, gain, query_weight, key_weight, value_weight = refs[:8]
+    pieces, outs = refs[10 : 10 + PIECES], refs[10 + PIECES :]
+    query, shifted, highest, totals, running, keys, values, halo, block = outs
     rows, width = own_query.shape
     is_high = place[:1, :1] > 0
     halo[:HALO, :] = norm_rows(jnp.where(is_high, inner[...], outer[...]), gain[...]).astype(bf16)
@@ -162,9 +179,9 @@
         edges = scaled_query(halo[...], query_weight, span, width)
         query[:HALO, span] = edges[:HALO]
         query[HALO + rows :, span] = edges[HALO:]
-    half = upper.shape[0]
-    block[:half, :] = upper[...]
-    block[half:, :] = lower[...]
+    for index, piece in enumerate(pieces):
+        size = piece.shape[0]
+        block[index * size : (index + 1) * size, :] = piece[...]
     project(block, key_weight, value_weight, keys, values, start)
     attend(query, keys, values, None, (shifted, highest, totals, running))
 
@@ -181,24 +198,21 @@
 
 def last_kernel(
     place, sibling, keys_in, values_in, query, key_weight, value_weight,
-    shifted_in, highest_in, totals_in, running_in,
+    shifted, highest, totals, running,
     frames, outer, inner, output_weight, gain, depthwise, bias,
-    block_out, keys, values, shifted, highest, totals, running, attended, mixer_in, held, sems,
+    block_out, keys, values, context, attended, mixer_in, held, sems,
 ):
     del keys_in, values_in
     rows, width = frames.shape
     project(sibling, key_weight, value_weight, keys, values, rows)
-    attend(
-        query, keys, values, (shifted_in, highest_in, totals_in, running_in), (shifted, highest, totals, running)
-    )
+    attend(query, keys, values, (shifted, highest, totals, running), None, context)
     is_high = place[:1, :1] > 0
-    context = (running[...] / totals[...]).astype(bf16)
     attended[:HALO, :] = jnp.where(is_high, inner[...], outer[...])
     attended[HALO : HALO + rows, :] = frames[...]
     attended[HALO + rows :, :] = jnp.where(is_high, outer[...], inner[...])
     for low in range(0, width, SPAN):
         span = slice(low, low + SPAN)
-        attended[:, span] += jnp.dot(context, output_weight[:, span], preferred_element_type=f32)
+        attended[:, span] += jnp.dot(context[...], output_weight[:, span], preferred_element_type=f32)
     mixer_in[...] = norm_rows(attended[...], gain[...])
 
     mixer_in[:HALO, :] = jnp.where(place[1:2, :1] > 0, mixer_in[:HALO, :], 0.0)
@@ -282,31 +296,39 @@
     outer = send(outer_edge, cross)
     ahead = send(normed, forward)
     inner = send(inner_edge, swap)
-    sibling = send(normed, swap)
+    size = rows // PIECES
+    sibling = [send(normed[start : start + size], swap) for start in range(0, rows, size)]
     def tall(blocks):
         return [jax.ShapeDtypeStruct((blocks * rows, width), bf16)] * 2
 
     projected = [pltpu.VMEM((2 * rows, width), bf16)] * 2
     own_query, *pool = call(
-        own_kernel, [jax.ShapeDtypeStruct((rows, width), bf16)] + tall(4), [VMEM] * 5, flops=OWN
-    )(normed, sibling, query_weight, key_weight, value_weight)
+        own_kernel,
+        [jax.ShapeDtypeStruct((rows, width), bf16)] + tall(4),
+        [VMEM] * (4 + PIECES),
+        [pltpu.VMEM((rows, width), bf16)],
+        flops=OWN,
+    )(normed, query_weight, key_weight, value_weight, *sibling)
     behind = send(normed, backward)
 
-    block, own_query, outer, inner = lax.optimization_barrier((ahead, own_query, outer, inner))
+    block, own_query, inner = lax.optimization_barrier((ahead, own_query, inner))
     ahead = send(block, forward)
-    half = rows // 2
-    upper, lower = send(block[:half], swap), send(block[half:], swap)
+    kept, outer = lax.optimization_barrier((block, outer))
+    size = rows // PIECES
+    pieces = [send(kept[start : start + size], swap) for start in range(0, rows, size)]
     pool = call(
         functools.partial(add_kernel, start=2 * rows), tall(4), [VMEM] * 5, aliases={3: 0, 4: 1}, flops=ADD
     )(block, key_weight, value_weight, *pool)
     query, *carry = call(
         functools.partial(first_kernel, start=3 * rows),
         [jax.ShapeDtypeStruct((query_rows, width), bf16)] + state + tall(4),
-        [VMEM] + [VMEM] * 11,
+        [VMEM] * (10 + PIECES),
         [pltpu.VMEM((2 * HALO, width), bf16), pltpu.VMEM((rows, width), bf16)],
-        aliases={10: 5, 11: 6},
+        aliases={8: 5, 9: 6},
         flops=FIRST,
-    )(place, own_query, outer, inner, gain, upper, lower, query_weight, key_weight, value_weight, *pool)
+    )(
+        place, own_query, outer, inner, gain, query_weight, key_weight, value_weight, *pool, *pieces
+    )
     carry = carry[:4]
     for step in range(2, chips - 1):
         if step % 2:
@@ -329,8 +351,8 @@
         last_kernel,
         [jax.ShapeDtypeStruct((rows, width), f32)] + tall(2),
         [VMEM] + [VMEM] * 17,
-        [pltpu.VMEM((8, LANES), f32)]
-        + [pltpu.VMEM((query_rows, width), f32)] * 5
+        [pltpu.VMEM((query_rows, width), bf16)]
+        + [pltpu.VMEM((query_rows, width), f32)] * 2
         + [pltpu.VMEM((rows, width), f32), pltpu.SemaphoreType.DMA((width // LANES,))],
         aliases={2: 1, 3: 2},
         out_specs=[HBM, VMEM, VMEM],

time: 59.4 us -> 59 us (level)
  waiting for transfers between devices: 4.09 us -> 0.83 us
  starting transfers between devices: 12.1 us -> 15.2 us
    ppermute x9 -> x12, waiting for transfers between devices: 4.09 us -> 0.83 us  [send(): return lax.ppermute(value, 'ctx', pairs)]
    ppermute x9 -> x12, starting transfers between devices: 12.1 us -> 15.2 us  [send(): return lax.ppermute(value, 'ctx', pairs)]
  transfers between devices with their start and end apart: 9 -> 12, of which waited for: 2 -> 2; matrix products, arithmetic and copies ran while one was open for 0% -> 0% of each run, Pallas kernels for 44% -> 44%
where the time goes in v4:
time: 59 us; the launch traced here: 58.7 us
  Pallas kernels  38.5 us (65%)
  starting transfers between devices  15.2 us (26%)
  blocking collectives  2.37 us (4%)
  local copies, waits for them, and re-layouts  1.3 us (2%)
  waiting for transfers between devices  0.83 us (1%)
    ppermute x12, starting transfers between devices, send(): return lax.ppermute(value, 'ctx', pairs)  15.2 us
    pallas_call x1, Pallas kernels, per_device(): call(functools.partial(first_kernel, start=3 * rows), [jax.ShapeDtypeStru...  12.5 us
    pallas_call x1, Pallas kernels, per_device(): call(last_kernel, [jax.ShapeDtypeStruct((rows, width), f32)] + tall(2), [...  12.3 us
    pallas_call x1, Pallas kernels, per_device(): call(block_kernel, list(state), [VMEM] * 8, projected, flops=BLOCK)  9.08 us
    all_gather x1, blocking collectives, per_device(): lax.all_gather(block, 'ctx', axis=0, tiled=True, axis_index_groups=siblings)  2.37 us
    pallas_call x1, Pallas kernels, per_device(): call(own_kernel, [jax.ShapeDtypeStruct((rows, width), bf16)] + tall(4), [...  2.28 us
  transfers between devices with their start and end apart: 12, of which 2 were waited for; matrix products, arithmetic and copies ran while one was open for 0% of the time, Pallas kernels for 44%

profile of v4, /device:TPU:1, one launch (start us, length us, event | category | flops | bytes accessed | tf_op | source)
XLA Modules:
  0.0 58.7 jit_solution(2322134796424356489)
XLA Ops:
  0.0 0.1 add_convert_fusion
  0.2 1.1 %copy-done.4 = f32[192,1024]{1,0:T(8,128)S(1)} copy-done((f32[192,1024]{1,0:T(8,128)S(1)}, f32[192,1024]{1,0:T(8,128)}, u32[]{:S(2)}) %copy-start.4) | copy-done | bytes 786456
  1.3 0.3 shard_map.92
  1.6 3.2 %collective-permute-start = (bf16[192,1024]{1,0:T(8,128)(2,1)S(1)}, bf16[192,1024]{1,0:T(8,128)(2,1)S(1)}, u32[]{:S(2)}, u32[]{:S(2)}) collective-permute-start(bf16[192,1024]{1,0:T(8,128)(2,1)S(1)} %get-tuple-element.34.refs_0_), channel_id=1, source_target_pairs={{0,4},{1,5},{4,6},{5,7},{6,2},{7,3},{2,0},{3,1},{8,12},{9,13},{12,... | collective-permute-start | bytes 1179656 | tf_op jit(solution)/shard_map/ppermute | solution.py:284
  4.8 1.0 %collective-permute-start.3 = (bf16[64,1024]{1,0:T(8,128)(2,1)S(1)}, bf16[64,1024]{1,0:T(8,128)(2,1)S(1)}, u32[]{:S(2)}, u32[]{:S(2)}) collective-permute-start(bf16[64,1024]{1,0:T(8,128)(2,1)S(1)} %get-tuple-element.66), channel_id=1, source_target_pairs={{0,1},{1,0},{2,3},{3,2},{4,5},{5,4},{6,7},{7,6},{8,9},{9,8},{10,11... | collective-permute-start | bytes 393224 | tf_op jit(solution)/shard_map/ppermute | solution.py:284
  5.8 0.1 collective-permute-start.2
  5.9 0.4 collective-permute-start.1
  6.4 0.1 collective-permute-start.4
  6.4 0.4 collective-permute-done.3.refs_6_
  6.8 1.9 %collective-permute-start.7 = (f32[16,1024]{1,0:T(8,128)S(1)}, f32[16,1024]{1,0:T(8,128)S(1)}, u32[]{:S(2)}, u32[]{:S(2)}) collective-permute-start(f32[16,1024]{1,0:T(8,128)S(1)} %get-tuple-element.39), channel_id=1, source_target_pairs={{1,2},{2,1},{3,4},{4,3},{5,6},{6,5},{9,10},{10,9},{11,12},{12,11},... | collective-permute-start | bytes 196616 | tf_op jit(solution)/shard_map/ppermute | solution.py:284
  8.8 1.9 %collective-permute-start.6 = (bf16[192,1024]{1,0:T(8,128)(2,1)S(1)}, bf16[192,1024]{1,0:T(8,128)(2,1)S(1)}, u32[]{:S(2)}, u32[]{:S(2)}) collective-permute-start(bf16[192,1024]{1,0:T(8,128)(2,1)S(1)} %get-tuple-element.34.refs_0_), channel_id=1, source_target_pairs={{4,0},{5,1},{6,4},{7,5},{2,6},{3,7},{0,2},{1,3},{12,8},{13,9},{14,... | collective-permute-start | bytes 1179656 | tf_op jit(solution)/shard_map/ppermute | solution.py:284
  10.6 2.3 %shard_map.93 = (bf16[192,1024]{1,0:T(8,128)(2,1)S(1)}, bf16[768,1024]{1,0:T(8,128)(2,1)S(1)}, bf16[768,1024]{1,0:T(8,128)(2,1)S(1)}) custom-call(bf16[192,1024]{1,0:T(8,128)(2,1)S(1)} %get-tuple-element.34.refs_0_, bf16[1024,1024]{1,0:T(8,128)(2,1)S(1)} %copy-done.2, bf16[1024,1024]{1,0:T(8,128)(2,1)S(1)} %copy-done, bf16[1024,1024]{1,0:T(8,128)(2,1)S(1)} %copy-done.1, ...), custom_call_target="tpu_custom_call" | custom-call | flops 1024 | bytes 1024 | tf_op jit(solution)/shard_map/pallas_call | solution.py:305
  13.0 2.8 %collective-permute-start.5 = (bf16[192,1024]{1,0:T(8,128)(2,1)S(1)}, bf16[192,1024]{1,0:T(8,128)(2,1)S(1)}, u32[]{:S(2)}, u32[]{:S(2)}) collective-permute-start(bf16[192,1024]{1,0:T(8,128)(2,1)S(1)} %collective-permute-done.block), channel_id=1, source_target_pairs={{0,4},{1,5},{4,6},{5,7},{6,2},{7,3},{2,0},{3,1},{8,12},{9,13},{12,... | collective-permute-start | bytes 1179656 | tf_op jit(solution)/shard_map/ppermute | solution.py:284
  15.7 3.0 %collective-permute-start.10 = (bf16[64,1024]{1,0:T(8,128)(2,1)S(1)}, bf16[64,1024]{1,0:T(8,128)(2,1)S(1)}, u32[]{:S(2)}, u32[]{:S(2)}) collective-permute-start(bf16[64,1024]{1,0:T(8,128)(2,1)S(1)} %get-tuple-element.63), channel_id=1, source_target_pairs={{0,1},{1,0},{2,3},{3,2},{4,5},{5,4},{6,7},{7,6},{8,9},{9,8},{10,11... | collective-permute-start | bytes 393224 | tf_op jit(solution)/shard_map/ppermute | solution.py:284
  18.8 0.1 collective-permute-start.9
  18.9 0.4 collective-permute-start.8
  19.3 1.0 %shard_map.94 = (bf16[768,1024]{1,0:T(8,128)(2,1)S(1)}, bf16[768,1024]{1,0:T(8,128)(2,1)S(1)}) custom-call(bf16[192,1024]{1,0:T(8,128)(2,1)S(1)} %collective-permute-done.block, bf16[1024,1024]{1,0:T(8,128)(2,1)S(1)} %copy-done, bf16[1024,1024]{1,0:T(8,128)(2,1)S(1)} %copy-done.1, ...), custom_call_target="tpu_custom_call", output_to_operand_aliasing={{0}: (3, {}), {1}: (4, {})} | custom-call | flops 1024 | bytes 1024 | tf_op jit(solution)/shard_map/pallas_call | solution.py:319
  20.4 12.5 %shard_map.95 = (bf16[224,1024]{1,0:T(8,128)(2,1)S(1)}, f32[8,128]{1,0:T(8,128)S(1)}, f32[224,1024]{1,0:T(8,128)S(1)}, f32[224,1024]{1,0:T(8,128)S(1)}, f32[224,...) custom-call(f32[3,128]{1,0:T(4,128)S(1)} %shard_map.91.place.refs_0_, ...), custom_call_target="tpu_custom_call", output_to_operand_aliasing={{5}: (8, {}), {6}: (9, {})} | custom-call | flops 1024 | bytes 1024 | tf_op jit(solution)/shard_map/pallas_call | solution.py:322
  32.9 2.4 %all_gather.3.block = bf16[384,1024]{1,0:T(8,128)(2,1)S(1)} all-gather(bf16[192,1024]{1,0:T(8,128)(2,1)S(1)} %collective-permute-done.6), channel_id=1, replica_groups={{0,1},{2,3},{4,5},{6,7},{8,9},{10,11},{12,13},{14,15},{16,17},{18,19},{..., dimensions={0}, use_global_device_ids=true | all-gather | bytes 1179648 | tf_op jit(solution)/shard_map/all_gather | solution.py:341
  35.3 9.1 %shard_map.96 = (f32[8,128]{1,0:T(8,128)S(1)}, f32[224,1024]{1,0:T(8,128)S(1)}, f32[224,1024]{1,0:T(8,128)S(1)}, f32[224,1024]{1,0:T(8,128)S(1)}) custom-call(bf16[384,1024]{1,0:T(8,128)(2,1)S(1)} %all_gather.3.block, bf16[224,1024]{1,0:T(8,128)(2,1)S(1)} %get-tuple-element.49.query, bf16[1024,1024]{1,0:T(8,128)(2,1)S(1)} %copy-done, ...), custom_call_target="tpu_custom_call" | custom-call | flops 1024 | bytes 1024 | tf_op jit(solution)/shard_map/pallas_call | solution.py:343
  44.4 0.3 collective-permute-start.11
  44.7 1.0 %shard_map.97 = (bf16[384,1024]{1,0:T(8,128)(2,1)S(1)}, bf16[384,1024]{1,0:T(8,128)(2,1)S(1)}) custom-call(bf16[192,1024]{1,0:T(8,128)(2,1)S(1)} %collective-permute-done.5.block, bf16[1024,1024]{1,0:T(8,128)(2,1)S(1)} %copy-done, bf16[1024,1024]{1,0:T(8,128)(2,1)S(1)} %copy-done.1), custom_call_target="tpu_custom_call" | custom-call | flops 1024 | bytes 1024 | tf_op jit(solution)/shard_map/pallas_call | solution.py:349
  45.8 0.4 collective-permute-done.11.sibling
  46.2 12.3 %shard_map.98 = (f32[192,1024]{1,0:T(8,128)}, bf16[384,1024]{1,0:T(8,128)(2,1)S(1)}, bf16[384,1024]{1,0:T(8,128)(2,1)S(1)}) custom-call(f32[3,128]{1,0:T(4,128)S(1)} %shard_map.91.place.refs_0_, bf16[192,1024]{1,0:T(8,128)(2,1)S(1)} %collective-permute-done.11.sibling, ...), custom_call_target="tpu_custom_call", output_to_operand_aliasing={{1}: (2, {}), {2}: (3, {})} | custom-call | flops 1024 | bytes 1024 | tf_op jit(solution)/shard_map/pallas_call | solution.py:350
  (31 shorter events, 0.2 us)
Async XLA Ops:
  0.2 1.1 %copy-start.4 = (f32[192,1024]{1,0:T(8,128)S(1)}, f32[192,1024]{1,0:T(8,128)}, u32[]{:S(2)}) copy-start(f32[192,1024]{1,0:T(8,128)} %frames.3) | copy-start | bytes 2359300
  0.2 1.1 %copy-start.6 = (f32[1024]{0:T(1024)S(1)}, f32[1024]{0:T(1024)}, u32[]{:S(2)}) copy-start(f32[1024]{0:T(1024)} %param.10) | copy-start | bytes 12292
  1.3 9.3 %copy-start = (bf16[1024,1024]{1,0:T(8,128)(2,1)S(1)}, bf16[1024,1024]{1,0:T(8,128)(2,1)}, u32[]{:S(2)}) copy-start(bf16[1024,1024]{1,0:T(8,128)(2,1)} %key_weight.7) | copy-start | bytes 6291460
  1.3 9.3 %copy-start.1 = (bf16[1024,1024]{1,0:T(8,128)(2,1)S(1)}, bf16[1024,1024]{1,0:T(8,128)(2,1)}, u32[]{:S(2)}) copy-start(bf16[1024,1024]{1,0:T(8,128)(2,1)} %value_weight.7) | copy-start | bytes 6291460
  1.3 9.3 %copy-start.2 = (bf16[1024,1024]{1,0:T(8,128)(2,1)S(1)}, bf16[1024,1024]{1,0:T(8,128)(2,1)}, u32[]{:S(2)}) copy-start(bf16[1024,1024]{1,0:T(8,128)(2,1)} %refs_5_.1) | copy-start | bytes 6291460
  1.6 11.3 %collective-permute-start = (bf16[192,1024]{1,0:T(8,128)(2,1)S(1)}, bf16[192,1024]{1,0:T(8,128)(2,1)S(1)}, u32[]{:S(2)}, u32[]{:S(2)}) collective-permute-start(bf16[192,1024]{1,0:T(8,128)(2,1)S(1)} %get-tuple-element.34.refs_0_), channel_id=1, source_target_pairs={{0,4},{1,5},{4,6},{5,7},{6,2},{7,3},{2,0},{3,1},{8,12},{9,13},{12,... | collective-permute-start | bytes 1179656 | tf_op jit(solution)/shard_map/ppermute | solution.py:284
  4.8 2.0 %collective-permute-start.3 = (bf16[64,1024]{1,0:T(8,128)(2,1)S(1)}, bf16[64,1024]{1,0:T(8,128)(2,1)S(1)}, u32[]{:S(2)}, u32[]{:S(2)}) collective-permute-start(bf16[64,1024]{1,0:T(8,128)(2,1)S(1)} %get-tuple-element.66), channel_id=1, source_target_pairs={{0,1},{1,0},{2,3},{3,2},{4,5},{5,4},{6,7},{7,6},{8,9},{9,8},{10,11... | collective-permute-start | bytes 393224 | tf_op jit(solution)/shard_map/ppermute | solution.py:284
  5.8 2.9 %collective-permute-start.2 = (bf16[64,1024]{1,0:T(8,128)(2,1)S(1)}, bf16[64,1024]{1,0:T(8,128)(2,1)S(1)}, u32[]{:S(2)}, u32[]{:S(2)}) collective-permute-start(bf16[64,1024]{1,0:T(8,128)(2,1)S(1)} %get-tuple-element.67), channel_id=1, source_target_pairs={{0,1},{1,0},{2,3},{3,2},{4,5},{5,4},{6,7},{7,6},{8,9},{9,8},{10,11... | collective-permute-start | bytes 393224 | tf_op jit(solution)/shard_map/ppermute | solution.py:284
  5.9 4.7 %collective-permute-start.1 = (bf16[64,1024]{1,0:T(8,128)(2,1)S(1)}, bf16[64,1024]{1,0:T(8,128)(2,1)S(1)}, u32[]{:S(2)}, u32[]{:S(2)}) collective-permute-start(bf16[64,1024]{1,0:T(8,128)(2,1)S(1)} %get-tuple-element.68), channel_id=1, source_target_pairs={{0,1},{1,0},{2,3},{3,2},{4,5},{5,4},{6,7},{7,6},{8,9},{9,8},{10,11... | collective-permute-start | bytes 393224 | tf_op jit(solution)/shard_map/ppermute | solution.py:284
  6.4 6.6 %collective-permute-start.4 = (f32[16,1024]{1,0:T(8,128)S(1)}, f32[16,1024]{1,0:T(8,128)S(1)}, u32[]{:S(2)}, u32[]{:S(2)}) collective-permute-start(f32[16,1024]{1,0:T(8,128)S(1)} %get-tuple-element.36), channel_id=1, source_target_pairs={{0,1},{1,0},{2,3},{3,2},{4,5},{5,4},{6,7},{7,6},{8,9},{9,8},{10,11... | collective-permute-start | bytes 196616 | tf_op jit(solution)/shard_map/ppermute | solution.py:284
  6.8 8.9 %collective-permute-start.7 = (f32[16,1024]{1,0:T(8,128)S(1)}, f32[16,1024]{1,0:T(8,128)S(1)}, u32[]{:S(2)}, u32[]{:S(2)}) collective-permute-start(f32[16,1024]{1,0:T(8,128)S(1)} %get-tuple-element.39), channel_id=1, source_target_pairs={{1,2},{2,1},{3,4},{4,3},{5,6},{6,5},{9,10},{10,9},{11,12},{12,11},... | collective-permute-start | bytes 196616 | tf_op jit(solution)/shard_map/ppermute | solution.py:284
  8.8 24.1 %collective-permute-start.6 = (bf16[192,1024]{1,0:T(8,128)(2,1)S(1)}, bf16[192,1024]{1,0:T(8,128)(2,1)S(1)}, u32[]{:S(2)}, u32[]{:S(2)}) collective-permute-start(bf16[192,1024]{1,0:T(8,128)(2,1)S(1)} %get-tuple-element.34.refs_0_), channel_id=1, source_target_pairs={{4,0},{5,1},{6,4},{7,5},{2,6},{3,7},{0,2},{1,3},{12,8},{13,9},{14,... | collective-permute-start | bytes 1179656 | tf_op jit(solution)/shard_map/ppermute | solution.py:284
  13.0 31.4 %collective-permute-start.5 = (bf16[192,1024]{1,0:T(8,128)(2,1)S(1)}, bf16[192,1024]{1,0:T(8,128)(2,1)S(1)}, u32[]{:S(2)}, u32[]{:S(2)}) collective-permute-start(bf16[192,1024]{1,0:T(8,128)(2,1)S(1)} %collective-permute-done.block), channel_id=1, source_target_pairs={{0,4},{1,5},{4,6},{5,7},{6,2},{7,3},{2,0},{3,1},{8,12},{9,13},{12,... | collective-permute-start | bytes 1179656 | tf_op jit(solution)/shard_map/ppermute | solution.py:284
  15.7 4.6 %collective-permute-start.10 = (bf16[64,1024]{1,0:T(8,128)(2,1)S(1)}, bf16[64,1024]{1,0:T(8,128)(2,1)S(1)}, u32[]{:S(2)}, u32[]{:S(2)}) collective-permute-start(bf16[64,1024]{1,0:T(8,128)(2,1)S(1)} %get-tuple-element.63), channel_id=1, source_target_pairs={{0,1},{1,0},{2,3},{3,2},{4,5},{5,4},{6,7},{7,6},{8,9},{9,8},{10,11... | collective-permute-start | bytes 393224 | tf_op jit(solution)/shard_map/ppermute | solution.py:284
  18.8 1.6 %collective-permute-start.9 = (bf16[64,1024]{1,0:T(8,128)(2,1)S(1)}, bf16[64,1024]{1,0:T(8,128)(2,1)S(1)}, u32[]{:S(2)}, u32[]{:S(2)}) collective-permute-start(bf16[64,1024]{1,0:T(8,128)(2,1)S(1)} %get-tuple-element.64), channel_id=1, source_target_pairs={{0,1},{1,0},{2,3},{3,2},{4,5},{5,4},{6,7},{7,6},{8,9},{9,8},{10,11... | collective-permute-start | bytes 393224 | tf_op jit(solution)/shard_map/ppermute | solution.py:284
  18.9 1.5 %collective-permute-start.8 = (bf16[64,1024]{1,0:T(8,128)(2,1)S(1)}, bf16[64,1024]{1,0:T(8,128)(2,1)S(1)}, u32[]{:S(2)}, u32[]{:S(2)}) collective-permute-start(bf16[64,1024]{1,0:T(8,128)(2,1)S(1)} %get-tuple-element.65), channel_id=1, source_target_pairs={{0,1},{1,0},{2,3},{3,2},{4,5},{5,4},{6,7},{7,6},{8,9},{9,8},{10,11... | collective-permute-start | bytes 393224 | tf_op jit(solution)/shard_map/ppermute | solution.py:284
  44.4 1.8 %copy-start.3 = (bf16[1024,1024]{1,0:T(8,128)(2,1)S(1)}, bf16[1024,1024]{1,0:T(8,128)(2,1)}, u32[]{:S(2)}) copy-start(bf16[1024,1024]{1,0:T(8,128)(2,1)} %output_weight.1) | copy-start | bytes 6291460
  44.4 1.8 %copy-start.5 = (f32[31,1024]{1,0:T(8,128)S(1)}, f32[31,1024]{1,0:T(8,128)}, u32[]{:S(2)}) copy-start(f32[31,1024]{1,0:T(8,128)} %depthwise.1) | copy-start | bytes 380932
  44.4 1.8 %copy-start.7 = (f32[1024]{0:T(1024)S(1)}, f32[1024]{0:T(1024)}, u32[]{:S(2)}) copy-start(f32[1024]{0:T(1024)} %param.15) | copy-start | bytes 12292
  44.4 1.8 %copy-start.8 = (f32[1024]{0:T(1024)S(1)}, f32[1024]{0:T(1024)}, u32[]{:S(2)}) copy-start(f32[1024]{0:T(1024)} %param.17) | copy-start | bytes 12292
  44.4 1.8 %collective-permute-start.11 = (bf16[192,1024]{1,0:T(8,128)(2,1)S(1)}, bf16[192,1024]{1,0:T(8,128)(2,1)S(1)}, u32[]{:S(2)}, u32[]{:S(2)}) collective-permute-start(bf16[192,1024]{1,0:T(8,128)(2,1)S(1)} %collective-permute-done.5.block), channel_id=1, source_target_pairs={{0,1},{1,0},{2,3},{3,2},{4,5},{5,4},{6,7},{7,6},{8,9},{9,8},{10,11... | collective-permute-start | bytes 1179656 | tf_op jit(solution)/shard_map/ppermute | solution.py:284

commit v5 on v4

--- a/solution.py
+++ b/solution.py
@@ -83,7 +83,7 @@
     return totals, jnp.where(low_half, out[:rows, :LANES], out[rows:, :LANES])
 
 
-def attend(query, keys, values, old, new, context=None):
+def attend(query, keys, values, old, new, context=None, after=None):
     query_rows, width = query.shape
     pairs = width // LANES
     most = least = None
@@ -104,6 +104,8 @@
             new[3][:, span] = running
         most = totals if most is None else jnp.maximum(most, totals)
         least = totals if least is None else jnp.minimum(least, totals)
+    if after is not None:
+        after()
     fits = jnp.logical_and(jnp.max(most) < CEILING, jnp.min(least) > FLOOR)
     if old is not None:
         fits = jnp.logical_and(fits, jnp.max(old[0][...]) == 0.0)
@@ -138,6 +140,9 @@
                 new[2][:, span] = totals
                 new[3][:, span] = running
 
+        if after is not None:
+            after()
+
 
 def scaled_query(rows, query_weight, span, width):
     scale = jnp.asarray((width // HEADS) ** (-0.5), bf16)
@@ -205,15 +210,21 @@
     del keys_in, values_in
     rows, width = frames.shape
     project(sibling, key_weight, value_weight, keys, values, rows)
-    attend(query, keys, values, (shifted, highest, totals, running), None, context)
     is_high = place[:1, :1] > 0
-    attended[:HALO, :] = jnp.where(is_high, inner[...], outer[...])
-    attended[HALO : HALO + rows, :] = frames[...]
-    attended[HALO + rows :, :] = jnp.where(is_high, outer[...], inner[...])
-    for low in range(0, width, SPAN):
-        span = slice(low, low + SPAN)
-        attended[:, span] += jnp.dot(context[...], output_weight[:, span], preferred_element_type=f32)
-    mixer_in[...] = norm_rows(attended[...], gain[...])
+
+    def add_attention():
+        for low in range(0, width, SPAN):
+            span = slice(low, low + SPAN)
+            near, far = inner[:, span], outer[:, span]
+            left, right = jnp.where(is_high, near, far), jnp.where(is_high, far, near)
+            attended[:, span] = jnp.concatenate([left, frames[:, span], right], axis=0) + jnp.dot(
+                context[...], output_weight[:, span], preferred_element_type=f32
+            )
+
+    attend(query, keys, values, (shifted, highest, totals, running), None, context, add_attention)
+    for top in range(0, query.shape[0], 32):
+        part = slice(top, top + 32)
+        mixer_in[part, :] = norm_rows(attended[part, :], gain[...])
 
     mixer_in[:HALO, :] = jnp.where(place[1:2, :1] > 0, mixer_in[:HALO, :], 0.0)
     mixer_in[HALO + rows :, :] = jnp.where(place[2:3, :1] > 0, mixer_in[HALO + rows :, :], 0.0)

time: 59 us -> 59.4 us (level)
  no operation moved by 1% of the time
where the time goes in v5:
time: 59.4 us; the launch traced here: 59.1 us
  Pallas kernels  38.9 us (65%)
  starting transfers between devices  15.2 us (26%)
  blocking collectives  2.37 us (4%)
  local copies, waits for them, and re-layouts  1.3 us (2%)
  waiting for transfers between devices  0.83 us (1%)
    ppermute x12, starting transfers between devices, send(): return lax.ppermute(value, 'ctx', pairs)  15.2 us
    pallas_call x1, Pallas kernels, per_device(): call(last_kernel, [jax.ShapeDtypeStruct((rows, width), f32)] + tall(2), [...  12.7 us
    pallas_call x1, Pallas kernels, per_device(): call(functools.partial(first_kernel, start=3 * rows), [jax.ShapeDtypeStru...  12.5 us
    pallas_call x1, Pallas kernels, per_device(): call(block_kernel, list(state), [VMEM] * 8, projected, flops=BLOCK)  9.08 us
    all_gather x1, blocking collectives, per_device(): lax.all_gather(block, 'ctx', axis=0, tiled=True, axis_index_groups=siblings)  2.37 us
    pallas_call x1, Pallas kernels, per_device(): call(own_kernel, [jax.ShapeDtypeStruct((rows, width), bf16)] + tall(4), [...  2.28 us
  transfers between devices with their start and end apart: 12, of which 2 were waited for; matrix products, arithmetic and copies ran while one was open for 0% of the time, Pallas kernels for 44%

profile of v5, /device:TPU:1, one launch (start us, length us, event | category | flops | bytes accessed | tf_op | source)
XLA Modules:
  0.0 59.1 jit_solution(6854676034835726471)
XLA Ops:
  0.0 0.1 add_convert_fusion
  0.2 1.1 %copy-done.4 = f32[192,1024]{1,0:T(8,128)S(1)} copy-done((f32[192,1024]{1,0:T(8,128)S(1)}, f32[192,1024]{1,0:T(8,128)}, u32[]{:S(2)}) %copy-start.4) | copy-done | bytes 786456
  1.3 0.3 shard_map.92
  1.6 3.2 %collective-permute-start = (bf16[192,1024]{1,0:T(8,128)(2,1)S(1)}, bf16[192,1024]{1,0:T(8,128)(2,1)S(1)}, u32[]{:S(2)}, u32[]{:S(2)}) collective-permute-start(bf16[192,1024]{1,0:T(8,128)(2,1)S(1)} %get-tuple-element.34.refs_0_), channel_id=1, source_target_pairs={{0,4},{1,5},{4,6},{5,7},{6,2},{7,3},{2,0},{3,1},{8,12},{9,13},{12,... | collective-permute-start | bytes 1179656 | tf_op jit(solution)/shard_map/ppermute | solution.py:295
  4.8 1.0 %collective-permute-start.3 = (bf16[64,1024]{1,0:T(8,128)(2,1)S(1)}, bf16[64,1024]{1,0:T(8,128)(2,1)S(1)}, u32[]{:S(2)}, u32[]{:S(2)}) collective-permute-start(bf16[64,1024]{1,0:T(8,128)(2,1)S(1)} %get-tuple-element.66), channel_id=1, source_target_pairs={{0,1},{1,0},{2,3},{3,2},{4,5},{5,4},{6,7},{7,6},{8,9},{9,8},{10,11... | collective-permute-start | bytes 393224 | tf_op jit(solution)/shard_map/ppermute | solution.py:295
  5.8 0.1 collective-permute-start.2
  5.9 0.4 collective-permute-start.1
  6.4 0.1 collective-permute-start.4
  6.4 0.4 collective-permute-done.3.refs_6_
  6.8 1.9 %collective-permute-start.7 = (f32[16,1024]{1,0:T(8,128)S(1)}, f32[16,1024]{1,0:T(8,128)S(1)}, u32[]{:S(2)}, u32[]{:S(2)}) collective-permute-start(f32[16,1024]{1,0:T(8,128)S(1)} %get-tuple-element.39), channel_id=1, source_target_pairs={{1,2},{2,1},{3,4},{4,3},{5,6},{6,5},{9,10},{10,9},{11,12},{12,11},... | collective-permute-start | bytes 196616 | tf_op jit(solution)/shard_map/ppermute | solution.py:295
  8.8 1.9 %collective-permute-start.6 = (bf16[192,1024]{1,0:T(8,128)(2,1)S(1)}, bf16[192,1024]{1,0:T(8,128)(2,1)S(1)}, u32[]{:S(2)}, u32[]{:S(2)}) collective-permute-start(bf16[192,1024]{1,0:T(8,128)(2,1)S(1)} %get-tuple-element.34.refs_0_), channel_id=1, source_target_pairs={{4,0},{5,1},{6,4},{7,5},{2,6},{3,7},{0,2},{1,3},{12,8},{13,9},{14,... | collective-permute-start | bytes 1179656 | tf_op jit(solution)/shard_map/ppermute | solution.py:295
  10.6 2.3 %shard_map.93 = (bf16[192,1024]{1,0:T(8,128)(2,1)S(1)}, bf16[768,1024]{1,0:T(8,128)(2,1)S(1)}, bf16[768,1024]{1,0:T(8,128)(2,1)S(1)}) custom-call(bf16[192,1024]{1,0:T(8,128)(2,1)S(1)} %get-tuple-element.34.refs_0_, bf16[1024,1024]{1,0:T(8,128)(2,1)S(1)} %copy-done.2, bf16[1024,1024]{1,0:T(8,128)(2,1)S(1)} %copy-done, bf16[1024,1024]{1,0:T(8,128)(2,1)S(1)} %copy-done.1, ...), custom_call_target="tpu_custom_call" | custom-call | flops 1024 | bytes 1024 | tf_op jit(solution)/shard_map/pallas_call | solution.py:316
  13.0 2.8 %collective-permute-start.5 = (bf16[192,1024]{1,0:T(8,128)(2,1)S(1)}, bf16[192,1024]{1,0:T(8,128)(2,1)S(1)}, u32[]{:S(2)}, u32[]{:S(2)}) collective-permute-start(bf16[192,1024]{1,0:T(8,128)(2,1)S(1)} %collective-permute-done.block), channel_id=1, source_target_pairs={{0,4},{1,5},{4,6},{5,7},{6,2},{7,3},{2,0},{3,1},{8,12},{9,13},{12,... | collective-permute-start | bytes 1179656 | tf_op jit(solution)/shard_map/ppermute | solution.py:295
  15.7 3.0 %collective-permute-start.10 = (bf16[64,1024]{1,0:T(8,128)(2,1)S(1)}, bf16[64,1024]{1,0:T(8,128)(2,1)S(1)}, u32[]{:S(2)}, u32[]{:S(2)}) collective-permute-start(bf16[64,1024]{1,0:T(8,128)(2,1)S(1)} %get-tuple-element.63), channel_id=1, source_target_pairs={{0,1},{1,0},{2,3},{3,2},{4,5},{5,4},{6,7},{7,6},{8,9},{9,8},{10,11... | collective-permute-start | bytes 393224 | tf_op jit(solution)/shard_map/ppermute | solution.py:295
  18.8 0.1 collective-permute-start.9
  18.9 0.4 collective-permute-start.8
  19.3 1.0 %shard_map.94 = (bf16[768,1024]{1,0:T(8,128)(2,1)S(1)}, bf16[768,1024]{1,0:T(8,128)(2,1)S(1)}) custom-call(bf16[192,1024]{1,0:T(8,128)(2,1)S(1)} %collective-permute-done.block, bf16[1024,1024]{1,0:T(8,128)(2,1)S(1)} %copy-done, bf16[1024,1024]{1,0:T(8,128)(2,1)S(1)} %copy-done.1, ...), custom_call_target="tpu_custom_call", output_to_operand_aliasing={{0}: (3, {}), {1}: (4, {})} | custom-call | flops 1024 | bytes 1024 | tf_op jit(solution)/shard_map/pallas_call | solution.py:330
  20.4 12.5 %shard_map.95 = (bf16[224,1024]{1,0:T(8,128)(2,1)S(1)}, f32[8,128]{1,0:T(8,128)S(1)}, f32[224,1024]{1,0:T(8,128)S(1)}, f32[224,1024]{1,0:T(8,128)S(1)}, f32[224,...) custom-call(f32[3,128]{1,0:T(4,128)S(1)} %shard_map.91.place.refs_0_, ...), custom_call_target="tpu_custom_call", output_to_operand_aliasing={{5}: (8, {}), {6}: (9, {})} | custom-call | flops 1024 | bytes 1024 | tf_op jit(solution)/shard_map/pallas_call | solution.py:333
  32.9 2.4 %all_gather.3.block = bf16[384,1024]{1,0:T(8,128)(2,1)S(1)} all-gather(bf16[192,1024]{1,0:T(8,128)(2,1)S(1)} %collective-permute-done.6), channel_id=1, replica_groups={{0,1},{2,3},{4,5},{6,7},{8,9},{10,11},{12,13},{14,15},{16,17},{18,19},{..., dimensions={0}, use_global_device_ids=true | all-gather | bytes 1179648 | tf_op jit(solution)/shard_map/all_gather | solution.py:352
  35.3 9.1 %shard_map.96 = (f32[8,128]{1,0:T(8,128)S(1)}, f32[224,1024]{1,0:T(8,128)S(1)}, f32[224,1024]{1,0:T(8,128)S(1)}, f32[224,1024]{1,0:T(8,128)S(1)}) custom-call(bf16[384,1024]{1,0:T(8,128)(2,1)S(1)} %all_gather.3.block, bf16[224,1024]{1,0:T(8,128)(2,1)S(1)} %get-tuple-element.49.query, bf16[1024,1024]{1,0:T(8,128)(2,1)S(1)} %copy-done, ...), custom_call_target="tpu_custom_call" | custom-call | flops 1024 | bytes 1024 | tf_op jit(solution)/shard_map/pallas_call | solution.py:354
  44.4 0.3 collective-permute-start.11
  44.7 1.0 %shard_map.97 = (bf16[384,1024]{1,0:T(8,128)(2,1)S(1)}, bf16[384,1024]{1,0:T(8,128)(2,1)S(1)}) custom-call(bf16[192,1024]{1,0:T(8,128)(2,1)S(1)} %collective-permute-done.5.block, bf16[1024,1024]{1,0:T(8,128)(2,1)S(1)} %copy-done, bf16[1024,1024]{1,0:T(8,128)(2,1)S(1)} %copy-done.1), custom_call_target="tpu_custom_call" | custom-call | flops 1024 | bytes 1024 | tf_op jit(solution)/shard_map/pallas_call | solution.py:360
  45.8 0.4 collective-permute-done.11.sibling
  46.2 12.7 %shard_map.98 = (f32[192,1024]{1,0:T(8,128)}, bf16[384,1024]{1,0:T(8,128)(2,1)S(1)}, bf16[384,1024]{1,0:T(8,128)(2,1)S(1)}) custom-call(f32[3,128]{1,0:T(4,128)S(1)} %shard_map.91.place.refs_0_, bf16[192,1024]{1,0:T(8,128)(2,1)S(1)} %collective-permute-done.11.sibling, ...), custom_call_target="tpu_custom_call", output_to_operand_aliasing={{1}: (2, {}), {2}: (3, {})} | custom-call | flops 1024 | bytes 1024 | tf_op jit(solution)/shard_map/pallas_call | solution.py:361
  (31 shorter events, 0.2 us)
Async XLA Ops:
  0.2 1.1 %copy-start.4 = (f32[192,1024]{1,0:T(8,128)S(1)}, f32[192,1024]{1,0:T(8,128)}, u32[]{:S(2)}) copy-start(f32[192,1024]{1,0:T(8,128)} %frames.3) | copy-start | bytes 2359300
  0.2 1.1 %copy-start.6 = (f32[1024]{0:T(1024)S(1)}, f32[1024]{0:T(1024)}, u32[]{:S(2)}) copy-start(f32[1024]{0:T(1024)} %param.10) | copy-start | bytes 12292
  1.3 9.3 %copy-start = (bf16[1024,1024]{1,0:T(8,128)(2,1)S(1)}, bf16[1024,1024]{1,0:T(8,128)(2,1)}, u32[]{:S(2)}) copy-start(bf16[1024,1024]{1,0:T(8,128)(2,1)} %key_weight.7) | copy-start | bytes 6291460
  1.3 9.3 %copy-start.1 = (bf16[1024,1024]{1,0:T(8,128)(2,1)S(1)}, bf16[1024,1024]{1,0:T(8,128)(2,1)}, u32[]{:S(2)}) copy-start(bf16[1024,1024]{1,0:T(8,128)(2,1)} %value_weight.7) | copy-start | bytes 6291460
  1.3 9.3 %copy-start.2 = (bf16[1024,1024]{1,0:T(8,128)(2,1)S(1)}, bf16[1024,1024]{1,0:T(8,128)(2,1)}, u32[]{:S(2)}) copy-start(bf16[1024,1024]{1,0:T(8,128)(2,1)} %refs_5_.1) | copy-start | bytes 6291460
  1.6 11.3 %collective-permute-start = (bf16[192,1024]{1,0:T(8,128)(2,1)S(1)}, bf16[192,1024]{1,0:T(8,128)(2,1)S(1)}, u32[]{:S(2)}, u32[]{:S(2)}) collective-permute-start(bf16[192,1024]{1,0:T(8,128)(2,1)S(1)} %get-tuple-element.34.refs_0_), channel_id=1, source_target_pairs={{0,4},{1,5},{4,6},{5,7},{6,2},{7,3},{2,0},{3,1},{8,12},{9,13},{12,... | collective-permute-start | bytes 1179656 | tf_op jit(solution)/shard_map/ppermute | solution.py:295
  4.8 2.0 %collective-permute-start.3 = (bf16[64,1024]{1,0:T(8,128)(2,1)S(1)}, bf16[64,1024]{1,0:T(8,128)(2,1)S(1)}, u32[]{:S(2)}, u32[]{:S(2)}) collective-permute-start(bf16[64,1024]{1,0:T(8,128)(2,1)S(1)} %get-tuple-element.66), channel_id=1, source_target_pairs={{0,1},{1,0},{2,3},{3,2},{4,5},{5,4},{6,7},{7,6},{8,9},{9,8},{10,11... | collective-permute-start | bytes 393224 | tf_op jit(solution)/shard_map/ppermute | solution.py:295
  5.8 2.9 %collective-permute-start.2 = (bf16[64,1024]{1,0:T(8,128)(2,1)S(1)}, bf16[64,1024]{1,0:T(8,128)(2,1)S(1)}, u32[]{:S(2)}, u32[]{:S(2)}) collective-permute-start(bf16[64,1024]{1,0:T(8,128)(2,1)S(1)} %get-tuple-element.67), channel_id=1, source_target_pairs={{0,1},{1,0},{2,3},{3,2},{4,5},{5,4},{6,7},{7,6},{8,9},{9,8},{10,11... | collective-permute-start | bytes 393224 | tf_op jit(solution)/shard_map/ppermute | solution.py:295
  5.9 4.7 %collective-permute-start.1 = (bf16[64,1024]{1,0:T(8,128)(2,1)S(1)}, bf16[64,1024]{1,0:T(8,128)(2,1)S(1)}, u32[]{:S(2)}, u32[]{:S(2)}) collective-permute-start(bf16[64,1024]{1,0:T(8,128)(2,1)S(1)} %get-tuple-element.68), channel_id=1, source_target_pairs={{0,1},{1,0},{2,3},{3,2},{4,5},{5,4},{6,7},{7,6},{8,9},{9,8},{10,11... | collective-permute-start | bytes 393224 | tf_op jit(solution)/shard_map/ppermute | solution.py:295
  6.4 6.6 %collective-permute-start.4 = (f32[16,1024]{1,0:T(8,128)S(1)}, f32[16,1024]{1,0:T(8,128)S(1)}, u32[]{:S(2)}, u32[]{:S(2)}) collective-permute-start(f32[16,1024]{1,0:T(8,128)S(1)} %get-tuple-element.36), channel_id=1, source_target_pairs={{0,1},{1,0},{2,3},{3,2},{4,5},{5,4},{6,7},{7,6},{8,9},{9,8},{10,11... | collective-permute-start | bytes 196616 | tf_op jit(solution)/shard_map/ppermute | solution.py:295
  6.8 8.9 %collective-permute-start.7 = (f32[16,1024]{1,0:T(8,128)S(1)}, f32[16,1024]{1,0:T(8,128)S(1)}, u32[]{:S(2)}, u32[]{:S(2)}) collective-permute-start(f32[16,1024]{1,0:T(8,128)S(1)} %get-tuple-element.39), channel_id=1, source_target_pairs={{1,2},{2,1},{3,4},{4,3},{5,6},{6,5},{9,10},{10,9},{11,12},{12,11},... | collective-permute-start | bytes 196616 | tf_op jit(solution)/shard_map/ppermute | solution.py:295
  8.8 24.1 %collective-permute-start.6 = (bf16[192,1024]{1,0:T(8,128)(2,1)S(1)}, bf16[192,1024]{1,0:T(8,128)(2,1)S(1)}, u32[]{:S(2)}, u32[]{:S(2)}) collective-permute-start(bf16[192,1024]{1,0:T(8,128)(2,1)S(1)} %get-tuple-element.34.refs_0_), channel_id=1, source_target_pairs={{4,0},{5,1},{6,4},{7,5},{2,6},{3,7},{0,2},{1,3},{12,8},{13,9},{14,... | collective-permute-start | bytes 1179656 | tf_op jit(solution)/shard_map/ppermute | solution.py:295
  13.0 31.4 %collective-permute-start.5 = (bf16[192,1024]{1,0:T(8,128)(2,1)S(1)}, bf16[192,1024]{1,0:T(8,128)(2,1)S(1)}, u32[]{:S(2)}, u32[]{:S(2)}) collective-permute-start(bf16[192,1024]{1,0:T(8,128)(2,1)S(1)} %collective-permute-done.block), channel_id=1, source_target_pairs={{0,4},{1,5},{4,6},{5,7},{6,2},{7,3},{2,0},{3,1},{8,12},{9,13},{12,... | collective-permute-start | bytes 1179656 | tf_op jit(solution)/shard_map/ppermute | solution.py:295
  15.7 4.6 %collective-permute-start.10 = (bf16[64,1024]{1,0:T(8,128)(2,1)S(1)}, bf16[64,1024]{1,0:T(8,128)(2,1)S(1)}, u32[]{:S(2)}, u32[]{:S(2)}) collective-permute-start(bf16[64,1024]{1,0:T(8,128)(2,1)S(1)} %get-tuple-element.63), channel_id=1, source_target_pairs={{0,1},{1,0},{2,3},{3,2},{4,5},{5,4},{6,7},{7,6},{8,9},{9,8},{10,11... | collective-permute-start | bytes 393224 | tf_op jit(solution)/shard_map/ppermute | solution.py:295
  18.8 1.6 %collective-permute-start.9 = (bf16[64,1024]{1,0:T(8,128)(2,1)S(1)}, bf16[64,1024]{1,0:T(8,128)(2,1)S(1)}, u32[]{:S(2)}, u32[]{:S(2)}) collective-permute-start(bf16[64,1024]{1,0:T(8,128)(2,1)S(1)} %get-tuple-element.64), channel_id=1, source_target_pairs={{0,1},{1,0},{2,3},{3,2},{4,5},{5,4},{6,7},{7,6},{8,9},{9,8},{10,11... | collective-permute-start | bytes 393224 | tf_op jit(solution)/shard_map/ppermute | solution.py:295
  18.9 1.5 %collective-permute-start.8 = (bf16[64,1024]{1,0:T(8,128)(2,1)S(1)}, bf16[64,1024]{1,0:T(8,128)(2,1)S(1)}, u32[]{:S(2)}, u32[]{:S(2)}) collective-permute-start(bf16[64,1024]{1,0:T(8,128)(2,1)S(1)} %get-tuple-element.65), channel_id=1, source_target_pairs={{0,1},{1,0},{2,3},{3,2},{4,5},{5,4},{6,7},{7,6},{8,9},{9,8},{10,11... | collective-permute-start | bytes 393224 | tf_op jit(solution)/shard_map/ppermute | solution.py:295
  44.4 1.8 %copy-start.3 = (bf16[1024,1024]{1,0:T(8,128)(2,1)S(1)}, bf16[1024,1024]{1,0:T(8,128)(2,1)}, u32[]{:S(2)}) copy-start(bf16[1024,1024]{1,0:T(8,128)(2,1)} %output_weight.1) | copy-start | bytes 6291460
  44.4 1.8 %copy-start.5 = (f32[31,1024]{1,0:T(8,128)S(1)}, f32[31,1024]{1,0:T(8,128)}, u32[]{:S(2)}) copy-start(f32[31,1024]{1,0:T(8,128)} %depthwise.1) | copy-start | bytes 380932
  44.4 1.8 %copy-start.7 = (f32[1024]{0:T(1024)S(1)}, f32[1024]{0:T(1024)}, u32[]{:S(2)}) copy-start(f32[1024]{0:T(1024)} %param.15) | copy-start | bytes 12292
  44.4 1.8 %copy-start.8 = (f32[1024]{0:T(1024)S(1)}, f32[1024]{0:T(1024)}, u32[]{:S(2)}) copy-start(f32[1024]{0:T(1024)} %param.17) | copy-start | bytes 12292
  44.4 1.8 %collective-permute-start.11 = (bf16[192,1024]{1,0:T(8,128)(2,1)S(1)}, bf16[192,1024]{1,0:T(8,128)(2,1)S(1)}, u32[]{:S(2)}, u32[]{:S(2)}) collective-permute-start(bf16[192,1024]{1,0:T(8,128)(2,1)S(1)} %collective-permute-done.5.block), channel_id=1, source_target_pairs={{0,1},{1,0},{2,3},{3,2},{4,5},{5,4},{6,7},{7,6},{8,9},{9,8},{10,11... | collective-permute-start | bytes 1179656 | tf_op jit(solution)/shard_map/ppermute | solution.py:295

commit v6 on v5

--- a/solution.py
+++ b/solution.py
@@ -87,11 +87,12 @@
     query_rows, width = query.shape
     pairs = width // LANES
     most = least = None
-    scores = pair_scores(query, keys, slice(0, LANES))
+    ahead = context is not None
+    scores = pair_scores(query, keys, slice(0, LANES)) if ahead else None
     for pair in range(pairs):
         span = slice(pair * LANES, (pair + 1) * LANES)
-        now = scores
-        if pair + 1 < pairs:
+        now = scores if ahead else pair_scores(query, keys, span)
+        if ahead and pair + 1 < pairs:
             scores = pair_scores(query, keys, slice((pair + 1) * LANES, (pair + 2) * LANES))
         totals, running = pair_sums(jnp.exp(now), values, span)
         if old is not None:

time: 59.4 us -> 59.4 us (level)
  no operation moved by 1% of the time
where the time goes in v6:
time: 59.4 us; the launch traced here: 59 us
  Pallas kernels  38.7 us (65%)
  starting transfers between devices  15.2 us (26%)
  blocking collectives  2.55 us (4%)
  local copies, waits for them, and re-layouts  1.3 us (2%)
  waiting for transfers between devices  0.83 us (1%)
    ppermute x12, starting transfers between devices, send(): return lax.ppermute(value, 'ctx', pairs)  15.2 us
    pallas_call x1, Pallas kernels, per_device(): call(last_kernel, [jax.ShapeDtypeStruct((rows, width), f32)] + tall(2), [...  12.7 us
    pallas_call x1, Pallas kernels, per_device(): call(functools.partial(first_kernel, start=3 * rows), [jax.ShapeDtypeStru...  12.5 us
    pallas_call x1, Pallas kernels, per_device(): call(block_kernel, list(state), [VMEM] * 8, projected, flops=BLOCK)  8.9 us
    all_gather x1, blocking collectives, per_device(): lax.all_gather(block, 'ctx', axis=0, tiled=True, axis_index_groups=siblings)  2.55 us
    pallas_call x1, Pallas kernels, per_device(): call(own_kernel, [jax.ShapeDtypeStruct((rows, width), bf16)] + tall(4), [...  2.28 us
  transfers between devices with their start and end apart: 12, of which 2 were waited for; matrix products, arithmetic and copies ran while one was open for 0% of the time, Pallas kernels for 44%

profile of v6, /device:TPU:1, one launch (start us, length us, event | category | flops | bytes accessed | tf_op | source)
XLA Modules:
  0.0 59.0 jit_solution(7968019113361316688)
XLA Ops:
  0.0 0.1 add_convert_fusion
  0.2 1.1 %copy-done.4 = f32[192,1024]{1,0:T(8,128)S(1)} copy-done((f32[192,1024]{1,0:T(8,128)S(1)}, f32[192,1024]{1,0:T(8,128)}, u32[]{:S(2)}) %copy-start.4) | copy-done | bytes 786456
  1.3 0.3 shard_map.92
  1.6 3.2 %collective-permute-start = (bf16[192,1024]{1,0:T(8,128)(2,1)S(1)}, bf16[192,1024]{1,0:T(8,128)(2,1)S(1)}, u32[]{:S(2)}, u32[]{:S(2)}) collective-permute-start(bf16[192,1024]{1,0:T(8,128)(2,1)S(1)} %get-tuple-element.34.refs_0_), channel_id=1, source_target_pairs={{0,4},{1,5},{4,6},{5,7},{6,2},{7,3},{2,0},{3,1},{8,12},{9,13},{12,... | collective-permute-start | bytes 1179656 | tf_op jit(solution)/shard_map/ppermute | solution.py:296
  4.8 1.0 %collective-permute-start.3 = (bf16[64,1024]{1,0:T(8,128)(2,1)S(1)}, bf16[64,1024]{1,0:T(8,128)(2,1)S(1)}, u32[]{:S(2)}, u32[]{:S(2)}) collective-permute-start(bf16[64,1024]{1,0:T(8,128)(2,1)S(1)} %get-tuple-element.66), channel_id=1, source_target_pairs={{0,1},{1,0},{2,3},{3,2},{4,5},{5,4},{6,7},{7,6},{8,9},{9,8},{10,11... | collective-permute-start | bytes 393224 | tf_op jit(solution)/shard_map/ppermute | solution.py:296
  5.8 0.1 collective-permute-start.2
  5.9 0.4 collective-permute-start.1
  6.4 0.1 collective-permute-start.4
  6.4 0.4 collective-permute-done.3.refs_6_
  6.8 1.9 %collective-permute-start.7 = (f32[16,1024]{1,0:T(8,128)S(1)}, f32[16,1024]{1,0:T(8,128)S(1)}, u32[]{:S(2)}, u32[]{:S(2)}) collective-permute-start(f32[16,1024]{1,0:T(8,128)S(1)} %get-tuple-element.39), channel_id=1, source_target_pairs={{1,2},{2,1},{3,4},{4,3},{5,6},{6,5},{9,10},{10,9},{11,12},{12,11},... | collective-permute-start | bytes 196616 | tf_op jit(solution)/shard_map/ppermute | solution.py:296
  8.8 1.9 %collective-permute-start.6 = (bf16[192,1024]{1,0:T(8,128)(2,1)S(1)}, bf16[192,1024]{1,0:T(8,128)(2,1)S(1)}, u32[]{:S(2)}, u32[]{:S(2)}) collective-permute-start(bf16[192,1024]{1,0:T(8,128)(2,1)S(1)} %get-tuple-element.34.refs_0_), channel_id=1, source_target_pairs={{4,0},{5,1},{6,4},{7,5},{2,6},{3,7},{0,2},{1,3},{12,8},{13,9},{14,... | collective-permute-start | bytes 1179656 | tf_op jit(solution)/shard_map/ppermute | solution.py:296
  10.6 2.3 %shard_map.93 = (bf16[192,1024]{1,0:T(8,128)(2,1)S(1)}, bf16[768,1024]{1,0:T(8,128)(2,1)S(1)}, bf16[768,1024]{1,0:T(8,128)(2,1)S(1)}) custom-call(bf16[192,1024]{1,0:T(8,128)(2,1)S(1)} %get-tuple-element.34.refs_0_, bf16[1024,1024]{1,0:T(8,128)(2,1)S(1)} %copy-done.2, bf16[1024,1024]{1,0:T(8,128)(2,1)S(1)} %copy-done, bf16[1024,1024]{1,0:T(8,128)(2,1)S(1)} %copy-done.1, ...), custom_call_target="tpu_custom_call" | custom-call | flops 1024 | bytes 1024 | tf_op jit(solution)/shard_map/pallas_call | solution.py:317
  13.0 2.8 %collective-permute-start.5 = (bf16[192,1024]{1,0:T(8,128)(2,1)S(1)}, bf16[192,1024]{1,0:T(8,128)(2,1)S(1)}, u32[]{:S(2)}, u32[]{:S(2)}) collective-permute-start(bf16[192,1024]{1,0:T(8,128)(2,1)S(1)} %collective-permute-done.block), channel_id=1, source_target_pairs={{0,4},{1,5},{4,6},{5,7},{6,2},{7,3},{2,0},{3,1},{8,12},{9,13},{12,... | collective-permute-start | bytes 1179656 | tf_op jit(solution)/shard_map/ppermute | solution.py:296
  15.7 3.0 %collective-permute-start.10 = (bf16[64,1024]{1,0:T(8,128)(2,1)S(1)}, bf16[64,1024]{1,0:T(8,128)(2,1)S(1)}, u32[]{:S(2)}, u32[]{:S(2)}) collective-permute-start(bf16[64,1024]{1,0:T(8,128)(2,1)S(1)} %get-tuple-element.63), channel_id=1, source_target_pairs={{0,1},{1,0},{2,3},{3,2},{4,5},{5,4},{6,7},{7,6},{8,9},{9,8},{10,11... | collective-permute-start | bytes 393224 | tf_op jit(solution)/shard_map/ppermute | solution.py:296
  18.8 0.1 collective-permute-start.9
  18.9 0.4 collective-permute-start.8
  19.3 1.0 %shard_map.94 = (bf16[768,1024]{1,0:T(8,128)(2,1)S(1)}, bf16[768,1024]{1,0:T(8,128)(2,1)S(1)}) custom-call(bf16[192,1024]{1,0:T(8,128)(2,1)S(1)} %collective-permute-done.block, bf16[1024,1024]{1,0:T(8,128)(2,1)S(1)} %copy-done, bf16[1024,1024]{1,0:T(8,128)(2,1)S(1)} %copy-done.1, ...), custom_call_target="tpu_custom_call", output_to_operand_aliasing={{0}: (3, {}), {1}: (4, {})} | custom-call | flops 1024 | bytes 1024 | tf_op jit(solution)/shard_map/pallas_call | solution.py:331
  20.4 12.5 %shard_map.95 = (bf16[224,1024]{1,0:T(8,128)(2,1)S(1)}, f32[8,128]{1,0:T(8,128)S(1)}, f32[224,1024]{1,0:T(8,128)S(1)}, f32[224,1024]{1,0:T(8,128)S(1)}, f32[224,...) custom-call(f32[3,128]{1,0:T(4,128)S(1)} %shard_map.91.place.refs_0_, ...), custom_call_target="tpu_custom_call", output_to_operand_aliasing={{5}: (8, {}), {6}: (9, {})} | custom-call | flops 1024 | bytes 1024 | tf_op jit(solution)/shard_map/pallas_call | solution.py:334
  32.8 2.5 %all_gather.3.block = bf16[384,1024]{1,0:T(8,128)(2,1)S(1)} all-gather(bf16[192,1024]{1,0:T(8,128)(2,1)S(1)} %collective-permute-done.6), channel_id=1, replica_groups={{0,1},{2,3},{4,5},{6,7},{8,9},{10,11},{12,13},{14,15},{16,17},{18,19},{..., dimensions={0}, use_global_device_ids=true | all-gather | bytes 1179648 | tf_op jit(solution)/shard_map/all_gather | solution.py:353
  35.4 8.9 %shard_map.96 = (f32[8,128]{1,0:T(8,128)S(1)}, f32[224,1024]{1,0:T(8,128)S(1)}, f32[224,1024]{1,0:T(8,128)S(1)}, f32[224,1024]{1,0:T(8,128)S(1)}) custom-call(bf16[384,1024]{1,0:T(8,128)(2,1)S(1)} %all_gather.3.block, bf16[224,1024]{1,0:T(8,128)(2,1)S(1)} %get-tuple-element.49.query, bf16[1024,1024]{1,0:T(8,128)(2,1)S(1)} %copy-done, ...), custom_call_target="tpu_custom_call" | custom-call | flops 1024 | bytes 1024 | tf_op jit(solution)/shard_map/pallas_call | solution.py:355
  44.4 0.3 collective-permute-start.11
  44.7 1.0 %shard_map.97 = (bf16[384,1024]{1,0:T(8,128)(2,1)S(1)}, bf16[384,1024]{1,0:T(8,128)(2,1)S(1)}) custom-call(bf16[192,1024]{1,0:T(8,128)(2,1)S(1)} %collective-permute-done.5.block, bf16[1024,1024]{1,0:T(8,128)(2,1)S(1)} %copy-done, bf16[1024,1024]{1,0:T(8,128)(2,1)S(1)} %copy-done.1), custom_call_target="tpu_custom_call" | custom-call | flops 1024 | bytes 1024 | tf_op jit(solution)/shard_map/pallas_call | solution.py:361
  45.7 0.4 collective-permute-done.11.sibling
  46.2 12.7 %shard_map.98 = (f32[192,1024]{1,0:T(8,128)}, bf16[384,1024]{1,0:T(8,128)(2,1)S(1)}, bf16[384,1024]{1,0:T(8,128)(2,1)S(1)}) custom-call(f32[3,128]{1,0:T(4,128)S(1)} %shard_map.91.place.refs_0_, bf16[192,1024]{1,0:T(8,128)(2,1)S(1)} %collective-permute-done.11.sibling, ...), custom_call_target="tpu_custom_call", output_to_operand_aliasing={{1}: (2, {}), {2}: (3, {})} | custom-call | flops 1024 | bytes 1024 | tf_op jit(solution)/shard_map/pallas_call | solution.py:362
  (31 shorter events, 0.2 us)
Async XLA Ops:
  0.2 1.1 %copy-start.4 = (f32[192,1024]{1,0:T(8,128)S(1)}, f32[192,1024]{1,0:T(8,128)}, u32[]{:S(2)}) copy-start(f32[192,1024]{1,0:T(8,128)} %frames.3) | copy-start | bytes 2359300
  0.2 1.1 %copy-start.6 = (f32[1024]{0:T(1024)S(1)}, f32[1024]{0:T(1024)}, u32[]{:S(2)}) copy-start(f32[1024]{0:T(1024)} %param.10) | copy-start | bytes 12292
  1.3 9.3 %copy-start = (bf16[1024,1024]{1,0:T(8,128)(2,1)S(1)}, bf16[1024,1024]{1,0:T(8,128)(2,1)}, u32[]{:S(2)}) copy-start(bf16[1024,1024]{1,0:T(8,128)(2,1)} %key_weight.7) | copy-start | bytes 6291460
  1.3 9.3 %copy-start.1 = (bf16[1024,1024]{1,0:T(8,128)(2,1)S(1)}, bf16[1024,1024]{1,0:T(8,128)(2,1)}, u32[]{:S(2)}) copy-start(bf16[1024,1024]{1,0:T(8,128)(2,1)} %value_weight.7) | copy-start | bytes 6291460
  1.3 9.3 %copy-start.2 = (bf16[1024,1024]{1,0:T(8,128)(2,1)S(1)}, bf16[1024,1024]{1,0:T(8,128)(2,1)}, u32[]{:S(2)}) copy-start(bf16[1024,1024]{1,0:T(8,128)(2,1)} %refs_5_.1) | copy-start | bytes 6291460
  1.6 11.3 %collective-permute-start = (bf16[192,1024]{1,0:T(8,128)(2,1)S(1)}, bf16[192,1024]{1,0:T(8,128)(2,1)S(1)}, u32[]{:S(2)}, u32[]{:S(2)}) collective-permute-start(bf16[192,1024]{1,0:T(8,128)(2,1)S(1)} %get-tuple-element.34.refs_0_), channel_id=1, source_target_pairs={{0,4},{1,5},{4,6},{5,7},{6,2},{7,3},{2,0},{3,1},{8,12},{9,13},{12,... | collective-permute-start | bytes 1179656 | tf_op jit(solution)/shard_map/ppermute | solution.py:296
  4.8 2.0 %collective-permute-start.3 = (bf16[64,1024]{1,0:T(8,128)(2,1)S(1)}, bf16[64,1024]{1,0:T(8,128)(2,1)S(1)}, u32[]{:S(2)}, u32[]{:S(2)}) collective-permute-start(bf16[64,1024]{1,0:T(8,128)(2,1)S(1)} %get-tuple-element.66), channel_id=1, source_target_pairs={{0,1},{1,0},{2,3},{3,2},{4,5},{5,4},{6,7},{7,6},{8,9},{9,8},{10,11... | collective-permute-start | bytes 393224 | tf_op jit(solution)/shard_map/ppermute | solution.py:296
  5.8 2.9 %collective-permute-start.2 = (bf16[64,1024]{1,0:T(8,128)(2,1)S(1)}, bf16[64,1024]{1,0:T(8,128)(2,1)S(1)}, u32[]{:S(2)}, u32[]{:S(2)}) collective-permute-start(bf16[64,1024]{1,0:T(8,128)(2,1)S(1)} %get-tuple-element.67), channel_id=1, source_target_pairs={{0,1},{1,0},{2,3},{3,2},{4,5},{5,4},{6,7},{7,6},{8,9},{9,8},{10,11... | collective-permute-start | bytes 393224 | tf_op jit(solution)/shard_map/ppermute | solution.py:296
  5.9 4.7 %collective-permute-start.1 = (bf16[64,1024]{1,0:T(8,128)(2,1)S(1)}, bf16[64,1024]{1,0:T(8,128)(2,1)S(1)}, u32[]{:S(2)}, u32[]{:S(2)}) collective-permute-start(bf16[64,1024]{1,0:T(8,128)(2,1)S(1)} %get-tuple-element.68), channel_id=1, source_target_pairs={{0,1},{1,0},{2,3},{3,2},{4,5},{5,4},{6,7},{7,6},{8,9},{9,8},{10,11... | collective-permute-start | bytes 393224 | tf_op jit(solution)/shard_map/ppermute | solution.py:296
  6.4 6.6 %collective-permute-start.4 = (f32[16,1024]{1,0:T(8,128)S(1)}, f32[16,1024]{1,0:T(8,128)S(1)}, u32[]{:S(2)}, u32[]{:S(2)}) collective-permute-start(f32[16,1024]{1,0:T(8,128)S(1)} %get-tuple-element.36), channel_id=1, source_target_pairs={{0,1},{1,0},{2,3},{3,2},{4,5},{5,4},{6,7},{7,6},{8,9},{9,8},{10,11... | collective-permute-start | bytes 196616 | tf_op jit(solution)/shard_map/ppermute | solution.py:296
  6.8 8.9 %collective-permute-start.7 = (f32[16,1024]{1,0:T(8,128)S(1)}, f32[16,1024]{1,0:T(8,128)S(1)}, u32[]{:S(2)}, u32[]{:S(2)}) collective-permute-start(f32[16,1024]{1,0:T(8,128)S(1)} %get-tuple-element.39), channel_id=1, source_target_pairs={{1,2},{2,1},{3,4},{4,3},{5,6},{6,5},{9,10},{10,9},{11,12},{12,11},... | collective-permute-start | bytes 196616 | tf_op jit(solution)/shard_map/ppermute | solution.py:296
  8.8 24.1 %collective-permute-start.6 = (bf16[192,1024]{1,0:T(8,128)(2,1)S(1)}, bf16[192,1024]{1,0:T(8,128)(2,1)S(1)}, u32[]{:S(2)}, u32[]{:S(2)}) collective-permute-start(bf16[192,1024]{1,0:T(8,128)(2,1)S(1)} %get-tuple-element.34.refs_0_), channel_id=1, source_target_pairs={{4,0},{5,1},{6,4},{7,5},{2,6},{3,7},{0,2},{1,3},{12,8},{13,9},{14,... | collective-permute-start | bytes 1179656 | tf_op jit(solution)/shard_map/ppermute | solution.py:296
  13.0 31.4 %collective-permute-start.5 = (bf16[192,1024]{1,0:T(8,128)(2,1)S(1)}, bf16[192,1024]{1,0:T(8,128)(2,1)S(1)}, u32[]{:S(2)}, u32[]{:S(2)}) collective-permute-start(bf16[192,1024]{1,0:T(8,128)(2,1)S(1)} %collective-permute-done.block), channel_id=1, source_target_pairs={{0,4},{1,5},{4,6},{5,7},{6,2},{7,3},{2,0},{3,1},{8,12},{9,13},{12,... | collective-permute-start | bytes 1179656 | tf_op jit(solution)/shard_map/ppermute | solution.py:296
  15.7 4.6 %collective-permute-start.10 = (bf16[64,1024]{1,0:T(8,128)(2,1)S(1)}, bf16[64,1024]{1,0:T(8,128)(2,1)S(1)}, u32[]{:S(2)}, u32[]{:S(2)}) collective-permute-start(bf16[64,1024]{1,0:T(8,128)(2,1)S(1)} %get-tuple-element.63), channel_id=1, source_target_pairs={{0,1},{1,0},{2,3},{3,2},{4,5},{5,4},{6,7},{7,6},{8,9},{9,8},{10,11... | collective-permute-start | bytes 393224 | tf_op jit(solution)/shard_map/ppermute | solution.py:296
  18.8 1.6 %collective-permute-start.9 = (bf16[64,1024]{1,0:T(8,128)(2,1)S(1)}, bf16[64,1024]{1,0:T(8,128)(2,1)S(1)}, u32[]{:S(2)}, u32[]{:S(2)}) collective-permute-start(bf16[64,1024]{1,0:T(8,128)(2,1)S(1)} %get-tuple-element.64), channel_id=1, source_target_pairs={{0,1},{1,0},{2,3},{3,2},{4,5},{5,4},{6,7},{7,6},{8,9},{9,8},{10,11... | collective-permute-start | bytes 393224 | tf_op jit(solution)/shard_map/ppermute | solution.py:296
  18.9 1.5 %collective-permute-start.8 = (bf16[64,1024]{1,0:T(8,128)(2,1)S(1)}, bf16[64,1024]{1,0:T(8,128)(2,1)S(1)}, u32[]{:S(2)}, u32[]{:S(2)}) collective-permute-start(bf16[64,1024]{1,0:T(8,128)(2,1)S(1)} %get-tuple-element.65), channel_id=1, source_target_pairs={{0,1},{1,0},{2,3},{3,2},{4,5},{5,4},{6,7},{7,6},{8,9},{9,8},{10,11... | collective-permute-start | bytes 393224 | tf_op jit(solution)/shard_map/ppermute | solution.py:296
  44.3 1.8 %copy-start.3 = (bf16[1024,1024]{1,0:T(8,128)(2,1)S(1)}, bf16[1024,1024]{1,0:T(8,128)(2,1)}, u32[]{:S(2)}) copy-start(bf16[1024,1024]{1,0:T(8,128)(2,1)} %output_weight.1) | copy-start | bytes 6291460
  44.3 1.8 %copy-start.5 = (f32[31,1024]{1,0:T(8,128)S(1)}, f32[31,1024]{1,0:T(8,128)}, u32[]{:S(2)}) copy-start(f32[31,1024]{1,0:T(8,128)} %depthwise.1) | copy-start | bytes 380932
  44.3 1.8 %copy-start.7 = (f32[1024]{0:T(1024)S(1)}, f32[1024]{0:T(1024)}, u32[]{:S(2)}) copy-start(f32[1024]{0:T(1024)} %param.15) | copy-start | bytes 12292
  44.4 1.8 %copy-start.8 = (f32[1024]{0:T(1024)S(1)}, f32[1024]{0:T(1024)}, u32[]{:S(2)}) copy-start(f32[1024]{0:T(1024)} %param.17) | copy-start | bytes 12292
  44.4 1.8 %collective-permute-start.11 = (bf16[192,1024]{1,0:T(8,128)(2,1)S(1)}, bf16[192,1024]{1,0:T(8,128)(2,1)S(1)}, u32[]{:S(2)}, u32[]{:S(2)}) collective-permute-start(bf16[192,1024]{1,0:T(8,128)(2,1)S(1)} %collective-permute-done.5.block), channel_id=1, source_target_pairs={{0,1},{1,0},{2,3},{3,2},{4,5},{5,4},{6,7},{7,6},{8,9},{9,8},{10,11... | collective-permute-start | bytes 1179656 | tf_op jit(solution)/shard_map/ppermute | solution.py:296

commit v7 on v5

--- a/solution.py
+++ b/solution.py
@@ -244,7 +244,8 @@
                 part = term if part is None else part + term
             if part is not None:
                 convolved = convolved + part[shift : shift + rows]
-        held[:, span] = attended[HALO : HALO + rows, span] + convolved / (1.0 + jnp.exp(-convolved))
+        half = 0.5 * convolved
+        held[:, span] = attended[HALO : HALO + rows, span] + (half + half * jnp.tanh(half))
         copies.append(pltpu.make_async_copy(held.at[:, span], block_out.at[:, span], sems.at[low // LANES]))
         copies[-1].start()
     for copy in copies:

time: 59.4 us -> 59.4 us (level)
  no operation moved by 1% of the time
where the time goes in v7:
time: 59.4 us; the launch traced here: 59 us
  Pallas kernels  38.9 us (65%)
  starting transfers between devices  15.2 us (26%)
  blocking collectives  2.37 us (4%)
  local copies, waits for them, and re-layouts  1.3 us (2%)
  waiting for transfers between devices  0.83 us (1%)
    ppermute x12, starting transfers between devices, send(): return lax.ppermute(value, 'ctx', pairs)  15.2 us
    pallas_call x1, Pallas kernels, per_device(): call(last_kernel, [jax.ShapeDtypeStruct((rows, width), f32)] + tall(2), [...  12.6 us
    pallas_call x1, Pallas kernels, per_device(): call(functools.partial(first_kernel, start=3 * rows), [jax.ShapeDtypeStru...  12.5 us
    pallas_call x1, Pallas kernels, per_device(): call(block_kernel, list(state), [VMEM] * 8, projected, flops=BLOCK)  9.08 us
    all_gather x1, blocking collectives, per_device(): lax.all_gather(block, 'ctx', axis=0, tiled=True, axis_index_groups=siblings)  2.37 us
    pallas_call x1, Pallas kernels, per_device(): call(own_kernel, [jax.ShapeDtypeStruct((rows, width), bf16)] + tall(4), [...  2.28 us
  transfers between devices with their start and end apart: 12, of which 2 were waited for; matrix products, arithmetic and copies ran while one was open for 0% of the time, Pallas kernels for 44%

profile of v7, /device:TPU:1, one launch (start us, length us, event | category | flops | bytes accessed | tf_op | source)
XLA Modules:
  0.0 59.0 jit_solution(792187669032713906)
XLA Ops:
  0.0 0.1 add_convert_fusion
  0.2 1.1 %copy-done.4 = f32[192,1024]{1,0:T(8,128)S(1)} copy-done((f32[192,1024]{1,0:T(8,128)S(1)}, f32[192,1024]{1,0:T(8,128)}, u32[]{:S(2)}) %copy-start.4) | copy-done | bytes 786456
  1.3 0.3 shard_map.92
  1.6 3.2 %collective-permute-start = (bf16[192,1024]{1,0:T(8,128)(2,1)S(1)}, bf16[192,1024]{1,0:T(8,128)(2,1)S(1)}, u32[]{:S(2)}, u32[]{:S(2)}) collective-permute-start(bf16[192,1024]{1,0:T(8,128)(2,1)S(1)} %get-tuple-element.34.refs_0_), channel_id=1, source_target_pairs={{0,4},{1,5},{4,6},{5,7},{6,2},{7,3},{2,0},{3,1},{8,12},{9,13},{12,... | collective-permute-start | bytes 1179656 | tf_op jit(solution)/shard_map/ppermute | solution.py:296
  4.8 1.0 %collective-permute-start.3 = (bf16[64,1024]{1,0:T(8,128)(2,1)S(1)}, bf16[64,1024]{1,0:T(8,128)(2,1)S(1)}, u32[]{:S(2)}, u32[]{:S(2)}) collective-permute-start(bf16[64,1024]{1,0:T(8,128)(2,1)S(1)} %get-tuple-element.66), channel_id=1, source_target_pairs={{0,1},{1,0},{2,3},{3,2},{4,5},{5,4},{6,7},{7,6},{8,9},{9,8},{10,11... | collective-permute-start | bytes 393224 | tf_op jit(solution)/shard_map/ppermute | solution.py:296
  5.8 0.1 collective-permute-start.2
  5.9 0.4 collective-permute-start.1
  6.4 0.1 collective-permute-start.4
  6.4 0.4 collective-permute-done.3.refs_6_
  6.8 1.9 %collective-permute-start.7 = (f32[16,1024]{1,0:T(8,128)S(1)}, f32[16,1024]{1,0:T(8,128)S(1)}, u32[]{:S(2)}, u32[]{:S(2)}) collective-permute-start(f32[16,1024]{1,0:T(8,128)S(1)} %get-tuple-element.39), channel_id=1, source_target_pairs={{1,2},{2,1},{3,4},{4,3},{5,6},{6,5},{9,10},{10,9},{11,12},{12,11},... | collective-permute-start | bytes 196616 | tf_op jit(solution)/shard_map/ppermute | solution.py:296
  8.8 1.9 %collective-permute-start.6 = (bf16[192,1024]{1,0:T(8,128)(2,1)S(1)}, bf16[192,1024]{1,0:T(8,128)(2,1)S(1)}, u32[]{:S(2)}, u32[]{:S(2)}) collective-permute-start(bf16[192,1024]{1,0:T(8,128)(2,1)S(1)} %get-tuple-element.34.refs_0_), channel_id=1, source_target_pairs={{4,0},{5,1},{6,4},{7,5},{2,6},{3,7},{0,2},{1,3},{12,8},{13,9},{14,... | collective-permute-start | bytes 1179656 | tf_op jit(solution)/shard_map/ppermute | solution.py:296
  10.6 2.3 %shard_map.93 = (bf16[192,1024]{1,0:T(8,128)(2,1)S(1)}, bf16[768,1024]{1,0:T(8,128)(2,1)S(1)}, bf16[768,1024]{1,0:T(8,128)(2,1)S(1)}) custom-call(bf16[192,1024]{1,0:T(8,128)(2,1)S(1)} %get-tuple-element.34.refs_0_, bf16[1024,1024]{1,0:T(8,128)(2,1)S(1)} %copy-done.2, bf16[1024,1024]{1,0:T(8,128)(2,1)S(1)} %copy-done, bf16[1024,1024]{1,0:T(8,128)(2,1)S(1)} %copy-done.1, ...), custom_call_target="tpu_custom_call" | custom-call | flops 1024 | bytes 1024 | tf_op jit(solution)/shard_map/pallas_call | solution.py:317
  13.0 2.8 %collective-permute-start.5 = (bf16[192,1024]{1,0:T(8,128)(2,1)S(1)}, bf16[192,1024]{1,0:T(8,128)(2,1)S(1)}, u32[]{:S(2)}, u32[]{:S(2)}) collective-permute-start(bf16[192,1024]{1,0:T(8,128)(2,1)S(1)} %collective-permute-done.block), channel_id=1, source_target_pairs={{0,4},{1,5},{4,6},{5,7},{6,2},{7,3},{2,0},{3,1},{8,12},{9,13},{12,... | collective-permute-start | bytes 1179656 | tf_op jit(solution)/shard_map/ppermute | solution.py:296
  15.7 3.0 %collective-permute-start.10 = (bf16[64,1024]{1,0:T(8,128)(2,1)S(1)}, bf16[64,1024]{1,0:T(8,128)(2,1)S(1)}, u32[]{:S(2)}, u32[]{:S(2)}) collective-permute-start(bf16[64,1024]{1,0:T(8,128)(2,1)S(1)} %get-tuple-element.63), channel_id=1, source_target_pairs={{0,1},{1,0},{2,3},{3,2},{4,5},{5,4},{6,7},{7,6},{8,9},{9,8},{10,11... | collective-permute-start | bytes 393224 | tf_op jit(solution)/shard_map/ppermute | solution.py:296
  18.8 0.1 collective-permute-start.9
  18.9 0.4 collective-permute-start.8
  19.3 1.0 %shard_map.94 = (bf16[768,1024]{1,0:T(8,128)(2,1)S(1)}, bf16[768,1024]{1,0:T(8,128)(2,1)S(1)}) custom-call(bf16[192,1024]{1,0:T(8,128)(2,1)S(1)} %collective-permute-done.block, bf16[1024,1024]{1,0:T(8,128)(2,1)S(1)} %copy-done, bf16[1024,1024]{1,0:T(8,128)(2,1)S(1)} %copy-done.1, ...), custom_call_target="tpu_custom_call", output_to_operand_aliasing={{0}: (3, {}), {1}: (4, {})} | custom-call | flops 1024 | bytes 1024 | tf_op jit(solution)/shard_map/pallas_call | solution.py:331
  20.4 12.5 %shard_map.95 = (bf16[224,1024]{1,0:T(8,128)(2,1)S(1)}, f32[8,128]{1,0:T(8,128)S(1)}, f32[224,1024]{1,0:T(8,128)S(1)}, f32[224,1024]{1,0:T(8,128)S(1)}, f32[224,...) custom-call(f32[3,128]{1,0:T(4,128)S(1)} %shard_map.91.place.refs_0_, ...), custom_call_target="tpu_custom_call", output_to_operand_aliasing={{5}: (8, {}), {6}: (9, {})} | custom-call | flops 1024 | bytes 1024 | tf_op jit(solution)/shard_map/pallas_call | solution.py:334
  32.9 2.4 %all_gather.3.block = bf16[384,1024]{1,0:T(8,128)(2,1)S(1)} all-gather(bf16[192,1024]{1,0:T(8,128)(2,1)S(1)} %collective-permute-done.6), channel_id=1, replica_groups={{0,1},{2,3},{4,5},{6,7},{8,9},{10,11},{12,13},{14,15},{16,17},{18,19},{..., dimensions={0}, use_global_device_ids=true | all-gather | bytes 1179648 | tf_op jit(solution)/shard_map/all_gather | solution.py:353
  35.3 9.1 %shard_map.96 = (f32[8,128]{1,0:T(8,128)S(1)}, f32[224,1024]{1,0:T(8,128)S(1)}, f32[224,1024]{1,0:T(8,128)S(1)}, f32[224,1024]{1,0:T(8,128)S(1)}) custom-call(bf16[384,1024]{1,0:T(8,128)(2,1)S(1)} %all_gather.3.block, bf16[224,1024]{1,0:T(8,128)(2,1)S(1)} %get-tuple-element.49.query, bf16[1024,1024]{1,0:T(8,128)(2,1)S(1)} %copy-done, ...), custom_call_target="tpu_custom_call" | custom-call | flops 1024 | bytes 1024 | tf_op jit(solution)/shard_map/pallas_call | solution.py:355
  44.4 0.3 collective-permute-start.11
  44.7 1.0 %shard_map.97 = (bf16[384,1024]{1,0:T(8,128)(2,1)S(1)}, bf16[384,1024]{1,0:T(8,128)(2,1)S(1)}) custom-call(bf16[192,1024]{1,0:T(8,128)(2,1)S(1)} %collective-permute-done.5.block, bf16[1024,1024]{1,0:T(8,128)(2,1)S(1)} %copy-done, bf16[1024,1024]{1,0:T(8,128)(2,1)S(1)} %copy-done.1), custom_call_target="tpu_custom_call" | custom-call | flops 1024 | bytes 1024 | tf_op jit(solution)/shard_map/pallas_call | solution.py:361
  45.8 0.4 collective-permute-done.11.sibling
  46.2 12.6 %shard_map.98 = (f32[192,1024]{1,0:T(8,128)}, bf16[384,1024]{1,0:T(8,128)(2,1)S(1)}, bf16[384,1024]{1,0:T(8,128)(2,1)S(1)}) custom-call(f32[3,128]{1,0:T(4,128)S(1)} %shard_map.91.place.refs_0_, bf16[192,1024]{1,0:T(8,128)(2,1)S(1)} %collective-permute-done.11.sibling, ...), custom_call_target="tpu_custom_call", output_to_operand_aliasing={{1}: (2, {}), {2}: (3, {})} | custom-call | flops 1024 | bytes 1024 | tf_op jit(solution)/shard_map/pallas_call | solution.py:362
  (31 shorter events, 0.2 us)
Async XLA Ops:
  0.2 1.1 %copy-start.4 = (f32[192,1024]{1,0:T(8,128)S(1)}, f32[192,1024]{1,0:T(8,128)}, u32[]{:S(2)}) copy-start(f32[192,1024]{1,0:T(8,128)} %frames.3) | copy-start | bytes 2359300
  0.2 1.1 %copy-start.6 = (f32[1024]{0:T(1024)S(1)}, f32[1024]{0:T(1024)}, u32[]{:S(2)}) copy-start(f32[1024]{0:T(1024)} %param.10) | copy-start | bytes 12292
  1.3 9.3 %copy-start = (bf16[1024,1024]{1,0:T(8,128)(2,1)S(1)}, bf16[1024,1024]{1,0:T(8,128)(2,1)}, u32[]{:S(2)}) copy-start(bf16[1024,1024]{1,0:T(8,128)(2,1)} %key_weight.7) | copy-start | bytes 6291460
  1.3 9.3 %copy-start.1 = (bf16[1024,1024]{1,0:T(8,128)(2,1)S(1)}, bf16[1024,1024]{1,0:T(8,128)(2,1)}, u32[]{:S(2)}) copy-start(bf16[1024,1024]{1,0:T(8,128)(2,1)} %value_weight.7) | copy-start | bytes 6291460
  1.3 9.3 %copy-start.2 = (bf16[1024,1024]{1,0:T(8,128)(2,1)S(1)}, bf16[1024,1024]{1,0:T(8,128)(2,1)}, u32[]{:S(2)}) copy-start(bf16[1024,1024]{1,0:T(8,128)(2,1)} %refs_5_.1) | copy-start | bytes 6291460
  1.6 11.3 %collective-permute-start = (bf16[192,1024]{1,0:T(8,128)(2,1)S(1)}, bf16[192,1024]{1,0:T(8,128)(2,1)S(1)}, u32[]{:S(2)}, u32[]{:S(2)}) collective-permute-start(bf16[192,1024]{1,0:T(8,128)(2,1)S(1)} %get-tuple-element.34.refs_0_), channel_id=1, source_target_pairs={{0,4},{1,5},{4,6},{5,7},{6,2},{7,3},{2,0},{3,1},{8,12},{9,13},{12,... | collective-permute-start | bytes 1179656 | tf_op jit(solution)/shard_map/ppermute | solution.py:296
  4.8 2.0 %collective-permute-start.3 = (bf16[64,1024]{1,0:T(8,128)(2,1)S(1)}, bf16[64,1024]{1,0:T(8,128)(2,1)S(1)}, u32[]{:S(2)}, u32[]{:S(2)}) collective-permute-start(bf16[64,1024]{1,0:T(8,128)(2,1)S(1)} %get-tuple-element.66), channel_id=1, source_target_pairs={{0,1},{1,0},{2,3},{3,2},{4,5},{5,4},{6,7},{7,6},{8,9},{9,8},{10,11... | collective-permute-start | bytes 393224 | tf_op jit(solution)/shard_map/ppermute | solution.py:296
  5.8 2.9 %collective-permute-start.2 = (bf16[64,1024]{1,0:T(8,128)(2,1)S(1)}, bf16[64,1024]{1,0:T(8,128)(2,1)S(1)}, u32[]{:S(2)}, u32[]{:S(2)}) collective-permute-start(bf16[64,1024]{1,0:T(8,128)(2,1)S(1)} %get-tuple-element.67), channel_id=1, source_target_pairs={{0,1},{1,0},{2,3},{3,2},{4,5},{5,4},{6,7},{7,6},{8,9},{9,8},{10,11... | collective-permute-start | bytes 393224 | tf_op jit(solution)/shard_map/ppermute | solution.py:296
  5.9 4.7 %collective-permute-start.1 = (bf16[64,1024]{1,0:T(8,128)(2,1)S(1)}, bf16[64,1024]{1,0:T(8,128)(2,1)S(1)}, u32[]{:S(2)}, u32[]{:S(2)}) collective-permute-start(bf16[64,1024]{1,0:T(8,128)(2,1)S(1)} %get-tuple-element.68), channel_id=1, source_target_pairs={{0,1},{1,0},{2,3},{3,2},{4,5},{5,4},{6,7},{7,6},{8,9},{9,8},{10,11... | collective-permute-start | bytes 393224 | tf_op jit(solution)/shard_map/ppermute | solution.py:296
  6.4 6.6 %collective-permute-start.4 = (f32[16,1024]{1,0:T(8,128)S(1)}, f32[16,1024]{1,0:T(8,128)S(1)}, u32[]{:S(2)}, u32[]{:S(2)}) collective-permute-start(f32[16,1024]{1,0:T(8,128)S(1)} %get-tuple-element.36), channel_id=1, source_target_pairs={{0,1},{1,0},{2,3},{3,2},{4,5},{5,4},{6,7},{7,6},{8,9},{9,8},{10,11... | collective-permute-start | bytes 196616 | tf_op jit(solution)/shard_map/ppermute | solution.py:296
  6.8 8.9 %collective-permute-start.7 = (f32[16,1024]{1,0:T(8,128)S(1)}, f32[16,1024]{1,0:T(8,128)S(1)}, u32[]{:S(2)}, u32[]{:S(2)}) collective-permute-start(f32[16,1024]{1,0:T(8,128)S(1)} %get-tuple-element.39), channel_id=1, source_target_pairs={{1,2},{2,1},{3,4},{4,3},{5,6},{6,5},{9,10},{10,9},{11,12},{12,11},... | collective-permute-start | bytes 196616 | tf_op jit(solution)/shard_map/ppermute | solution.py:296
  8.8 24.1 %collective-permute-start.6 = (bf16[192,1024]{1,0:T(8,128)(2,1)S(1)}, bf16[192,1024]{1,0:T(8,128)(2,1)S(1)}, u32[]{:S(2)}, u32[]{:S(2)}) collective-permute-start(bf16[192,1024]{1,0:T(8,128)(2,1)S(1)} %get-tuple-element.34.refs_0_), channel_id=1, source_target_pairs={{4,0},{5,1},{6,4},{7,5},{2,6},{3,7},{0,2},{1,3},{12,8},{13,9},{14,... | collective-permute-start | bytes 1179656 | tf_op jit(solution)/shard_map/ppermute | solution.py:296
  13.0 31.4 %collective-permute-start.5 = (bf16[192,1024]{1,0:T(8,128)(2,1)S(1)}, bf16[192,1024]{1,0:T(8,128)(2,1)S(1)}, u32[]{:S(2)}, u32[]{:S(2)}) collective-permute-start(bf16[192,1024]{1,0:T(8,128)(2,1)S(1)} %collective-permute-done.block), channel_id=1, source_target_pairs={{0,4},{1,5},{4,6},{5,7},{6,2},{7,3},{2,0},{3,1},{8,12},{9,13},{12,... | collective-permute-start | bytes 1179656 | tf_op jit(solution)/shard_map/ppermute | solution.py:296
  15.7 4.6 %collective-permute-start.10 = (bf16[64,1024]{1,0:T(8,128)(2,1)S(1)}, bf16[64,1024]{1,0:T(8,128)(2,1)S(1)}, u32[]{:S(2)}, u32[]{:S(2)}) collective-permute-start(bf16[64,1024]{1,0:T(8,128)(2,1)S(1)} %get-tuple-element.63), channel_id=1, source_target_pairs={{0,1},{1,0},{2,3},{3,2},{4,5},{5,4},{6,7},{7,6},{8,9},{9,8},{10,11... | collective-permute-start | bytes 393224 | tf_op jit(solution)/shard_map/ppermute | solution.py:296
  18.8 1.6 %collective-permute-start.9 = (bf16[64,1024]{1,0:T(8,128)(2,1)S(1)}, bf16[64,1024]{1,0:T(8,128)(2,1)S(1)}, u32[]{:S(2)}, u32[]{:S(2)}) collective-permute-start(bf16[64,1024]{1,0:T(8,128)(2,1)S(1)} %get-tuple-element.64), channel_id=1, source_target_pairs={{0,1},{1,0},{2,3},{3,2},{4,5},{5,4},{6,7},{7,6},{8,9},{9,8},{10,11... | collective-permute-start | bytes 393224 | tf_op jit(solution)/shard_map/ppermute | solution.py:296
  18.9 1.5 %collective-permute-start.8 = (bf16[64,1024]{1,0:T(8,128)(2,1)S(1)}, bf16[64,1024]{1,0:T(8,128)(2,1)S(1)}, u32[]{:S(2)}, u32[]{:S(2)}) collective-permute-start(bf16[64,1024]{1,0:T(8,128)(2,1)S(1)} %get-tuple-element.65), channel_id=1, source_target_pairs={{0,1},{1,0},{2,3},{3,2},{4,5},{5,4},{6,7},{7,6},{8,9},{9,8},{10,11... | collective-permute-start | bytes 393224 | tf_op jit(solution)/shard_map/ppermute | solution.py:296
  44.4 1.8 %copy-start.3 = (bf16[1024,1024]{1,0:T(8,128)(2,1)S(1)}, bf16[1024,1024]{1,0:T(8,128)(2,1)}, u32[]{:S(2)}) copy-start(bf16[1024,1024]{1,0:T(8,128)(2,1)} %output_weight.1) | copy-start | bytes 6291460
  44.4 1.8 %copy-start.5 = (f32[31,1024]{1,0:T(8,128)S(1)}, f32[31,1024]{1,0:T(8,128)}, u32[]{:S(2)}) copy-start(f32[31,1024]{1,0:T(8,128)} %depthwise.1) | copy-start | bytes 380932
  44.4 1.8 %copy-start.7 = (f32[1024]{0:T(1024)S(1)}, f32[1024]{0:T(1024)}, u32[]{:S(2)}) copy-start(f32[1024]{0:T(1024)} %param.15) | copy-start | bytes 12292
  44.4 1.8 %copy-start.8 = (f32[1024]{0:T(1024)S(1)}, f32[1024]{0:T(1024)}, u32[]{:S(2)}) copy-start(f32[1024]{0:T(1024)} %param.17) | copy-start | bytes 12292
  44.4 1.8 %collective-permute-start.11 = (bf16[192,1024]{1,0:T(8,128)(2,1)S(1)}, bf16[192,1024]{1,0:T(8,128)(2,1)S(1)}, u32[]{:S(2)}, u32[]{:S(2)}) collective-permute-start(bf16[192,1024]{1,0:T(8,128)(2,1)S(1)} %collective-permute-done.5.block), channel_id=1, source_target_pairs={{0,1},{1,0},{2,3},{3,2},{4,5},{5,4},{6,7},{7,6},{8,9},{9,8},{10,11... | collective-permute-start | bytes 1179656 | tf_op jit(solution)/shard_map/ppermute | solution.py:296
